TPU v7x, 256 devices: a whole 4x4x8 slice. The times are simulated.
256 devices in a mesh: outer: 16 (over y, x), seq: 16 (over z, core).
Axes of the slice: x: 4, y: 4, z: 8, core: 2. Of those that a mesh axis runs over, the one named last changes fastest.
Arguments:
- query_rows: bfloat16 [32768, 1024], P(('outer', 'seq')), may hold values from -6 to 6
- key_rows: bfloat16 [32768, 1024], P(('outer', 'seq')), may hold values from -6 to 6
- value_rows: bfloat16 [32768, 1024], P(('outer', 'seq')), may hold values from -6 to 6
- out_grad: bfloat16 [32768, 1024], P(('outer', 'seq')), may hold values from -6 to 6
Outputs:
- attended: bfloat16 [32768, 1024], P(('outer', 'seq'))
- query_grad: float32 [32768, 1024], P(('outer', 'seq'))
- key_grad: float32 [32768, 1024], P(('outer', 'seq'))
- value_grad: float32 [32768, 1024], P(('outer', 'seq'))
All inputs are finite; a program needn't handle non-finite values.
Results may differ from a plain program's by a relative error of at most 0.018.
Values may be sent and summed in bfloat16 or wider, within the bound.
No kernel may reach another device: no remote copies, remote signals or barrier semaphores. Data moves between devices by JAX's collectives and lax.ppermute only.
A program may use at most 128 MiB of HBM per device.

v0:
```python
import math

import jax
import jax.numpy as jnp
from jax import lax
from jax.experimental import pallas as pl
from jax.experimental.pallas import tpu as pltpu
from jax.sharding import PartitionSpec as P

HEADS = 8
HEAD = 128
LEVELS = 3
BLOCK = 128
HALF = 512
PAIR = 1024
ROW = 8
AXES = ("outer", "seq")
NEGATIVE = -1e30
FACTOR = 1.0 / math.sqrt(HEAD)
FACTOR2 = FACTOR / math.log(2.0)
BF16 = jnp.bfloat16
F32 = jnp.float32


def dot(a, b, dims=((1,), (0,))):
    return lax.dot_general(a, b, (dims, ((), ())), preferred_element_type=F32)


def pool_matrix(rows, columns, span):
    i = lax.broadcasted_iota(jnp.int32, (rows, columns), 0)
    j = lax.broadcasted_iota(jnp.int32, (rows, columns), 1)
    return jnp.where(j // span == i, 1.0 / span, 0.0).astype(BF16)


def spread_matrix(rows, columns, span):
    i = lax.broadcasted_iota(jnp.int32, (rows, columns), 0)
    j = lax.broadcasted_iota(jnp.int32, (rows, columns), 1)
    return jnp.where(i // span == j, 1.0 / span, 0.0).astype(BF16)


def half_columns(core):
    return pl.ds(pl.multiple_of(core * HALF, HALF), HALF)


def block_at(core):
    return pl.ds(pl.multiple_of(core * BLOCK, BLOCK), BLOCK)


def open_kernel(where, k, v, own, other, coarse):
    core = where[0] % 2
    halve = pool_matrix(64, BLOCK, 2)
    for n, half, fine in ((1, 1 - core, other), (0, core, own)):
        columns = half_columns(half)
        fine[:, 0:512] = k[:, columns]
        fine[:, 512:1024] = v[:, columns]
        coarse[64 * n : 64 * n + 64] = dot(halve, fine[...]).astype(BF16)


def sides(first, own, recv, fine_same, fine_cross, half_same, half_cross):
    def pick(a, b):
        return jnp.where(first, a[...], b[...])

    return (
        pick(own, recv),
        pick(recv, own),
        pick(fine_cross, fine_same),
        pick(fine_same, fine_cross),
        pick(half_same[0:64], half_cross[64:128]),
        pick(half_cross[64:128], half_same[0:64]),
    )


def coarse_kernel(
    where, own, recv, fine_same, fine_cross, half_same, half_cross, same2, cross2, other2, quad3
):
    even = (where[0] // 2) % 2 == 0
    first = where[0] % 2 == 0
    low, high, fine_below, fine_above, half_below, half_above = sides(
        first, own, recv, fine_same, fine_cross, half_same, half_cross
    )
    fine = jnp.concatenate([pool_matrix(32, BLOCK, 4), pool_matrix(16, BLOCK, 8)], axis=0)
    half = jnp.concatenate([pool_matrix(32, 64, 2), pool_matrix(16, 64, 4)], axis=0)
    own_low = dot(fine[32:48], low).astype(BF16)
    own_high = dot(fine[32:48], high).astype(BF16)
    below_low = dot(half, half_below).astype(BF16)
    below_high = dot(fine, fine_below).astype(BF16)
    above_low = dot(fine, fine_above).astype(BF16)
    above_high = dot(half, half_above).astype(BF16)
    b2 = jnp.concatenate([below_low[0:32], below_high[0:32]], axis=0)
    a2 = jnp.concatenate([above_low[0:32], above_high[0:32]], axis=0)
    same2[...] = jnp.where(first, b2, a2)
    cross2[...] = jnp.where(first, a2, b2)
    other2[...] = jnp.where(even, a2, b2)
    own3 = jnp.concatenate([own_low, own_high], axis=0)
    b3 = jnp.concatenate([below_low[32:48], below_high[32:48]], axis=0)
    a3 = jnp.concatenate([above_low[32:48], above_high[32:48]], axis=0)
    quad3[0:32] = jnp.where(even, own3, b3)
    quad3[32:64] = jnp.where(even, a3, own3)


NEAR = 576
FAR = 384
NT = ((1,), (1,))
TN = ((0,), (0,))


def bias(valid, level):
    return jnp.where(valid, F32(level), F32(NEGATIVE))


def row_bias(pieces):
    return jnp.concatenate([jnp.full((rows, 1), value, F32) for rows, value in pieces], axis=0)


def columns_of(h):
    return (
        slice(h * HEAD, (h + 1) * HEAD),
        slice(HALF + h * HEAD, HALF + (h + 1) * HEAD),
    )


def back(weight, near, columns):
    edges = jnp.concatenate(
        [
            dot(near[384:576, columns], weight[384:576, 0:128], TN),
            dot(near[576:768, columns], weight[384:576, 128:256], TN),
        ],
        axis=1,
    )
    return dot(near[0:384, columns], weight[0:384], TN) + edges


def near_kernel(
    where, q, g, recv_q, recv_g, own_kv, recv_kv, fine_same, fine_cross, half_same, half_cross,
    queries, grads, keyvals, weights, dprobs, stats, outputs,
):
    chips = where[1] // 2
    core = where[0] % 2
    chip = where[0] // 2
    mine = half_columns(core)
    queries[block_at(core), :] = q[:, mine]
    queries[block_at(1 - core), :] = recv_q[:, mine]
    grads[block_at(core), :] = g[:, mine]
    grads[block_at(1 - core), :] = recv_g[:, mine]
    low, high, fine_below, fine_above, half_below, half_above = sides(
        core == 0, own_kv, recv_kv, fine_same, fine_cross, half_same, half_cross
    )
    halve = pool_matrix(64, BLOCK, 2)
    keyvals[0:128] = low
    keyvals[128:256] = high
    keyvals[256:320] = half_below
    keyvals[320:384] = half_above
    keyvals[384:512] = fine_below
    keyvals[512:576] = dot(halve, fine_above).astype(BF16)
    keyvals[576:704] = fine_above
    keyvals[704:768] = dot(halve, fine_below).astype(BF16)
    has_below = chip >= 1
    has_above = chip < chips - 1
    side = lax.broadcasted_iota(jnp.int32, (1, 256), 1) < 128
    fine_bias = jnp.where(side, bias(has_below, 0), bias(has_above, 0))
    half_bias = jnp.where(side, bias(has_above, 1), bias(has_below, 1))
    rows_bias = row_bias(((256, F32(0.0)), (64, bias(has_below, 1)), (64, bias(has_above, 1))))

    def product(columns, rows):
        shared = dot(keyvals[0:384, columns], rows, NT)
        edges = jnp.concatenate(
            [
                dot(keyvals[384:576, columns], rows[0:128], NT),
                dot(keyvals[576:768, columns], rows[128:256], NT),
            ],
            axis=1,
        )
        return shared, edges

    for h in range(4):
        kc, vc = columns_of(h)
        at = NEAR * h
        shared, edges = product(kc, queries[:, kc])
        scores = jnp.concatenate(
            [
                shared * FACTOR2 + rows_bias,
                edges[0:128] * FACTOR2 + fine_bias,
                edges[128:192] * FACTOR2 + half_bias,
            ],
            axis=0,
        )
        highest = jnp.max(scores, axis=0, keepdims=True)
        weight = jnp.exp2(scores - highest)
        weights[at : at + NEAR] = weight
        stats[h : h + 1] = highest
        stats[4 + h : 5 + h] = jnp.sum(weight, axis=0, keepdims=True)
        outputs[HEAD * h : HEAD * h + HEAD] = back(weight.astype(BF16), keyvals, vc)
        shared, edges = product(vc, grads[:, kc])
        dprobs[at : at + 384] = shared
        dprobs[at + 384 : at + NEAR] = edges


def main_kernel(
    where, queries, grads, outputs, stats, m2, p2, s2, z3, x3, s3,
    output, scales, dscores, gm2, gp2, gs2, gz3, gx3, gs3,
    far,
):
    chips = where[1] // 2
    core = where[0] % 2
    chip = where[0] // 2
    quad = chip // 2
    for n, piece in enumerate((m2, p2, s2, z3, x3, s3)):
        far[64 * n : 64 * n + 64] = piece[...]
    far2 = jnp.where(chip % 2 == 0, chip + 3, chip - 3)
    far3 = jnp.where(quad % 2 == 0, quad + 3, quad - 3)
    quads = chips // 2
    rows_bias = row_bias(
        (
            (64, bias(jnp.where(core == 0, chip >= 2, chip + 2 < chips), 2)),
            (64, bias(jnp.where(core == 0, chip + 2 < chips, chip >= 2), 2)),
            (64, bias((far2 >= 0) & (far2 < chips), 2)),
            (64, F32(3)),
            (64, bias(jnp.where(chip % ROW < ROW // 2, chip >= ROW, chip + ROW < chips), 3)),
            (64, bias((far3 >= 0) & (far3 < quads), 3)),
        )
    )
    heads = [columns_of(h) for h in range(4)]
    scores = [dot(far[:, kc], queries[:, kc], NT) * FACTOR2 + rows_bias for kc, _ in heads]
    dprobs = [dot(far[:, vc], grads[:, kc], NT) for kc, vc in heads]
    probs = []
    for h in range(4):
        before = stats[h : h + 1]
        highest = jnp.maximum(before, jnp.max(scores[h], axis=0, keepdims=True))
        weight = jnp.exp2(scores[h] - highest)
        shrink = jnp.exp2(before - highest)
        total = stats[4 + h : 5 + h] * shrink + jnp.sum(weight, axis=0, keepdims=True)
        inverse = 1.0 / total
        scales[h : h + 1] = shrink * inverse
        probs.append(weight * inverse)
    lows = [p.astype(BF16) for p in probs]
    attended = [
        outputs[HEAD * h : HEAD * h + HEAD] * scales[h : h + 1] + dot(far[:, vc], lows[h], TN)
        for h, (_, vc) in enumerate(heads)
    ]
    terms_v = [dot(lows[h], grads[:, kc]).astype(BF16) for h, (kc, _) in enumerate(heads)]
    terms_k = []
    for h, (kc, _) in enumerate(heads):
        delta = jnp.sum(grads[:, kc].astype(F32).T * attended[h], axis=0, keepdims=True)
        scales[4 + h : 5 + h] = delta
        dscore = (probs[h] * (dprobs[h] - delta)).astype(BF16)
        dscores[FAR * h : FAR * h + FAR] = dscore
        terms_k.append((dot(dscore, queries[:, kc]) * FACTOR).astype(BF16))
    for h, (kc, vc) in enumerate(heads):
        output[:, kc] = attended[h].T
        for n, piece in enumerate((gm2, gp2, gs2, gz3, gx3, gs3)):
            piece[:, kc] = terms_k[h][64 * n : 64 * n + 64]
            piece[:, vc] = terms_v[h][64 * n : 64 * n + 64]


def rest_kernel(
    where, queries, grads, near, weights, dprobs, scales, dscores, output,
    m2, p2, s2, z3, x3, s3,
    keep, send, grad_below, grad_above,
    outs,
):
    core = where[0] % 2
    spread = spread_matrix(BLOCK, 64, 2)
    for h in range(4):
        kc, vc = columns_of(h)
        at = NEAR * h
        probs = weights[at : at + NEAR] * scales[h : h + 1]
        low = probs.astype(BF16)
        dscore = (probs * (dprobs[at : at + NEAR] - scales[4 + h : 5 + h])).astype(BF16)
        far = jnp.concatenate([piece[:, kc] for piece in (m2, p2, s2, z3, x3, s3)], axis=0)
        query_grad = back(dscore, near, kc) + dot(far, dscores[FAR * h : FAR * h + FAR], TN)
        outs[:, kc] = output[:, kc]
        outs[:, vc] = query_grad.T * FACTOR
        for columns, weight, rows, scale in (
            (kc, dscore, queries[:, kc], FACTOR),
            (vc, low, grads[:, kc], 1.0),
        ):
            shared = dot(weight[0:384], rows) * scale
            part_a = dot(weight[384:576, 0:128], rows[0:128]) * scale
            part_b = dot(weight[384:576, 128:256], rows[128:256]) * scale
            outs[:, PAIR + columns.start : PAIR + columns.stop] = shared[0:256]
            terms = shared[256:384].astype(BF16)
            grad_below[0:128, columns] = (
                part_a[0:128] + dot(spread, part_b[128:192].astype(BF16))
            ).astype(BF16)
            grad_below[128:192, columns] = terms[0:64]
            grad_above[0:128, columns] = (
                part_b[0:128] + dot(spread, part_a[128:192].astype(BF16))
            ).astype(BF16)
            grad_above[128:192, columns] = terms[64:128]
    keep[...] = outs[block_at(core), :]
    send[...] = outs[block_at(1 - core), :]


def fold_kernel(
    where, grad_below, grad_above, s3, z3, same2, cross2, other2,
    out_same, out_cross, half_same, half_cross, keep3, send3,
):
    even = (where[0] // 2) % 2 == 0

    def weigh(matrix, use):
        return jnp.where(use, matrix, jnp.zeros_like(matrix))

    def fold(base, pieces2, rows, use, fine, half):
        def rows_of(n):
            return jnp.concatenate(
                [piece[32 * n : 32 * n + 32] for piece in (pieces2, other2)]
                + [piece[rows + 16 * n : rows + 16 * n + 16] for piece in (z3, s3)],
                axis=0,
            )

        fine_matrix = jnp.concatenate(
            [spread_matrix(128, 32, 4), weigh(spread_matrix(128, 32, 4), use)]
            + [weigh(spread_matrix(128, 16, 8), use)] * 2,
            axis=1,
        )
        half_matrix = jnp.concatenate(
            [spread_matrix(64, 32, 2), weigh(spread_matrix(64, 32, 2), use)]
            + [weigh(spread_matrix(64, 16, 4), use)] * 2,
            axis=1,
        )
        return (
            (base[0:128].astype(F32) + dot(fine_matrix, rows_of(fine))).astype(BF16),
            (base[128:192].astype(F32) + dot(half_matrix, rows_of(half))).astype(BF16),
        )

    first = where[0] % 2 == 0
    from2 = jnp.where(first, same2[...], cross2[...])
    to2 = jnp.where(first, cross2[...], same2[...])
    fine_below, half_below = fold(grad_below, from2, 0, jnp.logical_not(even), 1, 0)
    fine_above, half_above = fold(grad_above, to2, 32, even, 0, 1)
    out_same[...] = jnp.where(first, fine_above, fine_below)
    out_cross[...] = jnp.where(first, fine_below, fine_above)
    half_same[...] = jnp.where(first, half_below, half_above)
    half_cross[...] = jnp.where(first, half_above, half_below)
    row = pl.multiple_of((where[0] // 2) % 2 * 32, 32)
    own3 = (z3[pl.ds(row, 32), :].astype(F32) + s3[pl.ds(row, 32), :].astype(F32)).astype(BF16)
    keep3[...] = jnp.where(first, own3[0:16], own3[16:32])
    send3[...] = jnp.where(first, own3[16:32], own3[0:16])


def join_kernel(where, out_keep, out_recv, attended, qg):
    core = where[0] % 2
    mine = half_columns(core)
    other = half_columns(1 - core)
    attended[:, mine] = out_keep[:, 0:512].astype(BF16)
    attended[:, other] = out_recv[:, 0:512].astype(BF16)
    qg[:, mine] = out_keep[:, 512:1024]
    qg[:, other] = out_recv[:, 512:1024]


def final_kernel(
    where, keep, recv, keep3, recv3, fine_same, fine_cross, half_same, half_cross,
    kg, vg, total, sems,
):
    core = where[0] % 2
    matrix = jnp.concatenate([spread_matrix(BLOCK, 64, 2), spread_matrix(BLOCK, 16, 8)], axis=1)
    copies = []
    for n, (side, own, fine, half, last) in enumerate(
        (
            (core, keep, fine_same, half_same, keep3),
            (1 - core, recv, fine_cross, half_cross, recv3),
        )
    ):
        coarse = jnp.concatenate([half[...], last[...]], axis=0)
        total[n] = own[:, PAIR : 2 * PAIR] + fine[...].astype(F32) + dot(matrix, coarse)
        for m, target in enumerate((kg, vg)):
            copies.append(
                pltpu.make_async_copy(
                    total.at[n, :, HALF * m : HALF * (m + 1)],
                    target.at[:, half_columns(side)],
                    sems.at[2 * n + m],
                )
            )
            copies[-1].start()
    for copy in copies:
        copy.wait()


def call(kernel, where, args, outs, scratch=(), space=pltpu.VMEM):
    return pl.pallas_call(
        kernel,
        out_shape=[jax.ShapeDtypeStruct(shape, dtype) for shape, dtype in outs],
        in_specs=[pl.BlockSpec(memory_space=pltpu.SMEM)]
        + [pl.BlockSpec(memory_space=pltpu.VMEM)] * len(args),
        out_specs=[pl.BlockSpec(memory_space=space)] * len(outs),
        scratch_shapes=list(scratch),
        compiler_params=pltpu.CompilerParams(vmem_limit_bytes=32 * 1024 * 1024),
    )(where, *args)


def sources(chips):
    def opposite(p):
        turn = ROW // 2 + 1 if p % 2 == 0 else ROW // 2 - 1
        return p - p % ROW + (p + turn) % ROW

    near = {
        "fine_same": lambda p, c: (p - 1, 1) if c == 1 else (p + 1, 0),
        "half_same": lambda p, c: (p - 1, 0) if c == 0 else (p + 1, 1),
        "far2": lambda p, c: (p + 2 if p % 2 == 0 else p - 2, c),
        "z3": lambda p, c: (opposite(p), c),
        "x3": lambda p, c: (p - ROW if p % ROW < ROW // 2 else p + ROW, c),
        "s3": lambda p, c: (p + 6 if p // 2 % 2 == 0 else p - 6, c),
    }
    closing = {
        "fine_same": lambda p, c: (p, 1 - c),
        "half_same": lambda p, c: (p, 1 - c),
        "far2": lambda p, c: (p ^ 1, c),
        "x3": lambda p, c: (p - p % ROW + ROW - 1 - p % ROW, c),
        "s3": lambda p, c: (p ^ 1, c),
    }

    def source(name, p, c):
        found = near[name](p, c)
        return found if 0 <= found[0] < chips else closing[name](p, c)

    return source


def on_device(query_rows, key_rows, value_rows, out_grad):
    position = lax.axis_index(AXES)
    devices = lax.axis_size(AXES)
    chips = devices // 2
    plan = sources(chips)
    where = jnp.stack([position, jnp.int32(devices)]).astype(jnp.int32)

    def swap(x):
        return lax.ppermute(x, AXES, [(i, i ^ 1) for i in range(devices)])

    def pairs(name):
        found = []
        for chip in range(chips):
            for core in range(2):
                source, side = plan(name, chip, core)
                found.append((2 * source + side, 2 * chip + core))
        return found

    def fetch(x, name):
        return lax.ppermute(x, AXES, pairs(name))

    def give(x, name):
        return lax.ppermute(x, AXES, [(b, a) for a, b in pairs(name)])

    recv_q = swap(query_rows)
    recv_g = swap(out_grad)
    own_kv, other_kv, half_kv = call(
        open_kernel, where, (key_rows, value_rows), [((BLOCK, PAIR), BF16)] * 3
    )
    recv_q, recv_g, own_kv, other_kv, half_kv = lax.optimization_barrier(
        (recv_q, recv_g, own_kv, other_kv, half_kv)
    )
    fine_cross = swap(fetch(other_kv, "fine_same"))
    half_same = fetch(half_kv, "half_same")
    half_cross = swap(half_same)
    fine_same = fetch(own_kv, "fine_same")
    recv_kv = swap(other_kv)
    near = (fine_same, fine_cross, half_same, half_cross)
    same2, cross2, other2, quad3 = call(
        coarse_kernel, where, (own_kv, recv_kv, *near), [((64, PAIR), BF16)] * 4
    )
    z3 = fetch(quad3, "z3")
    s3 = fetch(quad3, "s3")
    s2 = fetch(other2, "far2")
    same2 = fetch(same2, "half_same")
    cross2 = fetch(cross2, "fine_same")
    x3 = fetch(z3, "x3")
    queries, grads, near_kv, weights, dprobs, stats, outputs = call(
        near_kernel,
        where,
        (query_rows, out_grad, recv_q, recv_g, own_kv, recv_kv, *near),
        [
            ((2 * BLOCK, HALF), BF16),
            ((2 * BLOCK, HALF), BF16),
            ((768, PAIR), BF16),
            ((4 * NEAR, 2 * BLOCK), F32),
            ((4 * NEAR, 2 * BLOCK), F32),
            ((8, 2 * BLOCK), F32),
            ((4 * HEAD, 2 * BLOCK), F32),
        ],
    )
    far = (same2, cross2, s2, z3, x3, s3)
    output, scales, dscores, gm2, gp2, gs2, gz3, gx3, gs3 = call(
        main_kernel,
        where,
        (queries, grads, outputs, stats, *far),
        [
            ((2 * BLOCK, HALF), F32),
            ((8, 2 * BLOCK), F32),
            ((4 * FAR, 2 * BLOCK), BF16),
        ]
        + [((64, PAIR), BF16)] * 6,
        scratch=[pltpu.VMEM((FAR, PAIR), BF16)],
    )
    back_s3 = give(gs3, "s3")
    gz3, gs2, gp2, scales = lax.optimization_barrier((gz3 + give(gx3, "x3"), gs2, gp2, scales))
    back_z3 = give(gz3, "z3")
    back_s2 = give(gs2, "far2")
    back_m2 = give(gm2, "half_same")
    back_p2 = give(gp2, "fine_same")
    keep, send, grad_below, grad_above = call(
        rest_kernel,
        where,
        (queries, grads, near_kv, weights, dprobs, scales, dscores, output, *far),
        [
            ((BLOCK, 2 * PAIR), F32),
            ((BLOCK, 2 * PAIR), F32),
            ((192, PAIR), BF16),
            ((192, PAIR), BF16),
        ],
        scratch=[pltpu.VMEM((2 * BLOCK, 2 * PAIR), F32)],
    )
    fine_same, fine_cross, half_same, half_cross, keep3, send3 = call(
        fold_kernel,
        where,
        (grad_below, grad_above, back_s3, back_z3, back_m2, back_p2, back_s2),
        [((BLOCK, PAIR), BF16)] * 2
        + [((BLOCK // 2, PAIR), BF16)] * 2
        + [((16, PAIR), BF16)] * 2,
    )
    fine_same = give(fine_same, "fine_same")
    fine_cross = give(swap(fine_cross), "fine_same")
    half_same = give(half_same, "half_same")
    half_cross = give(swap(half_cross), "half_same")
    send, send3 = lax.optimization_barrier((send, send3))
    recv3 = swap(send3)
    recv = swap(send)
    attended, query_grad = call(
        join_kernel, where, (keep, recv), [((BLOCK, PAIR), BF16), ((BLOCK, PAIR), F32)]
    )
    attended, query_grad, keep3 = lax.optimization_barrier((attended, query_grad, keep3))
    key_grad, value_grad = call(
        final_kernel,
        where,
        (keep, recv, keep3, recv3, fine_same, fine_cross, half_same, half_cross),
        [((BLOCK, PAIR), F32)] * 2,
        scratch=[pltpu.VMEM((2, BLOCK, PAIR), F32), pltpu.SemaphoreType.DMA((4,))],
        space=pl.ANY,
    )
    return attended, query_grad, key_grad, value_grad


def solution(mesh):
    spec = P(AXES, None)
    return jax.shard_map(
        on_device, mesh=mesh, in_specs=(spec,) * 4, out_specs=(spec,) * 4, check_vma=False
    )
```

profile of v0, /device:TPU:25, one launch (start us, length us, event | category | flops | bytes accessed | tf_op | source)
XLA Modules:
  0.0 88.0 jit_solution(7048809580065877201)
XLA Ops:
  0.6 0.8 collective-permute-start
  1.4 0.1 collective-permute-start.1
  1.5 0.1 pad_add_fusion.where
  1.6 0.9 %copy-done = bf16[128,1024]{1,0:T(8,128)(2,1)S(1)} copy-done((bf16[128,1024]{1,0:T(8,128)(2,1)S(1)}, bf16[128,1024]{1,0:T(8,128)(2,1)}, u32[]{:S(2)}) %copy-start) | copy-done | bytes 262168
  2.5 0.9 %copy-done.1 = bf16[128,1024]{1,0:T(8,128)(2,1)S(1)} copy-done((bf16[128,1024]{1,0:T(8,128)(2,1)S(1)}, bf16[128,1024]{1,0:T(8,128)(2,1)}, u32[]{:S(2)}) %copy-start.1) | copy-done | bytes 262168
  3.5 0.8 shard_map.75
  4.3 0.0 collective-permute-done.recv_q
  4.3 0.0 collective-permute-done.1.recv_g
  4.3 8.0 %collective-permute-start.6 = (bf16[128,1024]{1,0:T(8,128)(2,1)S(1)}, bf16[128,1024]{1,0:T(8,128)(2,1)S(1)}, u32[]{:S(2)}, u32[]{:S(2)}) collective-permute-start(bf16[128,1024]{1,0:T(8,128)(2,1)S(1)} %get-tuple-element.62), channel_id=1, source_target_pairs={{1,0},{3,1},{0,2},{5,3},{2,4},{7,5},{4,6},{9,7},{6,8},{11,9},{8,10... | collective-permute-start | bytes 786440 | tf_op jit(solution)/shard_map/ppermute | solution.py:438
  12.3 0.0 collective-permute-start.4
  12.3 0.8 collective-permute-start.2
  13.1 0.0 collective-permute-start.3
  13.1 4.4 %collective-permute-done.6.half_same = bf16[128,1024]{1,0:T(8,128)(2,1)S(1)} collective-permute-done((bf16[128,1024]{1,0:T(8,128)(2,1)S(1)}, bf16[128,1024]{1,0:T(8,128)(2,1)S(1)}, u32[]{:S(2)}, u32[]{:S(2)}) %collective-permute-start.6) | collective-permute-done | bytes 262176 | tf_op jit(solution)/shard_map/ppermute | solution.py:438
  17.5 1.3 %collective-permute-start.7 = (bf16[128,1024]{1,0:T(8,128)(2,1)S(1)}, bf16[128,1024]{1,0:T(8,128)(2,1)S(1)}, u32[]{:S(2)}, u32[]{:S(2)}) collective-permute-start(bf16[128,1024]{1,0:T(8,128)(2,1)S(1)} %collective-permute-done.6.half_same), channel_id=1, source_target_pairs={{0,1},{1,0},{2,3},{3,2},{4,5},{5,4},{6,7},{7,6},{8,9},{9,8},{10,11... | collective-permute-start | bytes 786440 | tf_op jit(solution)/shard_map/ppermute | solution.py:427
  18.8 3.0 %collective-permute-done.4 = bf16[128,1024]{1,0:T(8,128)(2,1)S(1)} collective-permute-done((bf16[128,1024]{1,0:T(8,128)(2,1)S(1)}, bf16[128,1024]{1,0:T(8,128)(2,1)S(1)}, u32[]{:S(2)}, u32[]{:S(2)}) %collective-permute-start.4) | collective-permute-done | bytes 262176 | tf_op jit(solution)/shard_map/ppermute | solution.py:438
  21.8 0.0 collective-permute-start.5
  21.8 0.0 collective-permute-done.2.recv_kv.recv
  21.8 2.8 %collective-permute-done.3.fine_same = bf16[128,1024]{1,0:T(8,128)(2,1)S(1)} collective-permute-done((bf16[128,1024]{1,0:T(8,128)(2,1)S(1)}, bf16[128,1024]{1,0:T(8,128)(2,1)S(1)}, u32[]{:S(2)}, u32[]{:S(2)}) %collective-permute-start.3) | collective-permute-done | bytes 262176 | tf_op jit(solution)/shard_map/ppermute | solution.py:438
  24.6 0.0 collective-permute-done.7.half_cross
  24.6 0.0 collective-permute-done.5.fine_cross
  24.6 0.9 %shard_map.77 = (bf16[64,1024]{1,0:T(8,128)(2,1)S(1)}, bf16[64,1024]{1,0:T(8,128)(2,1)S(1)}, bf16[64,1024]{1,0:T(8,128)(2,1)S(1)}, bf16[64,1024]{1,0:T(8,128)(2,1)S(1)}) custom-call(s32[2]{0:T(128)S(1)} %pad_add_fusion.where, bf16[128,1024]{1,0:T(8,128)(2,1)S(1)} %get-tuple-element.60.own_kv.own, bf16[128,1024]{1,0:T(8,128)(2,1)S(1)} %collective-permute-done.2.recv_kv.recv, ...), custom_call_target="tpu_custom_call" | custom-call | tf_op jit(solution)/shard_map/pallas_call | solution.py:380
  25.5 0.1 collective-permute-start.11
  25.6 0.1 collective-permute-start.13
  25.7 3.9 %collective-permute-start.8 = (bf16[64,1024]{1,0:T(8,128)(2,1)S(1)}, bf16[64,1024]{1,0:T(8,128)(2,1)S(1)}, u32[]{:S(2)}, u32[]{:S(2)}) collective-permute-start(bf16[64,1024]{1,0:T(8,128)(2,1)S(1)} %get-tuple-element.70), channel_id=1, source_target_pairs={{1,0},{3,1},{0,2},{5,3},{2,4},{7,5},{4,6},{9,7},{6,8},{11,9},{8,10... | collective-permute-start | bytes 393224 | tf_op jit(solution)/shard_map/ppermute | solution.py:438
  29.6 1.2 %collective-permute-start.10 = (bf16[64,1024]{1,0:T(8,128)(2,1)S(1)}, bf16[64,1024]{1,0:T(8,128)(2,1)S(1)}, u32[]{:S(2)}, u32[]{:S(2)}) collective-permute-start(bf16[64,1024]{1,0:T(8,128)(2,1)S(1)} %get-tuple-element.72), channel_id=1, source_target_pairs={{4,0},{5,1},{0,2},{1,3},{8,4},{9,5},{2,6},{3,7},{12,8},{13,9},{6,1... | collective-permute-start | bytes 393224 | tf_op jit(solution)/shard_map/ppermute | solution.py:438
  30.8 3.4 %collective-permute-done.11.z3 = bf16[64,1024]{1,0:T(8,128)(2,1)S(1)} collective-permute-done((bf16[64,1024]{1,0:T(8,128)(2,1)S(1)}, bf16[64,1024]{1,0:T(8,128)(2,1)S(1)}, u32[]{:S(2)}, u32[]{:S(2)}) %collective-permute-start.11) | collective-permute-done | bytes 131104 | tf_op jit(solution)/shard_map/ppermute | solution.py:438
  34.2 0.0 collective-permute-start.12
  34.2 0.9 %copy-done.2 = bf16[128,1024]{1,0:T(8,128)(2,1)S(1)} copy-done((bf16[128,1024]{1,0:T(8,128)(2,1)S(1)}, bf16[128,1024]{1,0:T(8,128)(2,1)}, u32[]{:S(2)}) %copy-start.2) | copy-done | bytes 262168
  35.2 0.9 %copy-done.3 = bf16[128,1024]{1,0:T(8,128)(2,1)S(1)} copy-done((bf16[128,1024]{1,0:T(8,128)(2,1)S(1)}, bf16[128,1024]{1,0:T(8,128)(2,1)}, u32[]{:S(2)}) %copy-start.3) | copy-done | bytes 262168
  36.1 2.8 %shard_map.76 = (bf16[256,512]{1,0:T(8,128)(2,1)S(1)}, bf16[256,512]{1,0:T(8,128)(2,1)S(1)}, bf16[768,1024]{1,0:T(8,128)(2,1)S(1)}, f32[2304,256]{1,0:T(8,128)S(...) custom-call(s32[2]{0:T(128)S(1)} %pad_add_fusion.where, ...), custom_call_target="tpu_custom_call" | custom-call | tf_op jit(solution)/shard_map/pallas_call | solution.py:380
  39.0 0.2 collective-permute-done.8.m2
  39.2 2.9 %collective-permute-done.9.p2 = bf16[64,1024]{1,0:T(8,128)(2,1)S(1)} collective-permute-done((bf16[64,1024]{1,0:T(8,128)(2,1)S(1)}, bf16[64,1024]{1,0:T(8,128)(2,1)S(1)}, u32[]{:S(2)}, u32[]{:S(2)}) %collective-permute-start.9) | collective-permute-done | bytes 131104 | tf_op jit(solution)/shard_map/ppermute | solution.py:438
  42.1 0.0 collective-permute-done.10.s2
  42.1 0.0 collective-permute-done.13.s3
  42.1 2.2 %collective-permute-done.12.x3 = bf16[64,1024]{1,0:T(8,128)(2,1)S(1)} collective-permute-done((bf16[64,1024]{1,0:T(8,128)(2,1)S(1)}, bf16[64,1024]{1,0:T(8,128)(2,1)S(1)}, u32[]{:S(2)}, u32[]{:S(2)}) %collective-permute-start.12) | collective-permute-done | bytes 131104 | tf_op jit(solution)/shard_map/ppermute | solution.py:438
  44.4 2.3 %shard_map.78 = (f32[256,512]{1,0:T(8,128)S(1)}, f32[8,256]{1,0:T(8,128)S(1)}, bf16[1536,256]{1,0:T(8,128)(2,1)S(1)}, bf16[64,1024]{1,0:T(8,128)(2,1)S(1)}, bf16...) custom-call(s32[2]{0:T(128)S(1)} %pad_add_fusion.where, ...), custom_call_target="tpu_custom_call" | custom-call | tf_op jit(solution)/shard_map/pallas_call | solution.py:380
  46.7 0.1 collective-permute-start.14
  46.8 2.4 %collective-permute-start.15 = (bf16[64,1024]{1,0:T(8,128)(2,1)S(1)}, bf16[64,1024]{1,0:T(8,128)(2,1)S(1)}, u32[]{:S(2)}, u32[]{:S(2)}) collective-permute-start(bf16[64,1024]{1,0:T(8,128)(2,1)S(1)} %get-tuple-element.86), channel_id=1, source_target_pairs={{0,12},{1,13},{2,14},{3,15},{4,6},{5,7},{6,4},{7,5},{8,20},{9,21},... | collective-permute-start | bytes 393224 | tf_op jit(solution)/shard_map/ppermute | solution.py:441
  49.2 0.0 collective-permute-start.17
  49.3 1.9 %collective-permute-done.14 = bf16[64,1024]{1,0:T(8,128)(2,1)S(1)} collective-permute-done((bf16[64,1024]{1,0:T(8,128)(2,1)S(1)}, bf16[64,1024]{1,0:T(8,128)(2,1)S(1)}, u32[]{:S(2)}, u32[]{:S(2)}) %collective-permute-start.14) | collective-permute-done | bytes 131104 | tf_op jit(solution)/shard_map/ppermute | solution.py:441
  51.2 3.6 %collective-permute-start.16 = (bf16[64,1024]{1,0:T(8,128)(2,1)S(1)}, bf16[64,1024]{1,0:T(8,128)(2,1)S(1)}, u32[]{:S(2)}, u32[]{:S(2)}) collective-permute-start(bf16[64,1024]{1,0:T(8,128)(2,1)S(1)} %add.7), channel_id=1, source_target_pairs={{0,10},{1,11},{2,8},{3,9},{4,14},{5,15},{6,12},{7,13},{8,2},{9,3},... | collective-permute-start | bytes 393224 | tf_op jit(solution)/shard_map/ppermute | solution.py:441
  54.8 2.1 %collective-permute-start.18 = (bf16[64,1024]{1,0:T(8,128)(2,1)S(1)}, bf16[64,1024]{1,0:T(8,128)(2,1)S(1)}, u32[]{:S(2)}, u32[]{:S(2)}) collective-permute-start(bf16[64,1024]{1,0:T(8,128)(2,1)S(1)} %get-tuple-element.89), channel_id=1, source_target_pairs={{0,2},{1,0},{2,4},{3,1},{4,6},{5,3},{6,8},{7,5},{8,10},{9,7},{10,1... | collective-permute-start | bytes 393224 | tf_op jit(solution)/shard_map/ppermute | solution.py:441
  56.9 0.8 collective-permute-start.19
  57.6 3.2 %shard_map.79 = (f32[128,2048]{1,0:T(8,128)S(1)}, f32[128,2048]{1,0:T(8,128)S(1)}, bf16[192,1024]{1,0:T(8,128)(2,1)S(1)}, bf16[192,1024]{1,0:T(8,128)(2,1)S(1)}) custom-call(s32[2]{0:T(128)S(1)} %pad_add_fusion.where, bf16[256,512]{1,0:T(8,128)(2,1)S(1)} %get-tuple-element.63.queries, bf16[256,512]{1,0:T(8,128)(2,1)S(1)} %get-tuple-element.64.grads, ...), custom_call_target="tpu_custom_call" | custom-call | tf_op jit(solution)/shard_map/pallas_call | solution.py:380
  60.8 0.0 collective-permute-done.15.s3
  60.8 0.0 collective-permute-done.16.z3
  60.8 3.5 %collective-permute-done.18.cross2 = bf16[64,1024]{1,0:T(8,128)(2,1)S(1)} collective-permute-done((bf16[64,1024]{1,0:T(8,128)(2,1)S(1)}, bf16[64,1024]{1,0:T(8,128)(2,1)S(1)}, u32[]{:S(2)}, u32[]{:S(2)}) %collective-permute-start.18) | collective-permute-done | bytes 131104 | tf_op jit(solution)/shard_map/ppermute | solution.py:441
  64.4 2.7 %collective-permute-done.19.other2 = bf16[64,1024]{1,0:T(8,128)(2,1)S(1)} collective-permute-done((bf16[64,1024]{1,0:T(8,128)(2,1)S(1)}, bf16[64,1024]{1,0:T(8,128)(2,1)S(1)}, u32[]{:S(2)}, u32[]{:S(2)}) %collective-permute-start.19) | collective-permute-done | bytes 131104 | tf_op jit(solution)/shard_map/ppermute | solution.py:441
  67.1 1.0 %shard_map.80 = (bf16[128,1024]{1,0:T(8,128)(2,1)S(1)}, bf16[128,1024]{1,0:T(8,128)(2,1)S(1)}, bf16[64,1024]{1,0:T(8,128)(2,1)S(1)}, bf16[64,1024]{1,0:T(8,128)(...) custom-call(s32[2]{0:T(128)S(1)} %pad_add_fusion.where, ...), custom_call_target="tpu_custom_call" | custom-call | tf_op jit(solution)/shard_map/pallas_call | solution.py:380
  68.1 1.7 %collective-permute-start.20 = (f32[128,2048]{1,0:T(8,128)S(1)}, f32[128,2048]{1,0:T(8,128)S(1)}, u32[]{:S(2)}, u32[]{:S(2)}) collective-permute-start(f32[128,2048]{1,0:T(8,128)S(1)} %get-tuple-element.92), channel_id=1, source_target_pairs={{0,1},{1,0},{2,3},{3,2},{4,5},{5,4},{6,7},{7,6},{8,9},{9,8},{10,11... | collective-permute-start | bytes 3145736 | tf_op jit(solution)/shard_map/ppermute | solution.py:427
  69.8 0.1 collective-permute-start.23
  69.9 0.4 collective-permute-start.26
  70.4 3.7 %collective-permute-start.22 = (bf16[128,1024]{1,0:T(8,128)(2,1)S(1)}, bf16[128,1024]{1,0:T(8,128)(2,1)S(1)}, u32[]{:S(2)}, u32[]{:S(2)}) collective-permute-start(bf16[128,1024]{1,0:T(8,128)(2,1)S(1)} %get-tuple-element.100), channel_id=1, source_target_pairs={{0,2},{1,0},{2,4},{3,1},{4,6},{5,3},{6,8},{7,5},{8,10},{9,7},{10,1... | collective-permute-start | bytes 786440 | tf_op jit(solution)/shard_map/ppermute | solution.py:441
  74.1 2.1 %collective-permute-start.24 = (bf16[128,1024]{1,0:T(8,128)(2,1)S(1)}, bf16[128,1024]{1,0:T(8,128)(2,1)S(1)}, u32[]{:S(2)}, u32[]{:S(2)}) collective-permute-start(bf16[128,1024]{1,0:T(8,128)(2,1)S(1)} %collective-permute-done.23), channel_id=1, source_target_pairs={{0,2},{1,0},{2,4},{3,1},{4,6},{5,3},{6,8},{7,5},{8,10},{9,7},{10,1... | collective-permute-start | bytes 786440 | tf_op jit(solution)/shard_map/ppermute | solution.py:441
  76.2 0.0 collective-permute-start.25
  76.3 0.0 collective-permute-done.20.out_recv.recv
  76.3 3.0 %collective-permute-start.21 = (bf16[16,1024]{1,0:T(8,128)(2,1)S(1)}, bf16[16,1024]{1,0:T(8,128)(2,1)S(1)}, u32[]{:S(2)}, u32[]{:S(2)}) collective-permute-start(bf16[16,1024]{1,0:T(8,128)(2,1)S(1)} %get-tuple-element.99), channel_id=1, source_target_pairs={{0,1},{1,0},{2,3},{3,2},{4,5},{5,4},{6,7},{7,6},{8,9},{9,8},{10,11... | collective-permute-start | bytes 98312 | tf_op jit(solution)/shard_map/ppermute | solution.py:427
  79.2 1.5 %shard_map.81 = (bf16[128,1024]{1,0:T(8,128)(2,1)}, f32[128,1024]{1,0:T(8,128)}) custom-call(s32[2]{0:T(128)S(1)} %pad_add_fusion.where, f32[128,2048]{1,0:T(8,128)S(1)} %get-tuple-element.82.out_keep.keep, f32[128,2048]{1,0:T(8,128)S(1)} %collective-permute-done.20.out_recv.recv), custom_call_target="tpu_custom_call" | custom-call | tf_op jit(solution)/shard_map/pallas_call | solution.py:380
  80.7 0.0 collective-permute-done.21.recv3
  80.7 3.9 %collective-permute-done.25.half_same = bf16[64,1024]{1,0:T(8,128)(2,1)S(1)} collective-permute-done((bf16[64,1024]{1,0:T(8,128)(2,1)S(1)}, bf16[64,1024]{1,0:T(8,128)(2,1)S(1)}, u32[]{:S(2)}, u32[]{:S(2)}) %collective-permute-start.25) | collective-permute-done | bytes 131104 | tf_op jit(solution)/shard_map/ppermute | solution.py:441
  84.6 1.4 %collective-permute-done.27.half_cross = bf16[64,1024]{1,0:T(8,128)(2,1)S(1)} collective-permute-done((bf16[64,1024]{1,0:T(8,128)(2,1)S(1)}, bf16[64,1024]{1,0:T(8,128)(2,1)S(1)}, u32[]{:S(2)}, u32[]{:S(2)}) %collective-permute-start.27) | collective-permute-done | bytes 131104 | tf_op jit(solution)/shard_map/ppermute | solution.py:441
  86.0 0.0 collective-permute-done.22.fine_same
  86.0 0.0 collective-permute-done.24.fine_cross
  86.0 1.8 %shard_map.82 = (f32[128,1024]{1,0:T(8,128)}, f32[128,1024]{1,0:T(8,128)}) custom-call(s32[2]{0:T(128)S(1)} %pad_add_fusion.where, f32[128,2048]{1,0:T(8,128)S(1)} %get-tuple-element.82.out_keep.keep, f32[128,2048]{1,0:T(8,128)S(1)} %collective-permute-done.20.out_recv.recv, bf16[16,1024]{1,0:T(8,128)(2,1)S(1)} %get-tuple-element.98.keep3, ...), custom_call_target="tpu_custom_call" | custom-call | tf_op jit(solution)/shard_map/pallas_call | solution.py:380
  (10 shorter events, 0.1 us)
Async XLA Ops:
  0.6 3.6 %collective-permute-start = (bf16[128,1024]{1,0:T(8,128)(2,1)}, bf16[128,1024]{1,0:T(8,128)(2,1)S(1)}, u32[]{:S(2)}, u32[]{:S(2)}) collective-permute-start(bf16[128,1024]{1,0:T(8,128)(2,1)} %q.1), channel_id=1, source_target_pairs={{0,1},{1,0},{2,3},{3,2},{4,5},{5,4},{6,7},{7,6},{8,9},{9,8},{10,11... | collective-permute-start | bytes 786440 | tf_op jit(solution)/shard_map/ppermute | solution.py:427
  1.4 2.9 %collective-permute-start.1 = (bf16[128,1024]{1,0:T(8,128)(2,1)}, bf16[128,1024]{1,0:T(8,128)(2,1)S(1)}, u32[]{:S(2)}, u32[]{:S(2)}) collective-permute-start(bf16[128,1024]{1,0:T(8,128)(2,1)} %g.1), channel_id=1, source_target_pairs={{0,1},{1,0},{2,3},{3,2},{4,5},{5,4},{6,7},{7,6},{8,9},{9,8},{10,11... | collective-permute-start | bytes 786440 | tf_op jit(solution)/shard_map/ppermute | solution.py:427
  1.6 0.9 %copy-start = (bf16[128,1024]{1,0:T(8,128)(2,1)S(1)}, bf16[128,1024]{1,0:T(8,128)(2,1)}, u32[]{:S(2)}) copy-start(bf16[128,1024]{1,0:T(8,128)(2,1)} %k.1) | copy-start | bytes 786436
  2.5 0.9 %copy-start.1 = (bf16[128,1024]{1,0:T(8,128)(2,1)S(1)}, bf16[128,1024]{1,0:T(8,128)(2,1)}, u32[]{:S(2)}) copy-start(bf16[128,1024]{1,0:T(8,128)(2,1)} %v.1) | copy-start | bytes 786436
  4.3 13.2 %collective-permute-start.6 = (bf16[128,1024]{1,0:T(8,128)(2,1)S(1)}, bf16[128,1024]{1,0:T(8,128)(2,1)S(1)}, u32[]{:S(2)}, u32[]{:S(2)}) collective-permute-start(bf16[128,1024]{1,0:T(8,128)(2,1)S(1)} %get-tuple-element.62), channel_id=1, source_target_pairs={{1,0},{3,1},{0,2},{5,3},{2,4},{7,5},{4,6},{9,7},{6,8},{11,9},{8,10... | collective-permute-start | bytes 786440 | tf_op jit(solution)/shard_map/ppermute | solution.py:438
  12.3 9.4 %collective-permute-start.4 = (bf16[128,1024]{1,0:T(8,128)(2,1)S(1)}, bf16[128,1024]{1,0:T(8,128)(2,1)S(1)}, u32[]{:S(2)}, u32[]{:S(2)}) collective-permute-start(bf16[128,1024]{1,0:T(8,128)(2,1)S(1)} %get-tuple-element.61), channel_id=1, source_target_pairs={{2,0},{0,1},{4,2},{1,3},{6,4},{3,5},{8,6},{5,7},{10,8},{7,9},{12,1... | collective-permute-start | bytes 786440 | tf_op jit(solution)/shard_map/ppermute | solution.py:438
  12.3 9.4 %collective-permute-start.2 = (bf16[128,1024]{1,0:T(8,128)(2,1)S(1)}, bf16[128,1024]{1,0:T(8,128)(2,1)S(1)}, u32[]{:S(2)}, u32[]{:S(2)}) collective-permute-start(bf16[128,1024]{1,0:T(8,128)(2,1)S(1)} %get-tuple-element.61), channel_id=1, source_target_pairs={{0,1},{1,0},{2,3},{3,2},{4,5},{5,4},{6,7},{7,6},{8,9},{9,8},{10,11... | collective-permute-start | bytes 786440 | tf_op jit(solution)/shard_map/ppermute | solution.py:427
  13.1 11.5 %collective-permute-start.3 = (bf16[128,1024]{1,0:T(8,128)(2,1)S(1)}, bf16[128,1024]{1,0:T(8,128)(2,1)S(1)}, u32[]{:S(2)}, u32[]{:S(2)}) collective-permute-start(bf16[128,1024]{1,0:T(8,128)(2,1)S(1)} %get-tuple-element.60.own_kv.own), channel_id=1, source_target_pairs={{2,0},{0,1},{4,2},{1,3},{6,4},{3,5},{8,6},{5,7},{10,8},{7,9},{12,1... | collective-permute-start | bytes 786440 | tf_op jit(solution)/shard_map/ppermute | solution.py:438
  17.5 7.1 %collective-permute-start.7 = (bf16[128,1024]{1,0:T(8,128)(2,1)S(1)}, bf16[128,1024]{1,0:T(8,128)(2,1)S(1)}, u32[]{:S(2)}, u32[]{:S(2)}) collective-permute-start(bf16[128,1024]{1,0:T(8,128)(2,1)S(1)} %collective-permute-done.6.half_same), channel_id=1, source_target_pairs={{0,1},{1,0},{2,3},{3,2},{4,5},{5,4},{6,7},{7,6},{8,9},{9,8},{10,11... | collective-permute-start | bytes 786440 | tf_op jit(solution)/shard_map/ppermute | solution.py:427
  21.8 2.8 %collective-permute-start.5 = (bf16[128,1024]{1,0:T(8,128)(2,1)S(1)}, bf16[128,1024]{1,0:T(8,128)(2,1)S(1)}, u32[]{:S(2)}, u32[]{:S(2)}) collective-permute-start(bf16[128,1024]{1,0:T(8,128)(2,1)S(1)} %collective-permute-done.4), channel_id=1, source_target_pairs={{0,1},{1,0},{2,3},{3,2},{4,5},{5,4},{6,7},{7,6},{8,9},{9,8},{10,11... | collective-permute-start | bytes 786440 | tf_op jit(solution)/shard_map/ppermute | solution.py:427
  25.5 8.8 %collective-permute-start.11 = (bf16[64,1024]{1,0:T(8,128)(2,1)S(1)}, bf16[64,1024]{1,0:T(8,128)(2,1)S(1)}, u32[]{:S(2)}, u32[]{:S(2)}) collective-permute-start(bf16[64,1024]{1,0:T(8,128)(2,1)S(1)} %get-tuple-element.73), channel_id=1, source_target_pairs={{10,0},{11,1},{8,2},{9,3},{14,4},{15,5},{12,6},{13,7},{2,8},{3,9},... | collective-permute-start | bytes 393224 | tf_op jit(solution)/shard_map/ppermute | solution.py:438
  25.6 16.6 %collective-permute-start.13 = (bf16[64,1024]{1,0:T(8,128)(2,1)S(1)}, bf16[64,1024]{1,0:T(8,128)(2,1)S(1)}, u32[]{:S(2)}, u32[]{:S(2)}) collective-permute-start(bf16[64,1024]{1,0:T(8,128)(2,1)S(1)} %get-tuple-element.73), channel_id=1, source_target_pairs={{12,0},{13,1},{14,2},{15,3},{6,4},{7,5},{4,6},{5,7},{20,8},{21,9},... | collective-permute-start | bytes 393224 | tf_op jit(solution)/shard_map/ppermute | solution.py:438
  25.7 13.5 %collective-permute-start.8 = (bf16[64,1024]{1,0:T(8,128)(2,1)S(1)}, bf16[64,1024]{1,0:T(8,128)(2,1)S(1)}, u32[]{:S(2)}, u32[]{:S(2)}) collective-permute-start(bf16[64,1024]{1,0:T(8,128)(2,1)S(1)} %get-tuple-element.70), channel_id=1, source_target_pairs={{1,0},{3,1},{0,2},{5,3},{2,4},{7,5},{4,6},{9,7},{6,8},{11,9},{8,10... | collective-permute-start | bytes 393224 | tf_op jit(solution)/shard_map/ppermute | solution.py:438
  29.6 12.5 %collective-permute-start.9 = (bf16[64,1024]{1,0:T(8,128)(2,1)S(1)}, bf16[64,1024]{1,0:T(8,128)(2,1)S(1)}, u32[]{:S(2)}, u32[]{:S(2)}) collective-permute-start(bf16[64,1024]{1,0:T(8,128)(2,1)S(1)} %get-tuple-element.71), channel_id=1, source_target_pairs={{2,0},{0,1},{4,2},{1,3},{6,4},{3,5},{8,6},{5,7},{10,8},{7,9},{12,1... | collective-permute-start | bytes 393224 | tf_op jit(solution)/shard_map/ppermute | solution.py:438
  29.6 12.5 %collective-permute-start.10 = (bf16[64,1024]{1,0:T(8,128)(2,1)S(1)}, bf16[64,1024]{1,0:T(8,128)(2,1)S(1)}, u32[]{:S(2)}, u32[]{:S(2)}) collective-permute-start(bf16[64,1024]{1,0:T(8,128)(2,1)S(1)} %get-tuple-element.72), channel_id=1, source_target_pairs={{4,0},{5,1},{0,2},{1,3},{8,4},{9,5},{2,6},{3,7},{12,8},{13,9},{6,1... | collective-permute-start | bytes 393224 | tf_op jit(solution)/shard_map/ppermute | solution.py:438
  34.2 10.1 %collective-permute-start.12 = (bf16[64,1024]{1,0:T(8,128)(2,1)S(1)}, bf16[64,1024]{1,0:T(8,128)(2,1)S(1)}, u32[]{:S(2)}, u32[]{:S(2)}) collective-permute-start(bf16[64,1024]{1,0:T(8,128)(2,1)S(1)} %collective-permute-done.11.z3), channel_id=1, source_target_pairs={{14,0},{15,1},{12,2},{13,3},{10,4},{11,5},{8,6},{9,7},{24,8},{25,9... | collective-permute-start | bytes 393224 | tf_op jit(solution)/shard_map/ppermute | solution.py:438
  34.2 1.0 %copy-start.2 = (bf16[128,1024]{1,0:T(8,128)(2,1)S(1)}, bf16[128,1024]{1,0:T(8,128)(2,1)}, u32[]{:S(2)}) copy-start(bf16[128,1024]{1,0:T(8,128)(2,1)} %q.1) | copy-start | bytes 786436
  35.2 0.9 %copy-start.3 = (bf16[128,1024]{1,0:T(8,128)(2,1)S(1)}, bf16[128,1024]{1,0:T(8,128)(2,1)}, u32[]{:S(2)}) copy-start(bf16[128,1024]{1,0:T(8,128)(2,1)} %g.1) | copy-start | bytes 786436
  46.7 4.4 %collective-permute-start.14 = (bf16[64,1024]{1,0:T(8,128)(2,1)S(1)}, bf16[64,1024]{1,0:T(8,128)(2,1)S(1)}, u32[]{:S(2)}, u32[]{:S(2)}) collective-permute-start(bf16[64,1024]{1,0:T(8,128)(2,1)S(1)} %get-tuple-element.75), channel_id=1, source_target_pairs={{0,14},{1,15},{2,12},{3,13},{4,10},{5,11},{6,8},{7,9},{8,24},{9,25... | collective-permute-start | bytes 393224 | tf_op jit(solution)/shard_map/ppermute | solution.py:441
  46.8 14.0 %collective-permute-start.15 = (bf16[64,1024]{1,0:T(8,128)(2,1)S(1)}, bf16[64,1024]{1,0:T(8,128)(2,1)S(1)}, u32[]{:S(2)}, u32[]{:S(2)}) collective-permute-start(bf16[64,1024]{1,0:T(8,128)(2,1)S(1)} %get-tuple-element.86), channel_id=1, source_target_pairs={{0,12},{1,13},{2,14},{3,15},{4,6},{5,7},{6,4},{7,5},{8,20},{9,21},... | collective-permute-start | bytes 393224 | tf_op jit(solution)/shard_map/ppermute | solution.py:441
  49.2 11.6 %collective-permute-start.17 = (bf16[64,1024]{1,0:T(8,128)(2,1)S(1)}, bf16[64,1024]{1,0:T(8,128)(2,1)S(1)}, u32[]{:S(2)}, u32[]{:S(2)}) collective-permute-start(bf16[64,1024]{1,0:T(8,128)(2,1)S(1)} %get-tuple-element.88), channel_id=1, source_target_pairs={{0,1},{1,3},{2,0},{3,5},{4,2},{5,7},{6,4},{7,9},{8,6},{9,11},{10,8... | collective-permute-start | bytes 393224 | tf_op jit(solution)/shard_map/ppermute | solution.py:441
  51.2 9.7 %collective-permute-start.16 = (bf16[64,1024]{1,0:T(8,128)(2,1)S(1)}, bf16[64,1024]{1,0:T(8,128)(2,1)S(1)}, u32[]{:S(2)}, u32[]{:S(2)}) collective-permute-start(bf16[64,1024]{1,0:T(8,128)(2,1)S(1)} %add.7), channel_id=1, source_target_pairs={{0,10},{1,11},{2,8},{3,9},{4,14},{5,15},{6,12},{7,13},{8,2},{9,3},... | collective-permute-start | bytes 393224 | tf_op jit(solution)/shard_map/ppermute | solution.py:441
  54.8 9.5 %collective-permute-start.18 = (bf16[64,1024]{1,0:T(8,128)(2,1)S(1)}, bf16[64,1024]{1,0:T(8,128)(2,1)S(1)}, u32[]{:S(2)}, u32[]{:S(2)}) collective-permute-start(bf16[64,1024]{1,0:T(8,128)(2,1)S(1)} %get-tuple-element.89), channel_id=1, source_target_pairs={{0,2},{1,0},{2,4},{3,1},{4,6},{5,3},{6,8},{7,5},{8,10},{9,7},{10,1... | collective-permute-start | bytes 393224 | tf_op jit(solution)/shard_map/ppermute | solution.py:441
  56.9 10.2 %collective-permute-start.19 = (bf16[64,1024]{1,0:T(8,128)(2,1)S(1)}, bf16[64,1024]{1,0:T(8,128)(2,1)S(1)}, u32[]{:S(2)}, u32[]{:S(2)}) collective-permute-start(bf16[64,1024]{1,0:T(8,128)(2,1)S(1)} %get-tuple-element.90), channel_id=1, source_target_pairs={{0,4},{1,5},{2,0},{3,1},{4,8},{5,9},{6,2},{7,3},{8,12},{9,13},{10,... | collective-permute-start | bytes 393224 | tf_op jit(solution)/shard_map/ppermute | solution.py:441
  68.1 8.1 %collective-permute-start.20 = (f32[128,2048]{1,0:T(8,128)S(1)}, f32[128,2048]{1,0:T(8,128)S(1)}, u32[]{:S(2)}, u32[]{:S(2)}) collective-permute-start(f32[128,2048]{1,0:T(8,128)S(1)} %get-tuple-element.92), channel_id=1, source_target_pairs={{0,1},{1,0},{2,3},{3,2},{4,5},{5,4},{6,7},{7,6},{8,9},{9,8},{10,11... | collective-permute-start | bytes 3145736 | tf_op jit(solution)/shard_map/ppermute | solution.py:427
  69.8 4.3 %collective-permute-start.23 = (bf16[128,1024]{1,0:T(8,128)(2,1)S(1)}, bf16[128,1024]{1,0:T(8,128)(2,1)S(1)}, u32[]{:S(2)}, u32[]{:S(2)}) collective-permute-start(bf16[128,1024]{1,0:T(8,128)(2,1)S(1)} %get-tuple-element.101), channel_id=1, source_target_pairs={{0,1},{1,0},{2,3},{3,2},{4,5},{5,4},{6,7},{7,6},{8,9},{9,8},{10,11... | collective-permute-start | bytes 786440 | tf_op jit(solution)/shard_map/ppermute | solution.py:427
  69.9 6.3 %collective-permute-start.26 = (bf16[64,1024]{1,0:T(8,128)(2,1)S(1)}, bf16[64,1024]{1,0:T(8,128)(2,1)S(1)}, u32[]{:S(2)}, u32[]{:S(2)}) collective-permute-start(bf16[64,1024]{1,0:T(8,128)(2,1)S(1)} %get-tuple-element.103), channel_id=1, source_target_pairs={{0,1},{1,0},{2,3},{3,2},{4,5},{5,4},{6,7},{7,6},{8,9},{9,8},{10,11... | collective-permute-start | bytes 393224 | tf_op jit(solution)/shard_map/ppermute | solution.py:427
  70.4 15.6 %collective-permute-start.22 = (bf16[128,1024]{1,0:T(8,128)(2,1)S(1)}, bf16[128,1024]{1,0:T(8,128)(2,1)S(1)}, u32[]{:S(2)}, u32[]{:S(2)}) collective-permute-start(bf16[128,1024]{1,0:T(8,128)(2,1)S(1)} %get-tuple-element.100), channel_id=1, source_target_pairs={{0,2},{1,0},{2,4},{3,1},{4,6},{5,3},{6,8},{7,5},{8,10},{9,7},{10,1... | collective-permute-start | bytes 786440 | tf_op jit(solution)/shard_map/ppermute | solution.py:441
  74.1 11.9 %collective-permute-start.24 = (bf16[128,1024]{1,0:T(8,128)(2,1)S(1)}, bf16[128,1024]{1,0:T(8,128)(2,1)S(1)}, u32[]{:S(2)}, u32[]{:S(2)}) collective-permute-start(bf16[128,1024]{1,0:T(8,128)(2,1)S(1)} %collective-permute-done.23), channel_id=1, source_target_pairs={{0,2},{1,0},{2,4},{3,1},{4,6},{5,3},{6,8},{7,5},{8,10},{9,7},{10,1... | collective-permute-start | bytes 786440 | tf_op jit(solution)/shard_map/ppermute | solution.py:441
  76.2 8.3 %collective-permute-start.25 = (bf16[64,1024]{1,0:T(8,128)(2,1)S(1)}, bf16[64,1024]{1,0:T(8,128)(2,1)S(1)}, u32[]{:S(2)}, u32[]{:S(2)}) collective-permute-start(bf16[64,1024]{1,0:T(8,128)(2,1)S(1)} %get-tuple-element.102), channel_id=1, source_target_pairs={{0,1},{1,3},{2,0},{3,5},{4,2},{5,7},{6,4},{7,9},{8,6},{9,11},{10,8... | collective-permute-start | bytes 393224 | tf_op jit(solution)/shard_map/ppermute | solution.py:441
  76.3 9.7 %collective-permute-start.27 = (bf16[64,1024]{1,0:T(8,128)(2,1)S(1)}, bf16[64,1024]{1,0:T(8,128)(2,1)S(1)}, u32[]{:S(2)}, u32[]{:S(2)}) collective-permute-start(bf16[64,1024]{1,0:T(8,128)(2,1)S(1)} %collective-permute-done.26), channel_id=1, source_target_pairs={{0,1},{1,3},{2,0},{3,5},{4,2},{5,7},{6,4},{7,9},{8,6},{9,11},{10,8... | collective-permute-start | bytes 393224 | tf_op jit(solution)/shard_map/ppermute | solution.py:441
  76.3 4.4 %collective-permute-start.21 = (bf16[16,1024]{1,0:T(8,128)(2,1)S(1)}, bf16[16,1024]{1,0:T(8,128)(2,1)S(1)}, u32[]{:S(2)}, u32[]{:S(2)}) collective-permute-start(bf16[16,1024]{1,0:T(8,128)(2,1)S(1)} %get-tuple-element.99), channel_id=1, source_target_pairs={{0,1},{1,0},{2,3},{3,2},{4,5},{5,4},{6,7},{7,6},{8,9},{9,8},{10,11... | collective-permute-start | bytes 98312 | tf_op jit(solution)/shard_map/ppermute | solution.py:427
where the time goes:
time: 89.1 us; the launch traced here: 88 us
  starting transfers between devices  36.4 us (41%)
  waiting for transfers between devices  32.4 us (36%)
  Pallas kernels  14.3 us (16%)
  local copies, waits for them, and re-layouts  3.8 us (4%)
  between operations  0.96 us (1%)
    ppermute x9, waiting for transfers between devices, fetch(): return lax.ppermute(x, AXES, pairs(name))  19 us
    ppermute x10, starting transfers between devices, give(): return lax.ppermute(x, AXES, [(b, a) for a, b in pairs(name)])  14.9 us
    pallas_call x8, Pallas kernels, call(): pl.pallas_call(kernel, out_shape=[jax.ShapeDtypeStruct(shape, dtype) for...  14.3 us
    ppermute x10, waiting for transfers between devices, give(): return lax.ppermute(x, AXES, [(b, a) for a, b in pairs(name)])  13.4 us
    ppermute x9, starting transfers between devices, fetch(): return lax.ppermute(x, AXES, pairs(name))  13.4 us
    ppermute x9, starting transfers between devices, swap(): return lax.ppermute(x, AXES, [(i, i ^ 1) for i in range(devices)])  8.15 us
    unnamed x8, local copies, waits for them, and re-layouts  3.8 us
  transfers between devices with their start and end apart: 28, of which 12 were waited for; matrix products, arithmetic and copies ran while one was open for 0% of the time, Pallas kernels for 9%

commit v1 on v0

--- a/solution.py
+++ b/solution.py
@@ -75,17 +75,22 @@
 ):
     even = (where[0] // 2) % 2 == 0
     first = where[0] % 2 == 0
-    low, high, fine_below, fine_above, half_below, half_above = sides(
-        first, own, recv, fine_same, fine_cross, half_same, half_cross
-    )
     fine = jnp.concatenate([pool_matrix(32, BLOCK, 4), pool_matrix(16, BLOCK, 8)], axis=0)
     half = jnp.concatenate([pool_matrix(32, 64, 2), pool_matrix(16, 64, 4)], axis=0)
-    own_low = dot(fine[32:48], low).astype(BF16)
-    own_high = dot(fine[32:48], high).astype(BF16)
-    below_low = dot(half, half_below).astype(BF16)
-    below_high = dot(fine, fine_below).astype(BF16)
-    above_low = dot(fine, fine_above).astype(BF16)
-    above_high = dot(half, half_above).astype(BF16)
+    eighth = pool_matrix(16, BLOCK, 8)
+    pooled = [
+        dot(eighth, own[...]),
+        dot(eighth, recv[...]),
+        dot(fine, fine_same[...]),
+        dot(fine, fine_cross[...]),
+        dot(half, half_same[0:64]),
+        dot(half, half_cross[64:128]),
+    ]
+    mine, other, same, cross, part_same, part_cross = [x.astype(BF16) for x in pooled]
+    own_low, own_high = jnp.where(first, mine, other), jnp.where(first, other, mine)
+    below_high, above_low = jnp.where(first, cross, same), jnp.where(first, same, cross)
+    below_low = jnp.where(first, part_same, part_cross)
+    above_high = jnp.where(first, part_cross, part_same)
     b2 = jnp.concatenate([below_low[0:32], below_high[0:32]], axis=0)
     a2 = jnp.concatenate([above_low[0:32], above_high[0:32]], axis=0)
     same2[...] = jnp.where(first, b2, a2)
@@ -348,44 +353,48 @@
     qg[:, other] = out_recv[:, 512:1024]
 
 
-def final_kernel(
-    where, keep, recv, keep3, recv3, fine_same, fine_cross, half_same, half_cross,
-    kg, vg, total, sems,
-):
-    core = where[0] % 2
+def write_columns(where, turn, own, fine, half, last, kg, vg, total, sems):
+    side = (where[0] + turn) % 2
     matrix = jnp.concatenate([spread_matrix(BLOCK, 64, 2), spread_matrix(BLOCK, 16, 8)], axis=1)
+    coarse = jnp.concatenate([half[...], last[...]], axis=0)
     copies = []
-    for n, (side, own, fine, half, last) in enumerate(
-        (
-            (core, keep, fine_same, half_same, keep3),
-            (1 - core, recv, fine_cross, half_cross, recv3),
-        )
-    ):
-        coarse = jnp.concatenate([half[...], last[...]], axis=0)
-        total[n] = own[:, PAIR : 2 * PAIR] + fine[...].astype(F32) + dot(matrix, coarse)
-        for m, target in enumerate((kg, vg)):
-            copies.append(
-                pltpu.make_async_copy(
-                    total.at[n, :, HALF * m : HALF * (m + 1)],
-                    target.at[:, half_columns(side)],
-                    sems.at[2 * n + m],
-                )
+    for m, target in enumerate((kg, vg)):
+        columns = slice(HALF * m, HALF * (m + 1))
+        total[:, columns] = (
+            own[:, PAIR + HALF * m : PAIR + HALF * (m + 1)]
+            + fine[:, columns].astype(F32)
+            + dot(matrix, coarse[:, columns])
+        )
+        copies.append(
+            pltpu.make_async_copy(
+                total.at[:, columns], target.at[:, half_columns(side)], sems.at[m]
             )
-            copies[-1].start()
+        )
+        copies[-1].start()
     for copy in copies:
         copy.wait()
 
 
-def call(kernel, where, args, outs, scratch=(), space=pltpu.VMEM):
+def final_same_kernel(where, own, fine, half, last, kg, vg, total, sems):
+    write_columns(where, 0, own, fine, half, last, kg, vg, total, sems)
+
+
+def final_cross_kernel(where, own, fine, half, last, kg_in, vg_in, kg, vg, total, sems):
+    write_columns(where, 1, own, fine, half, last, kg, vg, total, sems)
+
+
+def call(kernel, where, args, outs, scratch=(), space=pltpu.VMEM, into=()):
     return pl.pallas_call(
         kernel,
         out_shape=[jax.ShapeDtypeStruct(shape, dtype) for shape, dtype in outs],
         in_specs=[pl.BlockSpec(memory_space=pltpu.SMEM)]
-        + [pl.BlockSpec(memory_space=pltpu.VMEM)] * len(args),
+        + [pl.BlockSpec(memory_space=pltpu.VMEM)] * len(args)
+        + [pl.BlockSpec(memory_space=pl.ANY)] * len(into),
         out_specs=[pl.BlockSpec(memory_space=space)] * len(outs),
         scratch_shapes=list(scratch),
         compiler_params=pltpu.CompilerParams(vmem_limit_bytes=32 * 1024 * 1024),
-    )(where, *args)
+        input_output_aliases={1 + len(args) + n: n for n in range(len(into))},
+    )(where, *args, *into)
 
 
 def sources(chips):
@@ -527,13 +536,23 @@
         join_kernel, where, (keep, recv), [((BLOCK, PAIR), BF16), ((BLOCK, PAIR), F32)]
     )
     attended, query_grad, keep3 = lax.optimization_barrier((attended, query_grad, keep3))
+    work = [pltpu.VMEM((BLOCK, PAIR), F32), pltpu.SemaphoreType.DMA((2,))]
+    written = call(
+        final_same_kernel,
+        where,
+        (keep, fine_same, half_same, keep3),
+        [((BLOCK, PAIR), F32)] * 2,
+        scratch=work,
+        space=pl.ANY,
+    )
     key_grad, value_grad = call(
-        final_kernel,
+        final_cross_kernel,
         where,
-        (keep, recv, keep3, recv3, fine_same, fine_cross, half_same, half_cross),
+        (recv, fine_cross, half_cross, recv3),
         [((BLOCK, PAIR), F32)] * 2,
-        scratch=[pltpu.VMEM((2, BLOCK, PAIR), F32), pltpu.SemaphoreType.DMA((4,))],
+        scratch=work,
         space=pl.ANY,
+        into=written,
     )
     return attended, query_grad, key_grad, value_grad
 

time: 89.1 us -> 89.8 us (level)
  waiting for transfers between devices: 32.4 us -> 30.6 us
  starting transfers between devices: 36.4 us -> 37.8 us
  Pallas kernels: 14.3 us -> 15.6 us
    ppermute x10, waiting for transfers between devices: 13.4 us -> 11.6 us  [give(): return lax.ppermute(x, AXES, [(b, a) for a, b in pairs(name)])]
    pallas_call x8 -> x9, Pallas kernels: 14.3 us -> 15.6 us  [call(): pl.pallas_call(kernel, out_shape=[jax.ShapeDtypeStruct(shape, dtype) for...]
  transfers between devices with their start and end apart: 28 -> 28, of which waited for: 12 -> 11; matrix products, arithmetic and copies ran while one was open for 0% -> 0% of each run, Pallas kernels for 9% -> 11%
where the time goes in v1:
time: 89.8 us; the launch traced here: 88.9 us
  starting transfers between devices  37.8 us (42%)
  waiting for transfers between devices  30.6 us (34%)
  Pallas kernels  15.6 us (17%)
  local copies, waits for them, and re-layouts  3.8 us (4%)
  between operations  0.99 us (1%)
    ppermute x9, waiting for transfers between devices, fetch(): return lax.ppermute(x, AXES, pairs(name))  19 us
    pallas_call x9, Pallas kernels, call(): pl.pallas_call(kernel, out_shape=[jax.ShapeDtypeStruct(shape, dtype) for...  15.6 us
    ppermute x10, starting transfers between devices, give(): return lax.ppermute(x, AXES, [(b, a) for a, b in pairs(name)])  15.4 us
    ppermute x9, starting transfers between devices, fetch(): return lax.ppermute(x, AXES, pairs(name))  13.4 us
    ppermute x10, waiting for transfers between devices, give(): return lax.ppermute(x, AXES, [(b, a) for a, b in pairs(name)])  11.6 us
    ppermute x9, starting transfers between devices, swap(): return lax.ppermute(x, AXES, [(i, i ^ 1) for i in range(devices)])  8.99 us
    unnamed x8, local copies, waits for them, and re-layouts  3.8 us
  transfers between devices with their start and end apart: 28, of which 11 were waited for; matrix products, arithmetic and copies ran while one was open for 0% of the time, Pallas kernels for 11%

profile of v1, /device:TPU:25, one launch (start us, length us, event | category | flops | bytes accessed | tf_op | source)
XLA Modules:
  0.0 88.9 jit_solution(11431394536587862250)
XLA Ops:
  0.6 0.8 collective-permute-start
  1.4 0.1 collective-permute-start.1
  1.5 0.1 pad_add_fusion.where
  1.6 0.9 %copy-done = bf16[128,1024]{1,0:T(8,128)(2,1)S(1)} copy-done((bf16[128,1024]{1,0:T(8,128)(2,1)S(1)}, bf16[128,1024]{1,0:T(8,128)(2,1)}, u32[]{:S(2)}) %copy-start) | copy-done | bytes 262168
  2.5 0.9 %copy-done.1 = bf16[128,1024]{1,0:T(8,128)(2,1)S(1)} copy-done((bf16[128,1024]{1,0:T(8,128)(2,1)S(1)}, bf16[128,1024]{1,0:T(8,128)(2,1)}, u32[]{:S(2)}) %copy-start.1) | copy-done | bytes 262168
  3.5 0.8 shard_map.75
  4.3 0.0 collective-permute-done.recv_q
  4.3 0.0 collective-permute-done.1.recv_g
  4.3 8.0 %collective-permute-start.6 = (bf16[128,1024]{1,0:T(8,128)(2,1)S(1)}, bf16[128,1024]{1,0:T(8,128)(2,1)S(1)}, u32[]{:S(2)}, u32[]{:S(2)}) collective-permute-start(bf16[128,1024]{1,0:T(8,128)(2,1)S(1)} %get-tuple-element.64), channel_id=1, source_target_pairs={{1,0},{3,1},{0,2},{5,3},{2,4},{7,5},{4,6},{9,7},{6,8},{11,9},{8,10... | collective-permute-start | bytes 786440 | tf_op jit(solution)/shard_map/ppermute | solution.py:447
  12.3 0.0 collective-permute-start.4
  12.3 0.8 collective-permute-start.2
  13.1 0.0 collective-permute-start.3
  13.1 4.4 %collective-permute-done.6.half_same = bf16[128,1024]{1,0:T(8,128)(2,1)S(1)} collective-permute-done((bf16[128,1024]{1,0:T(8,128)(2,1)S(1)}, bf16[128,1024]{1,0:T(8,128)(2,1)S(1)}, u32[]{:S(2)}, u32[]{:S(2)}) %collective-permute-start.6) | collective-permute-done | bytes 262176 | tf_op jit(solution)/shard_map/ppermute | solution.py:447
  17.5 1.3 %collective-permute-start.7 = (bf16[128,1024]{1,0:T(8,128)(2,1)S(1)}, bf16[128,1024]{1,0:T(8,128)(2,1)S(1)}, u32[]{:S(2)}, u32[]{:S(2)}) collective-permute-start(bf16[128,1024]{1,0:T(8,128)(2,1)S(1)} %collective-permute-done.6.half_same), channel_id=1, source_target_pairs={{0,1},{1,0},{2,3},{3,2},{4,5},{5,4},{6,7},{7,6},{8,9},{9,8},{10,11... | collective-permute-start | bytes 786440 | tf_op jit(solution)/shard_map/ppermute | solution.py:436
  18.8 3.0 %collective-permute-done.4 = bf16[128,1024]{1,0:T(8,128)(2,1)S(1)} collective-permute-done((bf16[128,1024]{1,0:T(8,128)(2,1)S(1)}, bf16[128,1024]{1,0:T(8,128)(2,1)S(1)}, u32[]{:S(2)}, u32[]{:S(2)}) %collective-permute-start.4) | collective-permute-done | bytes 262176 | tf_op jit(solution)/shard_map/ppermute | solution.py:447
  21.8 0.0 collective-permute-start.5
  21.8 0.0 collective-permute-done.2.recv_kv.recv
  21.8 2.8 %collective-permute-done.3.fine_same = bf16[128,1024]{1,0:T(8,128)(2,1)S(1)} collective-permute-done((bf16[128,1024]{1,0:T(8,128)(2,1)S(1)}, bf16[128,1024]{1,0:T(8,128)(2,1)S(1)}, u32[]{:S(2)}, u32[]{:S(2)}) %collective-permute-start.3) | collective-permute-done | bytes 262176 | tf_op jit(solution)/shard_map/ppermute | solution.py:447
  24.6 0.0 collective-permute-done.7.half_cross
  24.6 0.0 collective-permute-done.5.fine_cross
  24.6 0.9 %shard_map.77 = (bf16[64,1024]{1,0:T(8,128)(2,1)S(1)}, bf16[64,1024]{1,0:T(8,128)(2,1)S(1)}, bf16[64,1024]{1,0:T(8,128)(2,1)S(1)}, bf16[64,1024]{1,0:T(8,128)(2,1)S(1)}) custom-call(s32[2]{0:T(128)S(1)} %pad_add_fusion.where, bf16[128,1024]{1,0:T(8,128)(2,1)S(1)} %get-tuple-element.62.own_kv.own, bf16[128,1024]{1,0:T(8,128)(2,1)S(1)} %collective-permute-done.2.recv_kv.recv, ...), custom_call_target="tpu_custom_call" | custom-call | tf_op jit(solution)/shard_map/pallas_call | solution.py:387
  25.5 0.1 collective-permute-start.11
  25.6 0.1 collective-permute-start.13
  25.7 3.9 %collective-permute-start.8 = (bf16[64,1024]{1,0:T(8,128)(2,1)S(1)}, bf16[64,1024]{1,0:T(8,128)(2,1)S(1)}, u32[]{:S(2)}, u32[]{:S(2)}) collective-permute-start(bf16[64,1024]{1,0:T(8,128)(2,1)S(1)} %get-tuple-element.72), channel_id=1, source_target_pairs={{1,0},{3,1},{0,2},{5,3},{2,4},{7,5},{4,6},{9,7},{6,8},{11,9},{8,10... | collective-permute-start | bytes 393224 | tf_op jit(solution)/shard_map/ppermute | solution.py:447
  29.6 1.2 %collective-permute-start.10 = (bf16[64,1024]{1,0:T(8,128)(2,1)S(1)}, bf16[64,1024]{1,0:T(8,128)(2,1)S(1)}, u32[]{:S(2)}, u32[]{:S(2)}) collective-permute-start(bf16[64,1024]{1,0:T(8,128)(2,1)S(1)} %get-tuple-element.74), channel_id=1, source_target_pairs={{4,0},{5,1},{0,2},{1,3},{8,4},{9,5},{2,6},{3,7},{12,8},{13,9},{6,1... | collective-permute-start | bytes 393224 | tf_op jit(solution)/shard_map/ppermute | solution.py:447
  30.8 3.4 %collective-permute-done.11.z3 = bf16[64,1024]{1,0:T(8,128)(2,1)S(1)} collective-permute-done((bf16[64,1024]{1,0:T(8,128)(2,1)S(1)}, bf16[64,1024]{1,0:T(8,128)(2,1)S(1)}, u32[]{:S(2)}, u32[]{:S(2)}) %collective-permute-start.11) | collective-permute-done | bytes 131104 | tf_op jit(solution)/shard_map/ppermute | solution.py:447
  34.2 0.0 collective-permute-start.12
  34.3 0.9 %copy-done.2 = bf16[128,1024]{1,0:T(8,128)(2,1)S(1)} copy-done((bf16[128,1024]{1,0:T(8,128)(2,1)S(1)}, bf16[128,1024]{1,0:T(8,128)(2,1)}, u32[]{:S(2)}) %copy-start.2) | copy-done | bytes 262168
  35.2 0.9 %copy-done.3 = bf16[128,1024]{1,0:T(8,128)(2,1)S(1)} copy-done((bf16[128,1024]{1,0:T(8,128)(2,1)S(1)}, bf16[128,1024]{1,0:T(8,128)(2,1)}, u32[]{:S(2)}) %copy-start.3) | copy-done | bytes 262168
  36.2 2.8 %shard_map.76 = (bf16[256,512]{1,0:T(8,128)(2,1)S(1)}, bf16[256,512]{1,0:T(8,128)(2,1)S(1)}, bf16[768,1024]{1,0:T(8,128)(2,1)S(1)}, f32[2304,256]{1,0:T(8,128)S(...) custom-call(s32[2]{0:T(128)S(1)} %pad_add_fusion.where, ...), custom_call_target="tpu_custom_call" | custom-call | tf_op jit(solution)/shard_map/pallas_call | solution.py:387
  39.0 0.2 collective-permute-done.8.m2
  39.2 2.9 %collective-permute-done.9.p2 = bf16[64,1024]{1,0:T(8,128)(2,1)S(1)} collective-permute-done((bf16[64,1024]{1,0:T(8,128)(2,1)S(1)}, bf16[64,1024]{1,0:T(8,128)(2,1)S(1)}, u32[]{:S(2)}, u32[]{:S(2)}) %collective-permute-start.9) | collective-permute-done | bytes 131104 | tf_op jit(solution)/shard_map/ppermute | solution.py:447
  42.2 2.2 %collective-permute-done.12.x3 = bf16[64,1024]{1,0:T(8,128)(2,1)S(1)} collective-permute-done((bf16[64,1024]{1,0:T(8,128)(2,1)S(1)}, bf16[64,1024]{1,0:T(8,128)(2,1)S(1)}, u32[]{:S(2)}, u32[]{:S(2)}) %collective-permute-start.12) | collective-permute-done | bytes 131104 | tf_op jit(solution)/shard_map/ppermute | solution.py:447
  44.4 2.3 %shard_map.78 = (f32[256,512]{1,0:T(8,128)S(1)}, f32[8,256]{1,0:T(8,128)S(1)}, bf16[1536,256]{1,0:T(8,128)(2,1)S(1)}, bf16[64,1024]{1,0:T(8,128)(2,1)S(1)}, bf16...) custom-call(s32[2]{0:T(128)S(1)} %pad_add_fusion.where, ...), custom_call_target="tpu_custom_call" | custom-call | tf_op jit(solution)/shard_map/pallas_call | solution.py:387
  46.7 0.1 collective-permute-start.14
  46.8 2.5 %collective-permute-start.15 = (bf16[64,1024]{1,0:T(8,128)(2,1)S(1)}, bf16[64,1024]{1,0:T(8,128)(2,1)S(1)}, u32[]{:S(2)}, u32[]{:S(2)}) collective-permute-start(bf16[64,1024]{1,0:T(8,128)(2,1)S(1)} %get-tuple-element.88), channel_id=1, source_target_pairs={{0,12},{1,13},{2,14},{3,15},{4,6},{5,7},{6,4},{7,5},{8,20},{9,21},... | collective-permute-start | bytes 393224 | tf_op jit(solution)/shard_map/ppermute | solution.py:450
  49.3 0.0 collective-permute-start.17
  49.3 1.9 %collective-permute-done.14 = bf16[64,1024]{1,0:T(8,128)(2,1)S(1)} collective-permute-done((bf16[64,1024]{1,0:T(8,128)(2,1)S(1)}, bf16[64,1024]{1,0:T(8,128)(2,1)S(1)}, u32[]{:S(2)}, u32[]{:S(2)}) %collective-permute-start.14) | collective-permute-done | bytes 131104 | tf_op jit(solution)/shard_map/ppermute | solution.py:450
  51.2 3.6 %collective-permute-start.16 = (bf16[64,1024]{1,0:T(8,128)(2,1)S(1)}, bf16[64,1024]{1,0:T(8,128)(2,1)S(1)}, u32[]{:S(2)}, u32[]{:S(2)}) collective-permute-start(bf16[64,1024]{1,0:T(8,128)(2,1)S(1)} %add.7), channel_id=1, source_target_pairs={{0,10},{1,11},{2,8},{3,9},{4,14},{5,15},{6,12},{7,13},{8,2},{9,3},... | collective-permute-start | bytes 393224 | tf_op jit(solution)/shard_map/ppermute | solution.py:450
  54.8 2.1 %collective-permute-start.18 = (bf16[64,1024]{1,0:T(8,128)(2,1)S(1)}, bf16[64,1024]{1,0:T(8,128)(2,1)S(1)}, u32[]{:S(2)}, u32[]{:S(2)}) collective-permute-start(bf16[64,1024]{1,0:T(8,128)(2,1)S(1)} %get-tuple-element.91), channel_id=1, source_target_pairs={{0,2},{1,0},{2,4},{3,1},{4,6},{5,3},{6,8},{7,5},{8,10},{9,7},{10,1... | collective-permute-start | bytes 393224 | tf_op jit(solution)/shard_map/ppermute | solution.py:450
  56.9 0.8 collective-permute-start.19
  57.7 3.2 %shard_map.79 = (f32[128,2048]{1,0:T(8,128)S(1)}, f32[128,2048]{1,0:T(8,128)S(1)}, bf16[192,1024]{1,0:T(8,128)(2,1)S(1)}, bf16[192,1024]{1,0:T(8,128)(2,1)S(1)}) custom-call(s32[2]{0:T(128)S(1)} %pad_add_fusion.where, bf16[256,512]{1,0:T(8,128)(2,1)S(1)} %get-tuple-element.65.queries, bf16[256,512]{1,0:T(8,128)(2,1)S(1)} %get-tuple-element.66.grads, ...), custom_call_target="tpu_custom_call" | custom-call | tf_op jit(solution)/shard_map/pallas_call | solution.py:387
  60.8 0.0 collective-permute-done.17.same2
  60.9 0.0 collective-permute-done.16.z3
  60.9 3.5 %collective-permute-done.18.cross2 = bf16[64,1024]{1,0:T(8,128)(2,1)S(1)} collective-permute-done((bf16[64,1024]{1,0:T(8,128)(2,1)S(1)}, bf16[64,1024]{1,0:T(8,128)(2,1)S(1)}, u32[]{:S(2)}, u32[]{:S(2)}) %collective-permute-start.18) | collective-permute-done | bytes 131104 | tf_op jit(solution)/shard_map/ppermute | solution.py:450
  64.4 2.7 %collective-permute-done.19.other2 = bf16[64,1024]{1,0:T(8,128)(2,1)S(1)} collective-permute-done((bf16[64,1024]{1,0:T(8,128)(2,1)S(1)}, bf16[64,1024]{1,0:T(8,128)(2,1)S(1)}, u32[]{:S(2)}, u32[]{:S(2)}) %collective-permute-start.19) | collective-permute-done | bytes 131104 | tf_op jit(solution)/shard_map/ppermute | solution.py:450
  67.1 1.0 %shard_map.80 = (bf16[128,1024]{1,0:T(8,128)(2,1)S(1)}, bf16[128,1024]{1,0:T(8,128)(2,1)S(1)}, bf16[64,1024]{1,0:T(8,128)(2,1)S(1)}, bf16[64,1024]{1,0:T(8,128)(...) custom-call(s32[2]{0:T(128)S(1)} %pad_add_fusion.where, ...), custom_call_target="tpu_custom_call" | custom-call | tf_op jit(solution)/shard_map/pallas_call | solution.py:387
  68.1 1.7 %collective-permute-start.20 = (f32[128,2048]{1,0:T(8,128)S(1)}, f32[128,2048]{1,0:T(8,128)S(1)}, u32[]{:S(2)}, u32[]{:S(2)}) collective-permute-start(f32[128,2048]{1,0:T(8,128)S(1)} %get-tuple-element.94), channel_id=1, source_target_pairs={{0,1},{1,0},{2,3},{3,2},{4,5},{5,4},{6,7},{7,6},{8,9},{9,8},{10,11... | collective-permute-start | bytes 3145736 | tf_op jit(solution)/shard_map/ppermute | solution.py:436
  69.9 0.1 collective-permute-start.21
  70.0 3.7 %collective-permute-start.26 = (bf16[128,1024]{1,0:T(8,128)(2,1)S(1)}, bf16[128,1024]{1,0:T(8,128)(2,1)S(1)}, u32[]{:S(2)}, u32[]{:S(2)}) collective-permute-start(bf16[128,1024]{1,0:T(8,128)(2,1)S(1)} %get-tuple-element.103), channel_id=1, source_target_pairs={{0,2},{1,0},{2,4},{3,1},{4,6},{5,3},{6,8},{7,5},{8,10},{9,7},{10,1... | collective-permute-start | bytes 786440 | tf_op jit(solution)/shard_map/ppermute | solution.py:450
  73.7 0.0 collective-permute-start.23
  73.7 0.0 collective-permute-done.21
  73.7 2.6 %collective-permute-start.22 = (bf16[128,1024]{1,0:T(8,128)(2,1)S(1)}, bf16[128,1024]{1,0:T(8,128)(2,1)S(1)}, u32[]{:S(2)}, u32[]{:S(2)}) collective-permute-start(bf16[128,1024]{1,0:T(8,128)(2,1)S(1)} %collective-permute-done.21), channel_id=1, source_target_pairs={{0,2},{1,0},{2,4},{3,1},{4,6},{5,3},{6,8},{7,5},{8,10},{9,7},{10,1... | collective-permute-start | bytes 786440 | tf_op jit(solution)/shard_map/ppermute | solution.py:450
  76.3 0.0 collective-permute-start.27
  76.3 0.0 collective-permute-done.23
  76.3 0.0 collective-permute-start.24
  76.4 0.0 collective-permute-done.20.out_recv.own
  76.4 4.2 %collective-permute-start.25 = (bf16[16,1024]{1,0:T(8,128)(2,1)S(1)}, bf16[16,1024]{1,0:T(8,128)(2,1)S(1)}, u32[]{:S(2)}, u32[]{:S(2)}) collective-permute-start(bf16[16,1024]{1,0:T(8,128)(2,1)S(1)} %get-tuple-element.102), channel_id=1, source_target_pairs={{0,1},{1,0},{2,3},{3,2},{4,5},{5,4},{6,7},{7,6},{8,9},{9,8},{10,11... | collective-permute-start | bytes 98312 | tf_op jit(solution)/shard_map/ppermute | solution.py:436
  80.6 1.5 %shard_map.81 = (bf16[128,1024]{1,0:T(8,128)(2,1)}, f32[128,1024]{1,0:T(8,128)}) custom-call(s32[2]{0:T(128)S(1)} %pad_add_fusion.where, f32[128,2048]{1,0:T(8,128)S(1)} %get-tuple-element.84.out_keep.own, f32[128,2048]{1,0:T(8,128)S(1)} %collective-permute-done.20.out_recv.own), custom_call_target="tpu_custom_call" | custom-call | tf_op jit(solution)/shard_map/pallas_call | solution.py:387
  82.0 3.5 %collective-permute-done.27.half = bf16[64,1024]{1,0:T(8,128)(2,1)S(1)} collective-permute-done((bf16[64,1024]{1,0:T(8,128)(2,1)S(1)}, bf16[64,1024]{1,0:T(8,128)(2,1)S(1)}, u32[]{:S(2)}, u32[]{:S(2)}) %collective-permute-start.27) | collective-permute-done | bytes 131104 | tf_op jit(solution)/shard_map/ppermute | solution.py:450
  85.5 1.6 %shard_map.82 = (f32[128,1024]{1,0:T(8,128)}, f32[128,1024]{1,0:T(8,128)}) custom-call(s32[2]{0:T(128)S(1)} %pad_add_fusion.where, f32[128,2048]{1,0:T(8,128)S(1)} %get-tuple-element.84.out_keep.own, bf16[128,1024]{1,0:T(8,128)(2,1)S(1)} %collective-permute-done.26.fine, bf16[64,1024]{1,0:T(8,128)(2,1)S(1)} %collective-permute-done.27.half, ...), custom_call_target="tpu_custom_call" | custom-call | tf_op jit(solution)/shard_map/pallas_call | solution.py:387
  87.1 0.0 collective-permute-done.24.half
  87.1 0.0 collective-permute-done.22.fine
  87.1 1.6 %shard_map.83 = (f32[128,1024]{1,0:T(8,128)}, f32[128,1024]{1,0:T(8,128)}) custom-call(s32[2]{0:T(128)S(1)} %pad_add_fusion.where, f32[128,2048]{1,0:T(8,128)S(1)} %collective-permute-done.20.out_recv.own, bf16[128,1024]{1,0:T(8,128)(2,1)S(1)} %collective-permute-done.22.fine, ...), custom_call_target="tpu_custom_call", output_to_operand_aliasing={{0}: (5, {}), {1}: (6, {})} | custom-call | tf_op jit(solution)/shard_map/pallas_call | solution.py:387
  (11 shorter events, 0.1 us)
Async XLA Ops:
  0.6 3.6 %collective-permute-start = (bf16[128,1024]{1,0:T(8,128)(2,1)}, bf16[128,1024]{1,0:T(8,128)(2,1)S(1)}, u32[]{:S(2)}, u32[]{:S(2)}) collective-permute-start(bf16[128,1024]{1,0:T(8,128)(2,1)} %q.1), channel_id=1, source_target_pairs={{0,1},{1,0},{2,3},{3,2},{4,5},{5,4},{6,7},{7,6},{8,9},{9,8},{10,11... | collective-permute-start | bytes 786440 | tf_op jit(solution)/shard_map/ppermute | solution.py:436
  1.4 2.9 %collective-permute-start.1 = (bf16[128,1024]{1,0:T(8,128)(2,1)}, bf16[128,1024]{1,0:T(8,128)(2,1)S(1)}, u32[]{:S(2)}, u32[]{:S(2)}) collective-permute-start(bf16[128,1024]{1,0:T(8,128)(2,1)} %g.1), channel_id=1, source_target_pairs={{0,1},{1,0},{2,3},{3,2},{4,5},{5,4},{6,7},{7,6},{8,9},{9,8},{10,11... | collective-permute-start | bytes 786440 | tf_op jit(solution)/shard_map/ppermute | solution.py:436
  1.6 0.9 %copy-start = (bf16[128,1024]{1,0:T(8,128)(2,1)S(1)}, bf16[128,1024]{1,0:T(8,128)(2,1)}, u32[]{:S(2)}) copy-start(bf16[128,1024]{1,0:T(8,128)(2,1)} %k.1) | copy-start | bytes 786436
  2.5 0.9 %copy-start.1 = (bf16[128,1024]{1,0:T(8,128)(2,1)S(1)}, bf16[128,1024]{1,0:T(8,128)(2,1)}, u32[]{:S(2)}) copy-start(bf16[128,1024]{1,0:T(8,128)(2,1)} %v.1) | copy-start | bytes 786436
  4.3 13.2 %collective-permute-start.6 = (bf16[128,1024]{1,0:T(8,128)(2,1)S(1)}, bf16[128,1024]{1,0:T(8,128)(2,1)S(1)}, u32[]{:S(2)}, u32[]{:S(2)}) collective-permute-start(bf16[128,1024]{1,0:T(8,128)(2,1)S(1)} %get-tuple-element.64), channel_id=1, source_target_pairs={{1,0},{3,1},{0,2},{5,3},{2,4},{7,5},{4,6},{9,7},{6,8},{11,9},{8,10... | collective-permute-start | bytes 786440 | tf_op jit(solution)/shard_map/ppermute | solution.py:447
  12.3 9.4 %collective-permute-start.4 = (bf16[128,1024]{1,0:T(8,128)(2,1)S(1)}, bf16[128,1024]{1,0:T(8,128)(2,1)S(1)}, u32[]{:S(2)}, u32[]{:S(2)}) collective-permute-start(bf16[128,1024]{1,0:T(8,128)(2,1)S(1)} %get-tuple-element.63), channel_id=1, source_target_pairs={{2,0},{0,1},{4,2},{1,3},{6,4},{3,5},{8,6},{5,7},{10,8},{7,9},{12,1... | collective-permute-start | bytes 786440 | tf_op jit(solution)/shard_map/ppermute | solution.py:447
  12.3 9.4 %collective-permute-start.2 = (bf16[128,1024]{1,0:T(8,128)(2,1)S(1)}, bf16[128,1024]{1,0:T(8,128)(2,1)S(1)}, u32[]{:S(2)}, u32[]{:S(2)}) collective-permute-start(bf16[128,1024]{1,0:T(8,128)(2,1)S(1)} %get-tuple-element.63), channel_id=1, source_target_pairs={{0,1},{1,0},{2,3},{3,2},{4,5},{5,4},{6,7},{7,6},{8,9},{9,8},{10,11... | collective-permute-start | bytes 786440 | tf_op jit(solution)/shard_map/ppermute | solution.py:436
  13.1 11.5 %collective-permute-start.3 = (bf16[128,1024]{1,0:T(8,128)(2,1)S(1)}, bf16[128,1024]{1,0:T(8,128)(2,1)S(1)}, u32[]{:S(2)}, u32[]{:S(2)}) collective-permute-start(bf16[128,1024]{1,0:T(8,128)(2,1)S(1)} %get-tuple-element.62.own_kv.own), channel_id=1, source_target_pairs={{2,0},{0,1},{4,2},{1,3},{6,4},{3,5},{8,6},{5,7},{10,8},{7,9},{12,1... | collective-permute-start | bytes 786440 | tf_op jit(solution)/shard_map/ppermute | solution.py:447
  17.5 7.1 %collective-permute-start.7 = (bf16[128,1024]{1,0:T(8,128)(2,1)S(1)}, bf16[128,1024]{1,0:T(8,128)(2,1)S(1)}, u32[]{:S(2)}, u32[]{:S(2)}) collective-permute-start(bf16[128,1024]{1,0:T(8,128)(2,1)S(1)} %collective-permute-done.6.half_same), channel_id=1, source_target_pairs={{0,1},{1,0},{2,3},{3,2},{4,5},{5,4},{6,7},{7,6},{8,9},{9,8},{10,11... | collective-permute-start | bytes 786440 | tf_op jit(solution)/shard_map/ppermute | solution.py:436
  21.8 2.8 %collective-permute-start.5 = (bf16[128,1024]{1,0:T(8,128)(2,1)S(1)}, bf16[128,1024]{1,0:T(8,128)(2,1)S(1)}, u32[]{:S(2)}, u32[]{:S(2)}) collective-permute-start(bf16[128,1024]{1,0:T(8,128)(2,1)S(1)} %collective-permute-done.4), channel_id=1, source_target_pairs={{0,1},{1,0},{2,3},{3,2},{4,5},{5,4},{6,7},{7,6},{8,9},{9,8},{10,11... | collective-permute-start | bytes 786440 | tf_op jit(solution)/shard_map/ppermute | solution.py:436
  25.5 8.8 %collective-permute-start.11 = (bf16[64,1024]{1,0:T(8,128)(2,1)S(1)}, bf16[64,1024]{1,0:T(8,128)(2,1)S(1)}, u32[]{:S(2)}, u32[]{:S(2)}) collective-permute-start(bf16[64,1024]{1,0:T(8,128)(2,1)S(1)} %get-tuple-element.75), channel_id=1, source_target_pairs={{10,0},{11,1},{8,2},{9,3},{14,4},{15,5},{12,6},{13,7},{2,8},{3,9},... | collective-permute-start | bytes 393224 | tf_op jit(solution)/shard_map/ppermute | solution.py:447
  25.6 16.6 %collective-permute-start.13 = (bf16[64,1024]{1,0:T(8,128)(2,1)S(1)}, bf16[64,1024]{1,0:T(8,128)(2,1)S(1)}, u32[]{:S(2)}, u32[]{:S(2)}) collective-permute-start(bf16[64,1024]{1,0:T(8,128)(2,1)S(1)} %get-tuple-element.75), channel_id=1, source_target_pairs={{12,0},{13,1},{14,2},{15,3},{6,4},{7,5},{4,6},{5,7},{20,8},{21,9},... | collective-permute-start | bytes 393224 | tf_op jit(solution)/shard_map/ppermute | solution.py:447
  25.7 13.5 %collective-permute-start.8 = (bf16[64,1024]{1,0:T(8,128)(2,1)S(1)}, bf16[64,1024]{1,0:T(8,128)(2,1)S(1)}, u32[]{:S(2)}, u32[]{:S(2)}) collective-permute-start(bf16[64,1024]{1,0:T(8,128)(2,1)S(1)} %get-tuple-element.72), channel_id=1, source_target_pairs={{1,0},{3,1},{0,2},{5,3},{2,4},{7,5},{4,6},{9,7},{6,8},{11,9},{8,10... | collective-permute-start | bytes 393224 | tf_op jit(solution)/shard_map/ppermute | solution.py:447
  29.6 12.5 %collective-permute-start.9 = (bf16[64,1024]{1,0:T(8,128)(2,1)S(1)}, bf16[64,1024]{1,0:T(8,128)(2,1)S(1)}, u32[]{:S(2)}, u32[]{:S(2)}) collective-permute-start(bf16[64,1024]{1,0:T(8,128)(2,1)S(1)} %get-tuple-element.73), channel_id=1, source_target_pairs={{2,0},{0,1},{4,2},{1,3},{6,4},{3,5},{8,6},{5,7},{10,8},{7,9},{12,1... | collective-permute-start | bytes 393224 | tf_op jit(solution)/shard_map/ppermute | solution.py:447
  29.6 12.5 %collective-permute-start.10 = (bf16[64,1024]{1,0:T(8,128)(2,1)S(1)}, bf16[64,1024]{1,0:T(8,128)(2,1)S(1)}, u32[]{:S(2)}, u32[]{:S(2)}) collective-permute-start(bf16[64,1024]{1,0:T(8,128)(2,1)S(1)} %get-tuple-element.74), channel_id=1, source_target_pairs={{4,0},{5,1},{0,2},{1,3},{8,4},{9,5},{2,6},{3,7},{12,8},{13,9},{6,1... | collective-permute-start | bytes 393224 | tf_op jit(solution)/shard_map/ppermute | solution.py:447
  34.2 10.1 %collective-permute-start.12 = (bf16[64,1024]{1,0:T(8,128)(2,1)S(1)}, bf16[64,1024]{1,0:T(8,128)(2,1)S(1)}, u32[]{:S(2)}, u32[]{:S(2)}) collective-permute-start(bf16[64,1024]{1,0:T(8,128)(2,1)S(1)} %collective-permute-done.11.z3), channel_id=1, source_target_pairs={{14,0},{15,1},{12,2},{13,3},{10,4},{11,5},{8,6},{9,7},{24,8},{25,9... | collective-permute-start | bytes 393224 | tf_op jit(solution)/shard_map/ppermute | solution.py:447
  34.2 1.0 %copy-start.2 = (bf16[128,1024]{1,0:T(8,128)(2,1)S(1)}, bf16[128,1024]{1,0:T(8,128)(2,1)}, u32[]{:S(2)}) copy-start(bf16[128,1024]{1,0:T(8,128)(2,1)} %q.1) | copy-start | bytes 786436
  35.2 0.9 %copy-start.3 = (bf16[128,1024]{1,0:T(8,128)(2,1)S(1)}, bf16[128,1024]{1,0:T(8,128)(2,1)}, u32[]{:S(2)}) copy-start(bf16[128,1024]{1,0:T(8,128)(2,1)} %g.1) | copy-start | bytes 786436
  46.7 4.4 %collective-permute-start.14 = (bf16[64,1024]{1,0:T(8,128)(2,1)S(1)}, bf16[64,1024]{1,0:T(8,128)(2,1)S(1)}, u32[]{:S(2)}, u32[]{:S(2)}) collective-permute-start(bf16[64,1024]{1,0:T(8,128)(2,1)S(1)} %get-tuple-element.77), channel_id=1, source_target_pairs={{0,14},{1,15},{2,12},{3,13},{4,10},{5,11},{6,8},{7,9},{8,24},{9,25... | collective-permute-start | bytes 393224 | tf_op jit(solution)/shard_map/ppermute | solution.py:450
  46.8 14.0 %collective-permute-start.15 = (bf16[64,1024]{1,0:T(8,128)(2,1)S(1)}, bf16[64,1024]{1,0:T(8,128)(2,1)S(1)}, u32[]{:S(2)}, u32[]{:S(2)}) collective-permute-start(bf16[64,1024]{1,0:T(8,128)(2,1)S(1)} %get-tuple-element.88), channel_id=1, source_target_pairs={{0,12},{1,13},{2,14},{3,15},{4,6},{5,7},{6,4},{7,5},{8,20},{9,21},... | collective-permute-start | bytes 393224 | tf_op jit(solution)/shard_map/ppermute | solution.py:450
  49.3 11.6 %collective-permute-start.17 = (bf16[64,1024]{1,0:T(8,128)(2,1)S(1)}, bf16[64,1024]{1,0:T(8,128)(2,1)S(1)}, u32[]{:S(2)}, u32[]{:S(2)}) collective-permute-start(bf16[64,1024]{1,0:T(8,128)(2,1)S(1)} %get-tuple-element.90), channel_id=1, source_target_pairs={{0,1},{1,3},{2,0},{3,5},{4,2},{5,7},{6,4},{7,9},{8,6},{9,11},{10,8... | collective-permute-start | bytes 393224 | tf_op jit(solution)/shard_map/ppermute | solution.py:450
  51.2 9.7 %collective-permute-start.16 = (bf16[64,1024]{1,0:T(8,128)(2,1)S(1)}, bf16[64,1024]{1,0:T(8,128)(2,1)S(1)}, u32[]{:S(2)}, u32[]{:S(2)}) collective-permute-start(bf16[64,1024]{1,0:T(8,128)(2,1)S(1)} %add.7), channel_id=1, source_target_pairs={{0,10},{1,11},{2,8},{3,9},{4,14},{5,15},{6,12},{7,13},{8,2},{9,3},... | collective-permute-start | bytes 393224 | tf_op jit(solution)/shard_map/ppermute | solution.py:450
  54.8 9.6 %collective-permute-start.18 = (bf16[64,1024]{1,0:T(8,128)(2,1)S(1)}, bf16[64,1024]{1,0:T(8,128)(2,1)S(1)}, u32[]{:S(2)}, u32[]{:S(2)}) collective-permute-start(bf16[64,1024]{1,0:T(8,128)(2,1)S(1)} %get-tuple-element.91), channel_id=1, source_target_pairs={{0,2},{1,0},{2,4},{3,1},{4,6},{5,3},{6,8},{7,5},{8,10},{9,7},{10,1... | collective-permute-start | bytes 393224 | tf_op jit(solution)/shard_map/ppermute | solution.py:450
  56.9 10.2 %collective-permute-start.19 = (bf16[64,1024]{1,0:T(8,128)(2,1)S(1)}, bf16[64,1024]{1,0:T(8,128)(2,1)S(1)}, u32[]{:S(2)}, u32[]{:S(2)}) collective-permute-start(bf16[64,1024]{1,0:T(8,128)(2,1)S(1)} %get-tuple-element.92), channel_id=1, source_target_pairs={{0,4},{1,5},{2,0},{3,1},{4,8},{5,9},{6,2},{7,3},{8,12},{9,13},{10,... | collective-permute-start | bytes 393224 | tf_op jit(solution)/shard_map/ppermute | solution.py:450
  68.1 8.2 %collective-permute-start.20 = (f32[128,2048]{1,0:T(8,128)S(1)}, f32[128,2048]{1,0:T(8,128)S(1)}, u32[]{:S(2)}, u32[]{:S(2)}) collective-permute-start(f32[128,2048]{1,0:T(8,128)S(1)} %get-tuple-element.94), channel_id=1, source_target_pairs={{0,1},{1,0},{2,3},{3,2},{4,5},{5,4},{6,7},{7,6},{8,9},{9,8},{10,11... | collective-permute-start | bytes 3145736 | tf_op jit(solution)/shard_map/ppermute | solution.py:436
  69.9 3.8 %collective-permute-start.21 = (bf16[128,1024]{1,0:T(8,128)(2,1)S(1)}, bf16[128,1024]{1,0:T(8,128)(2,1)S(1)}, u32[]{:S(2)}, u32[]{:S(2)}) collective-permute-start(bf16[128,1024]{1,0:T(8,128)(2,1)S(1)} %get-tuple-element.100), channel_id=1, source_target_pairs={{0,1},{1,0},{2,3},{3,2},{4,5},{5,4},{6,7},{7,6},{8,9},{9,8},{10,11... | collective-permute-start | bytes 786440 | tf_op jit(solution)/shard_map/ppermute | solution.py:436
  70.0 15.6 %collective-permute-start.26 = (bf16[128,1024]{1,0:T(8,128)(2,1)S(1)}, bf16[128,1024]{1,0:T(8,128)(2,1)S(1)}, u32[]{:S(2)}, u32[]{:S(2)}) collective-permute-start(bf16[128,1024]{1,0:T(8,128)(2,1)S(1)} %get-tuple-element.103), channel_id=1, source_target_pairs={{0,2},{1,0},{2,4},{3,1},{4,6},{5,3},{6,8},{7,5},{8,10},{9,7},{10,1... | collective-permute-start | bytes 786440 | tf_op jit(solution)/shard_map/ppermute | solution.py:450
  73.7 2.6 %collective-permute-start.23 = (bf16[64,1024]{1,0:T(8,128)(2,1)S(1)}, bf16[64,1024]{1,0:T(8,128)(2,1)S(1)}, u32[]{:S(2)}, u32[]{:S(2)}) collective-permute-start(bf16[64,1024]{1,0:T(8,128)(2,1)S(1)} %get-tuple-element.101), channel_id=1, source_target_pairs={{0,1},{1,0},{2,3},{3,2},{4,5},{5,4},{6,7},{7,6},{8,9},{9,8},{10,11... | collective-permute-start | bytes 393224 | tf_op jit(solution)/shard_map/ppermute | solution.py:436
  73.7 13.4 %collective-permute-start.22 = (bf16[128,1024]{1,0:T(8,128)(2,1)S(1)}, bf16[128,1024]{1,0:T(8,128)(2,1)S(1)}, u32[]{:S(2)}, u32[]{:S(2)}) collective-permute-start(bf16[128,1024]{1,0:T(8,128)(2,1)S(1)} %collective-permute-done.21), channel_id=1, source_target_pairs={{0,2},{1,0},{2,4},{3,1},{4,6},{5,3},{6,8},{7,5},{8,10},{9,7},{10,1... | collective-permute-start | bytes 786440 | tf_op jit(solution)/shard_map/ppermute | solution.py:450
  76.3 9.2 %collective-permute-start.27 = (bf16[64,1024]{1,0:T(8,128)(2,1)S(1)}, bf16[64,1024]{1,0:T(8,128)(2,1)S(1)}, u32[]{:S(2)}, u32[]{:S(2)}) collective-permute-start(bf16[64,1024]{1,0:T(8,128)(2,1)S(1)} %get-tuple-element.104), channel_id=1, source_target_pairs={{0,1},{1,3},{2,0},{3,5},{4,2},{5,7},{6,4},{7,9},{8,6},{9,11},{10,8... | collective-permute-start | bytes 393224 | tf_op jit(solution)/shard_map/ppermute | solution.py:450
  76.3 10.8 %collective-permute-start.24 = (bf16[64,1024]{1,0:T(8,128)(2,1)S(1)}, bf16[64,1024]{1,0:T(8,128)(2,1)S(1)}, u32[]{:S(2)}, u32[]{:S(2)}) collective-permute-start(bf16[64,1024]{1,0:T(8,128)(2,1)S(1)} %collective-permute-done.23), channel_id=1, source_target_pairs={{0,1},{1,3},{2,0},{3,5},{4,2},{5,7},{6,4},{7,9},{8,6},{9,11},{10,8... | collective-permute-start | bytes 393224 | tf_op jit(solution)/shard_map/ppermute | solution.py:450
  76.4 10.7 %collective-permute-start.25 = (bf16[16,1024]{1,0:T(8,128)(2,1)S(1)}, bf16[16,1024]{1,0:T(8,128)(2,1)S(1)}, u32[]{:S(2)}, u32[]{:S(2)}) collective-permute-start(bf16[16,1024]{1,0:T(8,128)(2,1)S(1)} %get-tuple-element.102), channel_id=1, source_target_pairs={{0,1},{1,0},{2,3},{3,2},{4,5},{5,4},{6,7},{7,6},{8,9},{9,8},{10,11... | collective-permute-start | bytes 98312 | tf_op jit(solution)/shard_map/ppermute | solution.py:436

commit v2 on v0

--- a/solution.py
+++ b/solution.py
@@ -71,7 +71,7 @@
 
 
 def coarse_kernel(
-    where, own, recv, fine_same, fine_cross, half_same, half_cross, same2, cross2, other2, quad3
+    where, own, recv, fine_same, fine_cross, half_same, half_cross, cross2, pair2, quad3
 ):
     even = (where[0] // 2) % 2 == 0
     first = where[0] % 2 == 0
@@ -88,9 +88,8 @@
     above_high = dot(half, half_above).astype(BF16)
     b2 = jnp.concatenate([below_low[0:32], below_high[0:32]], axis=0)
     a2 = jnp.concatenate([above_low[0:32], above_high[0:32]], axis=0)
-    same2[...] = jnp.where(first, b2, a2)
-    cross2[...] = jnp.where(first, a2, b2)
-    other2[...] = jnp.where(even, a2, b2)
+    cross2[...] = jnp.where(even, a2, b2)
+    pair2[...] = jnp.where(even, b2, a2)
     own3 = jnp.concatenate([own_low, own_high], axis=0)
     b3 = jnp.concatenate([below_low[32:48], below_high[32:48]], axis=0)
     a3 = jnp.concatenate([above_low[32:48], above_high[32:48]], axis=0)
@@ -201,7 +200,6 @@
     far,
 ):
     chips = where[1] // 2
-    core = where[0] % 2
     chip = where[0] // 2
     quad = chip // 2
     for n, piece in enumerate((m2, p2, s2, z3, x3, s3)):
@@ -211,8 +209,8 @@
     quads = chips // 2
     rows_bias = row_bias(
         (
-            (64, bias(jnp.where(core == 0, chip >= 2, chip + 2 < chips), 2)),
-            (64, bias(jnp.where(core == 0, chip + 2 < chips, chip >= 2), 2)),
+            (64, bias(jnp.where(chip % 2 == 0, chip >= 2, chip + 2 < chips), 2)),
+            (64, bias(jnp.where(chip % 2 == 0, chip + 2 < chips, chip >= 2), 2)),
             (64, bias((far2 >= 0) & (far2 < chips), 2)),
             (64, F32(3)),
             (64, bias(jnp.where(chip % ROW < ROW // 2, chip >= ROW, chip + ROW < chips), 3)),
@@ -292,7 +290,7 @@
 
 
 def fold_kernel(
-    where, grad_below, grad_above, s3, z3, same2, cross2, other2,
+    where, grad_below, grad_above, s3, z3, cross2, pair2,
     out_same, out_cross, half_same, half_cross, keep3, send3,
 ):
     even = (where[0] // 2) % 2 == 0
@@ -303,18 +301,18 @@
     def fold(base, pieces2, rows, use, fine, half):
         def rows_of(n):
             return jnp.concatenate(
-                [piece[32 * n : 32 * n + 32] for piece in (pieces2, other2)]
+                [pieces2[32 * n : 32 * n + 32]]
                 + [piece[rows + 16 * n : rows + 16 * n + 16] for piece in (z3, s3)],
                 axis=0,
             )
 
         fine_matrix = jnp.concatenate(
-            [spread_matrix(128, 32, 4), weigh(spread_matrix(128, 32, 4), use)]
+            [spread_matrix(128, 32, 4)]
             + [weigh(spread_matrix(128, 16, 8), use)] * 2,
             axis=1,
         )
         half_matrix = jnp.concatenate(
-            [spread_matrix(64, 32, 2), weigh(spread_matrix(64, 32, 2), use)]
+            [spread_matrix(64, 32, 2)]
             + [weigh(spread_matrix(64, 16, 4), use)] * 2,
             axis=1,
         )
@@ -324,8 +322,8 @@
         )
 
     first = where[0] % 2 == 0
-    from2 = jnp.where(first, same2[...], cross2[...])
-    to2 = jnp.where(first, cross2[...], same2[...])
+    from2 = jnp.where(even, pair2[...], cross2[...])
+    to2 = jnp.where(even, cross2[...], pair2[...])
     fine_below, half_below = fold(grad_below, from2, 0, jnp.logical_not(even), 1, 0)
     fine_above, half_above = fold(grad_above, to2, 32, even, 0, 1)
     out_same[...] = jnp.where(first, fine_above, fine_below)
@@ -396,7 +394,8 @@
     near = {
         "fine_same": lambda p, c: (p - 1, 1) if c == 1 else (p + 1, 0),
         "half_same": lambda p, c: (p - 1, 0) if c == 0 else (p + 1, 1),
-        "far2": lambda p, c: (p + 2 if p % 2 == 0 else p - 2, c),
+        "cross": lambda p, c: (p - 1 if p % 2 == 0 else p + 1, c),
+        "pair": lambda p, c: (p ^ 1, c),
         "z3": lambda p, c: (opposite(p), c),
         "x3": lambda p, c: (p - ROW if p % ROW < ROW // 2 else p + ROW, c),
         "s3": lambda p, c: (p + 6 if p // 2 % 2 == 0 else p - 6, c),
@@ -404,7 +403,7 @@
     closing = {
         "fine_same": lambda p, c: (p, 1 - c),
         "half_same": lambda p, c: (p, 1 - c),
-        "far2": lambda p, c: (p ^ 1, c),
+        "cross": lambda p, c: (p, 1 - c),
         "x3": lambda p, c: (p - p % ROW + ROW - 1 - p % ROW, c),
         "s3": lambda p, c: (p ^ 1, c),
     }
@@ -454,14 +453,14 @@
     fine_same = fetch(own_kv, "fine_same")
     recv_kv = swap(other_kv)
     near = (fine_same, fine_cross, half_same, half_cross)
-    same2, cross2, other2, quad3 = call(
-        coarse_kernel, where, (own_kv, recv_kv, *near), [((64, PAIR), BF16)] * 4
+    cross2, pair2, quad3 = call(
+        coarse_kernel, where, (own_kv, recv_kv, *near), [((64, PAIR), BF16)] * 3
     )
     z3 = fetch(quad3, "z3")
     s3 = fetch(quad3, "s3")
-    s2 = fetch(other2, "far2")
-    same2 = fetch(same2, "half_same")
-    cross2 = fetch(cross2, "fine_same")
+    c2 = fetch(cross2, "cross")
+    b2 = fetch(pair2, "pair")
+    f2 = fetch(c2, "pair")
     x3 = fetch(z3, "x3")
     queries, grads, near_kv, weights, dprobs, stats, outputs = call(
         near_kernel,
@@ -477,7 +476,7 @@
             ((4 * HEAD, 2 * BLOCK), F32),
         ],
     )
-    far = (same2, cross2, s2, z3, x3, s3)
+    far = (c2, b2, f2, z3, x3, s3)
     output, scales, dscores, gm2, gp2, gs2, gz3, gx3, gs3 = call(
         main_kernel,
         where,
@@ -491,11 +490,13 @@
         scratch=[pltpu.VMEM((FAR, PAIR), BF16)],
     )
     back_s3 = give(gs3, "s3")
-    gz3, gs2, gp2, scales = lax.optimization_barrier((gz3 + give(gx3, "x3"), gs2, gp2, scales))
+    gz3, shared, scales = lax.optimization_barrier(
+        (gz3 + give(gx3, "x3"), fetch(gs2, "pair"), scales)
+    )
+    gm2 = gm2 + shared
     back_z3 = give(gz3, "z3")
-    back_s2 = give(gs2, "far2")
-    back_m2 = give(gm2, "half_same")
-    back_p2 = give(gp2, "fine_same")
+    back_c2 = give(gm2, "cross")
+    back_b2 = give(gp2, "pair")
     keep, send, grad_below, grad_above = call(
         rest_kernel,
         where,
@@ -511,7 +512,7 @@
     fine_same, fine_cross, half_same, half_cross, keep3, send3 = call(
         fold_kernel,
         where,
-        (grad_below, grad_above, back_s3, back_z3, back_m2, back_p2, back_s2),
+        (grad_below, grad_above, back_s3, back_z3, back_c2, back_b2),
         [((BLOCK, PAIR), BF16)] * 2
         + [((BLOCK // 2, PAIR), BF16)] * 2
         + [((16, PAIR), BF16)] * 2,

time: 89.1 us -> 90 us (1.010); the launches traced: 88 us -> 89.8 us
  waiting for transfers between devices: 32.4 us -> 34.4 us
    ppermute x9 -> x10, waiting for transfers between devices: 19 us -> 25.7 us  [fetch(): return lax.ppermute(x, AXES, pairs(name))]
    ppermute x10 -> x9, waiting for transfers between devices: 13.4 us -> 8.69 us  [give(): return lax.ppermute(x, AXES, [(b, a) for a, b in pairs(name)])]
    ppermute x9, starting transfers between devices: 8.15 us -> 11.1 us  [swap(): return lax.ppermute(x, AXES, [(i, i ^ 1) for i in range(devices)])]
    ppermute x9 -> x10, starting transfers between devices: 13.4 us -> 11.4 us  [fetch(): return lax.ppermute(x, AXES, pairs(name))]
    ppermute x10 -> x9, starting transfers between devices: 14.9 us -> 13.7 us  [give(): return lax.ppermute(x, AXES, [(b, a) for a, b in pairs(name)])]
  transfers between devices with their start and end apart: 28 -> 28, of which waited for: 12 -> 10; matrix products, arithmetic and copies ran while one was open for 0% -> 0% of each run, Pallas kernels for 9% -> 9%
where the time goes in v2:
time: 90 us; the launch traced here: 89.8 us
  starting transfers between devices  36.2 us (40%)
  waiting for transfers between devices  34.4 us (38%)
  Pallas kernels  14.3 us (16%)
  local copies, waits for them, and re-layouts  3.79 us (4%)
  between operations  0.99 us (1%)
    ppermute x10, waiting for transfers between devices, fetch(): return lax.ppermute(x, AXES, pairs(name))  25.7 us
    pallas_call x8, Pallas kernels, call(): pl.pallas_call(kernel, out_shape=[jax.ShapeDtypeStruct(shape, dtype) for...  14.3 us
    ppermute x9, starting transfers between devices, give(): return lax.ppermute(x, AXES, [(b, a) for a, b in pairs(name)])  13.7 us
    ppermute x10, starting transfers between devices, fetch(): return lax.ppermute(x, AXES, pairs(name))  11.4 us
    ppermute x9, starting transfers between devices, swap(): return lax.ppermute(x, AXES, [(i, i ^ 1) for i in range(devices)])  11.1 us
    ppermute x9, waiting for transfers between devices, give(): return lax.ppermute(x, AXES, [(b, a) for a, b in pairs(name)])  8.69 us
    unnamed x8, local copies, waits for them, and re-layouts  3.79 us
  transfers between devices with their start and end apart: 28, of which 10 were waited for; matrix products, arithmetic and copies ran while one was open for 0% of the time, Pallas kernels for 9%

profile of v2, /device:TPU:25, one launch (start us, length us, event | category | flops | bytes accessed | tf_op | source)
XLA Modules:
  0.0 89.8 jit_solution(5149894244359514958)
XLA Ops:
  0.6 0.8 collective-permute-start
  1.4 0.1 collective-permute-start.1
  1.5 0.1 pad_add_fusion.where
  1.6 0.9 %copy-done = bf16[128,1024]{1,0:T(8,128)(2,1)S(1)} copy-done((bf16[128,1024]{1,0:T(8,128)(2,1)S(1)}, bf16[128,1024]{1,0:T(8,128)(2,1)}, u32[]{:S(2)}) %copy-start) | copy-done | bytes 262168
  2.5 0.9 %copy-done.1 = bf16[128,1024]{1,0:T(8,128)(2,1)S(1)} copy-done((bf16[128,1024]{1,0:T(8,128)(2,1)S(1)}, bf16[128,1024]{1,0:T(8,128)(2,1)}, u32[]{:S(2)}) %copy-start.1) | copy-done | bytes 262168
  3.5 0.8 shard_map.75
  4.3 0.0 collective-permute-done.recv_q
  4.3 0.0 collective-permute-done.1.recv_g
  4.3 8.0 %collective-permute-start.6 = (bf16[128,1024]{1,0:T(8,128)(2,1)S(1)}, bf16[128,1024]{1,0:T(8,128)(2,1)S(1)}, u32[]{:S(2)}, u32[]{:S(2)}) collective-permute-start(bf16[128,1024]{1,0:T(8,128)(2,1)S(1)} %get-tuple-element.60), channel_id=1, source_target_pairs={{1,0},{3,1},{0,2},{5,3},{2,4},{7,5},{4,6},{9,7},{6,8},{11,9},{8,10... | collective-permute-start | bytes 786440 | tf_op jit(solution)/shard_map/ppermute | solution.py:437
  12.3 0.0 collective-permute-start.4
  12.3 0.8 collective-permute-start.2
  13.1 0.0 collective-permute-start.3
  13.1 4.4 %collective-permute-done.6.half_same = bf16[128,1024]{1,0:T(8,128)(2,1)S(1)} collective-permute-done((bf16[128,1024]{1,0:T(8,128)(2,1)S(1)}, bf16[128,1024]{1,0:T(8,128)(2,1)S(1)}, u32[]{:S(2)}, u32[]{:S(2)}) %collective-permute-start.6) | collective-permute-done | bytes 262176 | tf_op jit(solution)/shard_map/ppermute | solution.py:437
  17.5 1.3 %collective-permute-start.7 = (bf16[128,1024]{1,0:T(8,128)(2,1)S(1)}, bf16[128,1024]{1,0:T(8,128)(2,1)S(1)}, u32[]{:S(2)}, u32[]{:S(2)}) collective-permute-start(bf16[128,1024]{1,0:T(8,128)(2,1)S(1)} %collective-permute-done.6.half_same), channel_id=1, source_target_pairs={{0,1},{1,0},{2,3},{3,2},{4,5},{5,4},{6,7},{7,6},{8,9},{9,8},{10,11... | collective-permute-start | bytes 786440 | tf_op jit(solution)/shard_map/ppermute | solution.py:426
  18.8 3.0 %collective-permute-done.4 = bf16[128,1024]{1,0:T(8,128)(2,1)S(1)} collective-permute-done((bf16[128,1024]{1,0:T(8,128)(2,1)S(1)}, bf16[128,1024]{1,0:T(8,128)(2,1)S(1)}, u32[]{:S(2)}, u32[]{:S(2)}) %collective-permute-start.4) | collective-permute-done | bytes 262176 | tf_op jit(solution)/shard_map/ppermute | solution.py:437
  21.8 0.0 collective-permute-start.5
  21.8 0.0 collective-permute-done.2.recv_kv.recv
  21.8 2.8 %collective-permute-done.3.fine_same = bf16[128,1024]{1,0:T(8,128)(2,1)S(1)} collective-permute-done((bf16[128,1024]{1,0:T(8,128)(2,1)S(1)}, bf16[128,1024]{1,0:T(8,128)(2,1)S(1)}, u32[]{:S(2)}, u32[]{:S(2)}) %collective-permute-start.3) | collective-permute-done | bytes 262176 | tf_op jit(solution)/shard_map/ppermute | solution.py:437
  24.6 0.0 collective-permute-done.7.half_cross
  24.6 0.0 collective-permute-done.5.fine_cross
  24.6 0.9 shard_map.77
  25.5 1.9 %collective-permute-start.8 = (bf16[64,1024]{1,0:T(8,128)(2,1)S(1)}, bf16[64,1024]{1,0:T(8,128)(2,1)S(1)}, u32[]{:S(2)}, u32[]{:S(2)}) collective-permute-start(bf16[64,1024]{1,0:T(8,128)(2,1)S(1)} %get-tuple-element.68), channel_id=1, source_target_pairs={{1,0},{0,1},{4,2},{5,3},{2,4},{3,5},{8,6},{9,7},{6,8},{7,9},{12,10... | collective-permute-start | bytes 393224 | tf_op jit(solution)/shard_map/ppermute | solution.py:437
  27.4 0.0 collective-permute-start.11
  27.4 0.0 collective-permute-start.13
  27.4 0.0 collective-permute-start.9
  27.4 12.2 %collective-permute-done.8.m2 = bf16[64,1024]{1,0:T(8,128)(2,1)S(1)} collective-permute-done((bf16[64,1024]{1,0:T(8,128)(2,1)S(1)}, bf16[64,1024]{1,0:T(8,128)(2,1)S(1)}, u32[]{:S(2)}, u32[]{:S(2)}) %collective-permute-start.8) | collective-permute-done | bytes 131104 | tf_op jit(solution)/shard_map/ppermute | solution.py:437
  39.6 0.0 collective-permute-start.10
  39.6 0.0 collective-permute-done.11.z3
  39.6 0.0 collective-permute-start.12
  39.7 0.0 copy-start.2
  39.7 0.9 %copy-done.2 = bf16[128,1024]{1,0:T(8,128)(2,1)S(1)} copy-done((bf16[128,1024]{1,0:T(8,128)(2,1)S(1)}, bf16[128,1024]{1,0:T(8,128)(2,1)}, u32[]{:S(2)}) %copy-start.2) | copy-done | bytes 262168
  40.6 0.9 %copy-done.3 = bf16[128,1024]{1,0:T(8,128)(2,1)S(1)} copy-done((bf16[128,1024]{1,0:T(8,128)(2,1)S(1)}, bf16[128,1024]{1,0:T(8,128)(2,1)}, u32[]{:S(2)}) %copy-start.3) | copy-done | bytes 262168
  41.6 2.8 %shard_map.76 = (bf16[256,512]{1,0:T(8,128)(2,1)S(1)}, bf16[256,512]{1,0:T(8,128)(2,1)S(1)}, bf16[768,1024]{1,0:T(8,128)(2,1)S(1)}, f32[2304,256]{1,0:T(8,128)S(...) custom-call(s32[2]{0:T(128)S(1)} %pad_add_fusion.where, ...), custom_call_target="tpu_custom_call" | custom-call | tf_op jit(solution)/shard_map/pallas_call | solution.py:378
  44.4 0.0 collective-permute-done.9.p2
  44.4 1.2 %collective-permute-done.12.x3 = bf16[64,1024]{1,0:T(8,128)(2,1)S(1)} collective-permute-done((bf16[64,1024]{1,0:T(8,128)(2,1)S(1)}, bf16[64,1024]{1,0:T(8,128)(2,1)S(1)}, u32[]{:S(2)}, u32[]{:S(2)}) %collective-permute-start.12) | collective-permute-done | bytes 131104 | tf_op jit(solution)/shard_map/ppermute | solution.py:437
  45.6 2.3 %shard_map.78 = (f32[256,512]{1,0:T(8,128)S(1)}, f32[8,256]{1,0:T(8,128)S(1)}, bf16[1536,256]{1,0:T(8,128)(2,1)S(1)}, bf16[64,1024]{1,0:T(8,128)(2,1)S(1)}, bf16...) custom-call(s32[2]{0:T(128)S(1)} %pad_add_fusion.where, ...), custom_call_target="tpu_custom_call" | custom-call | tf_op jit(solution)/shard_map/pallas_call | solution.py:378
  47.9 2.5 %collective-permute-start.14 = (bf16[64,1024]{1,0:T(8,128)(2,1)S(1)}, bf16[64,1024]{1,0:T(8,128)(2,1)S(1)}, u32[]{:S(2)}, u32[]{:S(2)}) collective-permute-start(bf16[64,1024]{1,0:T(8,128)(2,1)S(1)} %get-tuple-element.72), channel_id=1, source_target_pairs={{0,14},{1,15},{2,12},{3,13},{4,10},{5,11},{6,8},{7,9},{8,24},{9,25... | collective-permute-start | bytes 393224 | tf_op jit(solution)/shard_map/ppermute | solution.py:440
  50.4 1.5 %collective-permute-start.15 = (bf16[64,1024]{1,0:T(8,128)(2,1)S(1)}, bf16[64,1024]{1,0:T(8,128)(2,1)S(1)}, u32[]{:S(2)}, u32[]{:S(2)}) collective-permute-start(bf16[64,1024]{1,0:T(8,128)(2,1)S(1)} %get-tuple-element.73), channel_id=1, source_target_pairs={{2,0},{3,1},{0,2},{1,3},{6,4},{7,5},{4,6},{5,7},{10,8},{11,9},{8,1... | collective-permute-start | bytes 393224 | tf_op jit(solution)/shard_map/ppermute | solution.py:437
  51.9 0.0 collective-permute-start.19
  51.9 0.4 collective-permute-done.14
  52.4 2.1 %collective-permute-done.15 = bf16[64,1024]{1,0:T(8,128)(2,1)S(1)} collective-permute-done((bf16[64,1024]{1,0:T(8,128)(2,1)S(1)}, bf16[64,1024]{1,0:T(8,128)(2,1)S(1)}, u32[]{:S(2)}, u32[]{:S(2)}) %collective-permute-start.15) | collective-permute-done | bytes 131104 | tf_op jit(solution)/shard_map/ppermute | solution.py:437
  54.5 1.4 %collective-permute-start.17 = (bf16[64,1024]{1,0:T(8,128)(2,1)S(1)}, bf16[64,1024]{1,0:T(8,128)(2,1)S(1)}, u32[]{:S(2)}, u32[]{:S(2)}) collective-permute-start(bf16[64,1024]{1,0:T(8,128)(2,1)S(1)} %add.10), channel_id=1, source_target_pairs={{0,10},{1,11},{2,8},{3,9},{4,14},{5,15},{6,12},{7,13},{8,2},{9,3},... | collective-permute-start | bytes 393224 | tf_op jit(solution)/shard_map/ppermute | solution.py:440
  56.0 4.4 %collective-permute-start.18 = (bf16[64,1024]{1,0:T(8,128)(2,1)S(1)}, bf16[64,1024]{1,0:T(8,128)(2,1)S(1)}, u32[]{:S(2)}, u32[]{:S(2)}) collective-permute-start(bf16[64,1024]{1,0:T(8,128)(2,1)S(1)} %add.11), channel_id=1, source_target_pairs={{0,1},{1,0},{2,4},{3,5},{4,2},{5,3},{6,8},{7,9},{8,6},{9,7},{10,12... | collective-permute-start | bytes 393224 | tf_op jit(solution)/shard_map/ppermute | solution.py:440
  60.3 3.2 %shard_map.79 = (f32[128,2048]{1,0:T(8,128)S(1)}, f32[128,2048]{1,0:T(8,128)S(1)}, bf16[192,1024]{1,0:T(8,128)(2,1)S(1)}, bf16[192,1024]{1,0:T(8,128)(2,1)S(1)}) custom-call(s32[2]{0:T(128)S(1)} %pad_add_fusion.where, bf16[256,512]{1,0:T(8,128)(2,1)S(1)} %get-tuple-element.61.queries, bf16[256,512]{1,0:T(8,128)(2,1)S(1)} %get-tuple-element.62.grads, ...), custom_call_target="tpu_custom_call" | custom-call | tf_op jit(solution)/shard_map/pallas_call | solution.py:378
  63.5 0.0 collective-permute-done.16.s3
  63.5 0.0 collective-permute-done.17.z3
  63.5 3.0 %collective-permute-done.18.cross2 = bf16[64,1024]{1,0:T(8,128)(2,1)S(1)} collective-permute-done((bf16[64,1024]{1,0:T(8,128)(2,1)S(1)}, bf16[64,1024]{1,0:T(8,128)(2,1)S(1)}, u32[]{:S(2)}, u32[]{:S(2)}) %collective-permute-start.18) | collective-permute-done | bytes 131104 | tf_op jit(solution)/shard_map/ppermute | solution.py:440
  66.5 1.0 %shard_map.80 = (bf16[128,1024]{1,0:T(8,128)(2,1)S(1)}, bf16[128,1024]{1,0:T(8,128)(2,1)S(1)}, bf16[64,1024]{1,0:T(8,128)(2,1)S(1)}, bf16[64,1024]{1,0:T(8,128)(...) custom-call(s32[2]{0:T(128)S(1)} %pad_add_fusion.where, ...), custom_call_target="tpu_custom_call" | custom-call | tf_op jit(solution)/shard_map/pallas_call | solution.py:378
  67.5 4.1 %collective-permute-start.20 = (f32[128,2048]{1,0:T(8,128)S(1)}, f32[128,2048]{1,0:T(8,128)S(1)}, u32[]{:S(2)}, u32[]{:S(2)}) collective-permute-start(f32[128,2048]{1,0:T(8,128)S(1)} %get-tuple-element.88), channel_id=1, source_target_pairs={{0,1},{1,0},{2,3},{3,2},{4,5},{5,4},{6,7},{7,6},{8,9},{9,8},{10,11... | collective-permute-start | bytes 3145736 | tf_op jit(solution)/shard_map/ppermute | solution.py:426
  71.7 0.1 collective-permute-start.23
  71.8 0.4 collective-permute-start.26
  72.2 3.2 %collective-permute-start.22 = (bf16[128,1024]{1,0:T(8,128)(2,1)S(1)}, bf16[128,1024]{1,0:T(8,128)(2,1)S(1)}, u32[]{:S(2)}, u32[]{:S(2)}) collective-permute-start(bf16[128,1024]{1,0:T(8,128)(2,1)S(1)} %get-tuple-element.96), channel_id=1, source_target_pairs={{0,2},{1,0},{2,4},{3,1},{4,6},{5,3},{6,8},{7,5},{8,10},{9,7},{10,1... | collective-permute-start | bytes 786440 | tf_op jit(solution)/shard_map/ppermute | solution.py:440
  75.4 0.0 collective-permute-done.23
  75.4 2.1 %collective-permute-start.24 = (bf16[128,1024]{1,0:T(8,128)(2,1)S(1)}, bf16[128,1024]{1,0:T(8,128)(2,1)S(1)}, u32[]{:S(2)}, u32[]{:S(2)}) collective-permute-start(bf16[128,1024]{1,0:T(8,128)(2,1)S(1)} %collective-permute-done.23), channel_id=1, source_target_pairs={{0,2},{1,0},{2,4},{3,1},{4,6},{5,3},{6,8},{7,5},{8,10},{9,7},{10,1... | collective-permute-start | bytes 786440 | tf_op jit(solution)/shard_map/ppermute | solution.py:440
  77.6 0.0 collective-permute-done.26
  77.6 0.0 collective-permute-start.27
  77.6 3.5 %collective-permute-start.21 = (bf16[16,1024]{1,0:T(8,128)(2,1)S(1)}, bf16[16,1024]{1,0:T(8,128)(2,1)S(1)}, u32[]{:S(2)}, u32[]{:S(2)}) collective-permute-start(bf16[16,1024]{1,0:T(8,128)(2,1)S(1)} %get-tuple-element.95), channel_id=1, source_target_pairs={{0,1},{1,0},{2,3},{3,2},{4,5},{5,4},{6,7},{7,6},{8,9},{9,8},{10,11... | collective-permute-start | bytes 98312 | tf_op jit(solution)/shard_map/ppermute | solution.py:426
  81.1 1.5 %shard_map.81 = (bf16[128,1024]{1,0:T(8,128)(2,1)}, f32[128,1024]{1,0:T(8,128)}) custom-call(s32[2]{0:T(128)S(1)} %pad_add_fusion.where, f32[128,2048]{1,0:T(8,128)S(1)} %get-tuple-element.78.out_keep.keep, f32[128,2048]{1,0:T(8,128)S(1)} %collective-permute-done.20.out_recv.recv), custom_call_target="tpu_custom_call" | custom-call | tf_op jit(solution)/shard_map/pallas_call | solution.py:378
  82.5 0.0 collective-permute-done.21.recv3
  82.5 3.9 %collective-permute-done.25.half_same = bf16[64,1024]{1,0:T(8,128)(2,1)S(1)} collective-permute-done((bf16[64,1024]{1,0:T(8,128)(2,1)S(1)}, bf16[64,1024]{1,0:T(8,128)(2,1)S(1)}, u32[]{:S(2)}, u32[]{:S(2)}) %collective-permute-start.25) | collective-permute-done | bytes 131104 | tf_op jit(solution)/shard_map/ppermute | solution.py:440
  86.4 1.4 %collective-permute-done.27.half_cross = bf16[64,1024]{1,0:T(8,128)(2,1)S(1)} collective-permute-done((bf16[64,1024]{1,0:T(8,128)(2,1)S(1)}, bf16[64,1024]{1,0:T(8,128)(2,1)S(1)}, u32[]{:S(2)}, u32[]{:S(2)}) %collective-permute-start.27) | collective-permute-done | bytes 131104 | tf_op jit(solution)/shard_map/ppermute | solution.py:440
  87.8 0.0 collective-permute-done.22.fine_same
  87.8 0.0 collective-permute-done.24.fine_cross
  87.8 1.8 %shard_map.82 = (f32[128,1024]{1,0:T(8,128)}, f32[128,1024]{1,0:T(8,128)}) custom-call(s32[2]{0:T(128)S(1)} %pad_add_fusion.where, f32[128,2048]{1,0:T(8,128)S(1)} %get-tuple-element.78.out_keep.keep, f32[128,2048]{1,0:T(8,128)S(1)} %collective-permute-done.20.out_recv.recv, bf16[16,1024]{1,0:T(8,128)(2,1)S(1)} %get-tuple-element.94.keep3, ...), custom_call_target="tpu_custom_call" | custom-call | tf_op jit(solution)/shard_map/pallas_call | solution.py:378
  (11 shorter events, 0.1 us)
Async XLA Ops:
  0.6 3.6 %collective-permute-start = (bf16[128,1024]{1,0:T(8,128)(2,1)}, bf16[128,1024]{1,0:T(8,128)(2,1)S(1)}, u32[]{:S(2)}, u32[]{:S(2)}) collective-permute-start(bf16[128,1024]{1,0:T(8,128)(2,1)} %q.1), channel_id=1, source_target_pairs={{0,1},{1,0},{2,3},{3,2},{4,5},{5,4},{6,7},{7,6},{8,9},{9,8},{10,11... | collective-permute-start | bytes 786440 | tf_op jit(solution)/shard_map/ppermute | solution.py:426
  1.4 2.9 %collective-permute-start.1 = (bf16[128,1024]{1,0:T(8,128)(2,1)}, bf16[128,1024]{1,0:T(8,128)(2,1)S(1)}, u32[]{:S(2)}, u32[]{:S(2)}) collective-permute-start(bf16[128,1024]{1,0:T(8,128)(2,1)} %g.1), channel_id=1, source_target_pairs={{0,1},{1,0},{2,3},{3,2},{4,5},{5,4},{6,7},{7,6},{8,9},{9,8},{10,11... | collective-permute-start | bytes 786440 | tf_op jit(solution)/shard_map/ppermute | solution.py:426
  1.6 0.9 %copy-start = (bf16[128,1024]{1,0:T(8,128)(2,1)S(1)}, bf16[128,1024]{1,0:T(8,128)(2,1)}, u32[]{:S(2)}) copy-start(bf16[128,1024]{1,0:T(8,128)(2,1)} %k.1) | copy-start | bytes 786436
  2.5 0.9 %copy-start.1 = (bf16[128,1024]{1,0:T(8,128)(2,1)S(1)}, bf16[128,1024]{1,0:T(8,128)(2,1)}, u32[]{:S(2)}) copy-start(bf16[128,1024]{1,0:T(8,128)(2,1)} %v.1) | copy-start | bytes 786436
  4.3 13.2 %collective-permute-start.6 = (bf16[128,1024]{1,0:T(8,128)(2,1)S(1)}, bf16[128,1024]{1,0:T(8,128)(2,1)S(1)}, u32[]{:S(2)}, u32[]{:S(2)}) collective-permute-start(bf16[128,1024]{1,0:T(8,128)(2,1)S(1)} %get-tuple-element.60), channel_id=1, source_target_pairs={{1,0},{3,1},{0,2},{5,3},{2,4},{7,5},{4,6},{9,7},{6,8},{11,9},{8,10... | collective-permute-start | bytes 786440 | tf_op jit(solution)/shard_map/ppermute | solution.py:437
  12.3 9.4 %collective-permute-start.4 = (bf16[128,1024]{1,0:T(8,128)(2,1)S(1)}, bf16[128,1024]{1,0:T(8,128)(2,1)S(1)}, u32[]{:S(2)}, u32[]{:S(2)}) collective-permute-start(bf16[128,1024]{1,0:T(8,128)(2,1)S(1)} %get-tuple-element.59), channel_id=1, source_target_pairs={{2,0},{0,1},{4,2},{1,3},{6,4},{3,5},{8,6},{5,7},{10,8},{7,9},{12,1... | collective-permute-start | bytes 786440 | tf_op jit(solution)/shard_map/ppermute | solution.py:437
  12.3 9.4 %collective-permute-start.2 = (bf16[128,1024]{1,0:T(8,128)(2,1)S(1)}, bf16[128,1024]{1,0:T(8,128)(2,1)S(1)}, u32[]{:S(2)}, u32[]{:S(2)}) collective-permute-start(bf16[128,1024]{1,0:T(8,128)(2,1)S(1)} %get-tuple-element.59), channel_id=1, source_target_pairs={{0,1},{1,0},{2,3},{3,2},{4,5},{5,4},{6,7},{7,6},{8,9},{9,8},{10,11... | collective-permute-start | bytes 786440 | tf_op jit(solution)/shard_map/ppermute | solution.py:426
  13.1 11.5 %collective-permute-start.3 = (bf16[128,1024]{1,0:T(8,128)(2,1)S(1)}, bf16[128,1024]{1,0:T(8,128)(2,1)S(1)}, u32[]{:S(2)}, u32[]{:S(2)}) collective-permute-start(bf16[128,1024]{1,0:T(8,128)(2,1)S(1)} %get-tuple-element.58.own_kv.own), channel_id=1, source_target_pairs={{2,0},{0,1},{4,2},{1,3},{6,4},{3,5},{8,6},{5,7},{10,8},{7,9},{12,1... | collective-permute-start | bytes 786440 | tf_op jit(solution)/shard_map/ppermute | solution.py:437
  17.5 7.1 %collective-permute-start.7 = (bf16[128,1024]{1,0:T(8,128)(2,1)S(1)}, bf16[128,1024]{1,0:T(8,128)(2,1)S(1)}, u32[]{:S(2)}, u32[]{:S(2)}) collective-permute-start(bf16[128,1024]{1,0:T(8,128)(2,1)S(1)} %collective-permute-done.6.half_same), channel_id=1, source_target_pairs={{0,1},{1,0},{2,3},{3,2},{4,5},{5,4},{6,7},{7,6},{8,9},{9,8},{10,11... | collective-permute-start | bytes 786440 | tf_op jit(solution)/shard_map/ppermute | solution.py:426
  21.8 2.8 %collective-permute-start.5 = (bf16[128,1024]{1,0:T(8,128)(2,1)S(1)}, bf16[128,1024]{1,0:T(8,128)(2,1)S(1)}, u32[]{:S(2)}, u32[]{:S(2)}) collective-permute-start(bf16[128,1024]{1,0:T(8,128)(2,1)S(1)} %collective-permute-done.4), channel_id=1, source_target_pairs={{0,1},{1,0},{2,3},{3,2},{4,5},{5,4},{6,7},{7,6},{8,9},{9,8},{10,11... | collective-permute-start | bytes 786440 | tf_op jit(solution)/shard_map/ppermute | solution.py:426
  25.5 14.2 %collective-permute-start.8 = (bf16[64,1024]{1,0:T(8,128)(2,1)S(1)}, bf16[64,1024]{1,0:T(8,128)(2,1)S(1)}, u32[]{:S(2)}, u32[]{:S(2)}) collective-permute-start(bf16[64,1024]{1,0:T(8,128)(2,1)S(1)} %get-tuple-element.68), channel_id=1, source_target_pairs={{1,0},{0,1},{4,2},{5,3},{2,4},{3,5},{8,6},{9,7},{6,8},{7,9},{12,10... | collective-permute-start | bytes 393224 | tf_op jit(solution)/shard_map/ppermute | solution.py:437
  27.4 12.2 %collective-permute-start.11 = (bf16[64,1024]{1,0:T(8,128)(2,1)S(1)}, bf16[64,1024]{1,0:T(8,128)(2,1)S(1)}, u32[]{:S(2)}, u32[]{:S(2)}) collective-permute-start(bf16[64,1024]{1,0:T(8,128)(2,1)S(1)} %get-tuple-element.70), channel_id=1, source_target_pairs={{10,0},{11,1},{8,2},{9,3},{14,4},{15,5},{12,6},{13,7},{2,8},{3,9},... | collective-permute-start | bytes 393224 | tf_op jit(solution)/shard_map/ppermute | solution.py:437
  27.4 17.0 %collective-permute-start.13 = (bf16[64,1024]{1,0:T(8,128)(2,1)S(1)}, bf16[64,1024]{1,0:T(8,128)(2,1)S(1)}, u32[]{:S(2)}, u32[]{:S(2)}) collective-permute-start(bf16[64,1024]{1,0:T(8,128)(2,1)S(1)} %get-tuple-element.70), channel_id=1, source_target_pairs={{12,0},{13,1},{14,2},{15,3},{6,4},{7,5},{4,6},{5,7},{20,8},{21,9},... | collective-permute-start | bytes 393224 | tf_op jit(solution)/shard_map/ppermute | solution.py:437
  27.4 17.0 %collective-permute-start.9 = (bf16[64,1024]{1,0:T(8,128)(2,1)S(1)}, bf16[64,1024]{1,0:T(8,128)(2,1)S(1)}, u32[]{:S(2)}, u32[]{:S(2)}) collective-permute-start(bf16[64,1024]{1,0:T(8,128)(2,1)S(1)} %get-tuple-element.69), channel_id=1, source_target_pairs={{2,0},{3,1},{0,2},{1,3},{6,4},{7,5},{4,6},{5,7},{10,8},{11,9},{8,1... | collective-permute-start | bytes 393224 | tf_op jit(solution)/shard_map/ppermute | solution.py:437
  39.6 4.8 %collective-permute-start.10 = (bf16[64,1024]{1,0:T(8,128)(2,1)S(1)}, bf16[64,1024]{1,0:T(8,128)(2,1)S(1)}, u32[]{:S(2)}, u32[]{:S(2)}) collective-permute-start(bf16[64,1024]{1,0:T(8,128)(2,1)S(1)} %collective-permute-done.8.m2), channel_id=1, source_target_pairs={{2,0},{3,1},{0,2},{1,3},{6,4},{7,5},{4,6},{5,7},{10,8},{11,9},{8,1... | collective-permute-start | bytes 393224 | tf_op jit(solution)/shard_map/ppermute | solution.py:437
  39.6 5.9 %collective-permute-start.12 = (bf16[64,1024]{1,0:T(8,128)(2,1)S(1)}, bf16[64,1024]{1,0:T(8,128)(2,1)S(1)}, u32[]{:S(2)}, u32[]{:S(2)}) collective-permute-start(bf16[64,1024]{1,0:T(8,128)(2,1)S(1)} %collective-permute-done.11.z3), channel_id=1, source_target_pairs={{14,0},{15,1},{12,2},{13,3},{10,4},{11,5},{8,6},{9,7},{24,8},{25,9... | collective-permute-start | bytes 393224 | tf_op jit(solution)/shard_map/ppermute | solution.py:437
  39.7 1.0 %copy-start.2 = (bf16[128,1024]{1,0:T(8,128)(2,1)S(1)}, bf16[128,1024]{1,0:T(8,128)(2,1)}, u32[]{:S(2)}) copy-start(bf16[128,1024]{1,0:T(8,128)(2,1)} %q.1) | copy-start | bytes 786436
  40.6 0.9 %copy-start.3 = (bf16[128,1024]{1,0:T(8,128)(2,1)S(1)}, bf16[128,1024]{1,0:T(8,128)(2,1)}, u32[]{:S(2)}) copy-start(bf16[128,1024]{1,0:T(8,128)(2,1)} %g.1) | copy-start | bytes 786436
  47.9 4.5 %collective-permute-start.14 = (bf16[64,1024]{1,0:T(8,128)(2,1)S(1)}, bf16[64,1024]{1,0:T(8,128)(2,1)S(1)}, u32[]{:S(2)}, u32[]{:S(2)}) collective-permute-start(bf16[64,1024]{1,0:T(8,128)(2,1)S(1)} %get-tuple-element.72), channel_id=1, source_target_pairs={{0,14},{1,15},{2,12},{3,13},{4,10},{5,11},{6,8},{7,9},{8,24},{9,25... | collective-permute-start | bytes 393224 | tf_op jit(solution)/shard_map/ppermute | solution.py:440
  50.4 4.1 %collective-permute-start.15 = (bf16[64,1024]{1,0:T(8,128)(2,1)S(1)}, bf16[64,1024]{1,0:T(8,128)(2,1)S(1)}, u32[]{:S(2)}, u32[]{:S(2)}) collective-permute-start(bf16[64,1024]{1,0:T(8,128)(2,1)S(1)} %get-tuple-element.73), channel_id=1, source_target_pairs={{2,0},{3,1},{0,2},{1,3},{6,4},{7,5},{4,6},{5,7},{10,8},{11,9},{8,1... | collective-permute-start | bytes 393224 | tf_op jit(solution)/shard_map/ppermute | solution.py:437
  51.9 11.6 %collective-permute-start.16 = (bf16[64,1024]{1,0:T(8,128)(2,1)S(1)}, bf16[64,1024]{1,0:T(8,128)(2,1)S(1)}, u32[]{:S(2)}, u32[]{:S(2)}) collective-permute-start(bf16[64,1024]{1,0:T(8,128)(2,1)S(1)} %get-tuple-element.82), channel_id=1, source_target_pairs={{0,12},{1,13},{2,14},{3,15},{4,6},{5,7},{6,4},{7,5},{8,20},{9,21},... | collective-permute-start | bytes 393224 | tf_op jit(solution)/shard_map/ppermute | solution.py:440
  51.9 11.7 %collective-permute-start.19 = (bf16[64,1024]{1,0:T(8,128)(2,1)S(1)}, bf16[64,1024]{1,0:T(8,128)(2,1)S(1)}, u32[]{:S(2)}, u32[]{:S(2)}) collective-permute-start(bf16[64,1024]{1,0:T(8,128)(2,1)S(1)} %get-tuple-element.86), channel_id=1, source_target_pairs={{0,2},{1,3},{2,0},{3,1},{4,6},{5,7},{6,4},{7,5},{8,10},{9,11},{10,... | collective-permute-start | bytes 393224 | tf_op jit(solution)/shard_map/ppermute | solution.py:440
  54.5 9.0 %collective-permute-start.17 = (bf16[64,1024]{1,0:T(8,128)(2,1)S(1)}, bf16[64,1024]{1,0:T(8,128)(2,1)S(1)}, u32[]{:S(2)}, u32[]{:S(2)}) collective-permute-start(bf16[64,1024]{1,0:T(8,128)(2,1)S(1)} %add.10), channel_id=1, source_target_pairs={{0,10},{1,11},{2,8},{3,9},{4,14},{5,15},{6,12},{7,13},{8,2},{9,3},... | collective-permute-start | bytes 393224 | tf_op jit(solution)/shard_map/ppermute | solution.py:440
  56.0 10.6 %collective-permute-start.18 = (bf16[64,1024]{1,0:T(8,128)(2,1)S(1)}, bf16[64,1024]{1,0:T(8,128)(2,1)S(1)}, u32[]{:S(2)}, u32[]{:S(2)}) collective-permute-start(bf16[64,1024]{1,0:T(8,128)(2,1)S(1)} %add.11), channel_id=1, source_target_pairs={{0,1},{1,0},{2,4},{3,5},{4,2},{5,3},{6,8},{7,9},{8,6},{9,7},{10,12... | collective-permute-start | bytes 393224 | tf_op jit(solution)/shard_map/ppermute | solution.py:440
  67.5 10.1 %collective-permute-start.20 = (f32[128,2048]{1,0:T(8,128)S(1)}, f32[128,2048]{1,0:T(8,128)S(1)}, u32[]{:S(2)}, u32[]{:S(2)}) collective-permute-start(f32[128,2048]{1,0:T(8,128)S(1)} %get-tuple-element.88), channel_id=1, source_target_pairs={{0,1},{1,0},{2,3},{3,2},{4,5},{5,4},{6,7},{7,6},{8,9},{9,8},{10,11... | collective-permute-start | bytes 3145736 | tf_op jit(solution)/shard_map/ppermute | solution.py:426
  71.7 3.7 %collective-permute-start.23 = (bf16[128,1024]{1,0:T(8,128)(2,1)S(1)}, bf16[128,1024]{1,0:T(8,128)(2,1)S(1)}, u32[]{:S(2)}, u32[]{:S(2)}) collective-permute-start(bf16[128,1024]{1,0:T(8,128)(2,1)S(1)} %get-tuple-element.97), channel_id=1, source_target_pairs={{0,1},{1,0},{2,3},{3,2},{4,5},{5,4},{6,7},{7,6},{8,9},{9,8},{10,11... | collective-permute-start | bytes 786440 | tf_op jit(solution)/shard_map/ppermute | solution.py:426
  71.8 5.8 %collective-permute-start.26 = (bf16[64,1024]{1,0:T(8,128)(2,1)S(1)}, bf16[64,1024]{1,0:T(8,128)(2,1)S(1)}, u32[]{:S(2)}, u32[]{:S(2)}) collective-permute-start(bf16[64,1024]{1,0:T(8,128)(2,1)S(1)} %get-tuple-element.99), channel_id=1, source_target_pairs={{0,1},{1,0},{2,3},{3,2},{4,5},{5,4},{6,7},{7,6},{8,9},{9,8},{10,11... | collective-permute-start | bytes 393224 | tf_op jit(solution)/shard_map/ppermute | solution.py:426
  72.2 15.6 %collective-permute-start.22 = (bf16[128,1024]{1,0:T(8,128)(2,1)S(1)}, bf16[128,1024]{1,0:T(8,128)(2,1)S(1)}, u32[]{:S(2)}, u32[]{:S(2)}) collective-permute-start(bf16[128,1024]{1,0:T(8,128)(2,1)S(1)} %get-tuple-element.96), channel_id=1, source_target_pairs={{0,2},{1,0},{2,4},{3,1},{4,6},{5,3},{6,8},{7,5},{8,10},{9,7},{10,1... | collective-permute-start | bytes 786440 | tf_op jit(solution)/shard_map/ppermute | solution.py:440
  75.4 12.4 %collective-permute-start.24 = (bf16[128,1024]{1,0:T(8,128)(2,1)S(1)}, bf16[128,1024]{1,0:T(8,128)(2,1)S(1)}, u32[]{:S(2)}, u32[]{:S(2)}) collective-permute-start(bf16[128,1024]{1,0:T(8,128)(2,1)S(1)} %collective-permute-done.23), channel_id=1, source_target_pairs={{0,2},{1,0},{2,4},{3,1},{4,6},{5,3},{6,8},{7,5},{8,10},{9,7},{10,1... | collective-permute-start | bytes 786440 | tf_op jit(solution)/shard_map/ppermute | solution.py:440
  77.6 8.8 %collective-permute-start.25 = (bf16[64,1024]{1,0:T(8,128)(2,1)S(1)}, bf16[64,1024]{1,0:T(8,128)(2,1)S(1)}, u32[]{:S(2)}, u32[]{:S(2)}) collective-permute-start(bf16[64,1024]{1,0:T(8,128)(2,1)S(1)} %get-tuple-element.98), channel_id=1, source_target_pairs={{0,1},{1,3},{2,0},{3,5},{4,2},{5,7},{6,4},{7,9},{8,6},{9,11},{10,8... | collective-permute-start | bytes 393224 | tf_op jit(solution)/shard_map/ppermute | solution.py:440
  77.6 10.2 %collective-permute-start.27 = (bf16[64,1024]{1,0:T(8,128)(2,1)S(1)}, bf16[64,1024]{1,0:T(8,128)(2,1)S(1)}, u32[]{:S(2)}, u32[]{:S(2)}) collective-permute-start(bf16[64,1024]{1,0:T(8,128)(2,1)S(1)} %collective-permute-done.26), channel_id=1, source_target_pairs={{0,1},{1,3},{2,0},{3,5},{4,2},{5,7},{6,4},{7,9},{8,6},{9,11},{10,8... | collective-permute-start | bytes 393224 | tf_op jit(solution)/shard_map/ppermute | solution.py:440
  77.6 4.9 %collective-permute-start.21 = (bf16[16,1024]{1,0:T(8,128)(2,1)S(1)}, bf16[16,1024]{1,0:T(8,128)(2,1)S(1)}, u32[]{:S(2)}, u32[]{:S(2)}) collective-permute-start(bf16[16,1024]{1,0:T(8,128)(2,1)S(1)} %get-tuple-element.95), channel_id=1, source_target_pairs={{0,1},{1,0},{2,3},{3,2},{4,5},{5,4},{6,7},{7,6},{8,9},{9,8},{10,11... | collective-permute-start | bytes 98312 | tf_op jit(solution)/shard_map/ppermute | solution.py:426

commit v3 on v2

--- a/solution.py
+++ b/solution.py
@@ -396,6 +396,7 @@
         "half_same": lambda p, c: (p - 1, 0) if c == 0 else (p + 1, 1),
         "cross": lambda p, c: (p - 1 if p % 2 == 0 else p + 1, c),
         "pair": lambda p, c: (p ^ 1, c),
+        "far2": lambda p, c: (p + 2 if p % 2 == 0 else p - 2, c),
         "z3": lambda p, c: (opposite(p), c),
         "x3": lambda p, c: (p - ROW if p % ROW < ROW // 2 else p + ROW, c),
         "s3": lambda p, c: (p + 6 if p // 2 % 2 == 0 else p - 6, c),
@@ -404,6 +405,7 @@
         "fine_same": lambda p, c: (p, 1 - c),
         "half_same": lambda p, c: (p, 1 - c),
         "cross": lambda p, c: (p, 1 - c),
+        "far2": lambda p, c: (p ^ 1, c),
         "x3": lambda p, c: (p - p % ROW + ROW - 1 - p % ROW, c),
         "s3": lambda p, c: (p ^ 1, c),
     }
@@ -460,7 +462,7 @@
     s3 = fetch(quad3, "s3")
     c2 = fetch(cross2, "cross")
     b2 = fetch(pair2, "pair")
-    f2 = fetch(c2, "pair")
+    f2 = fetch(cross2, "far2")
     x3 = fetch(z3, "x3")
     queries, grads, near_kv, weights, dprobs, stats, outputs = call(
         near_kernel,

time: 90 us -> 87.5 us (0.972)
  waiting for transfers between devices: 34.4 us -> 29.6 us
  starting transfers between devices: 36.2 us -> 38.3 us
    ppermute x10, waiting for transfers between devices: 25.7 us -> 17.4 us  [fetch(): return lax.ppermute(x, AXES, pairs(name))]
    ppermute x10, starting transfers between devices: 11.4 us -> 17.8 us  [fetch(): return lax.ppermute(x, AXES, pairs(name))]
    ppermute x9, waiting for transfers between devices: 8.69 us -> 12.2 us  [give(): return lax.ppermute(x, AXES, [(b, a) for a, b in pairs(name)])]
    ppermute x9, starting transfers between devices: 11.1 us -> 8.44 us  [swap(): return lax.ppermute(x, AXES, [(i, i ^ 1) for i in range(devices)])]
    ppermute x9, starting transfers between devices: 13.7 us -> 12.1 us  [give(): return lax.ppermute(x, AXES, [(b, a) for a, b in pairs(name)])]
  transfers between devices with their start and end apart: 28 -> 28, of which waited for: 10 -> 11; matrix products, arithmetic and copies ran while one was open for 0% -> 0% of each run, Pallas kernels for 9% -> 9%
where the time goes in v3:
time: 87.5 us; the launch traced here: 87.1 us
  starting transfers between devices  38.3 us (44%)
  waiting for transfers between devices  29.6 us (34%)
  Pallas kernels  14.3 us (16%)
  local copies, waits for them, and re-layouts  3.8 us (4%)
  between operations  0.98 us (1%)
    ppermute x10, starting transfers between devices, fetch(): return lax.ppermute(x, AXES, pairs(name))  17.8 us
    ppermute x10, waiting for transfers between devices, fetch(): return lax.ppermute(x, AXES, pairs(name))  17.4 us
    pallas_call x8, Pallas kernels, call(): pl.pallas_call(kernel, out_shape=[jax.ShapeDtypeStruct(shape, dtype) for...  14.3 us
    ppermute x9, waiting for transfers between devices, give(): return lax.ppermute(x, AXES, [(b, a) for a, b in pairs(name)])  12.2 us
    ppermute x9, starting transfers between devices, give(): return lax.ppermute(x, AXES, [(b, a) for a, b in pairs(name)])  12.1 us
    ppermute x9, starting transfers between devices, swap(): return lax.ppermute(x, AXES, [(i, i ^ 1) for i in range(devices)])  8.44 us
    unnamed x8, local copies, waits for them, and re-layouts  3.8 us
  transfers between devices with their start and end apart: 28, of which 11 were waited for; matrix products, arithmetic and copies ran while one was open for 0% of the time, Pallas kernels for 9%

profile of v3, /device:TPU:25, one launch (start us, length us, event | category | flops | bytes accessed | tf_op | source)
XLA Modules:
  0.0 87.1 jit_solution(5401668458339160994)
XLA Ops:
  0.6 0.8 collective-permute-start
  1.4 0.1 collective-permute-start.1
  1.5 0.1 pad_add_fusion.where
  1.6 0.9 %copy-done = bf16[128,1024]{1,0:T(8,128)(2,1)S(1)} copy-done((bf16[128,1024]{1,0:T(8,128)(2,1)S(1)}, bf16[128,1024]{1,0:T(8,128)(2,1)}, u32[]{:S(2)}) %copy-start) | copy-done | bytes 262168
  2.5 0.9 %copy-done.1 = bf16[128,1024]{1,0:T(8,128)(2,1)S(1)} copy-done((bf16[128,1024]{1,0:T(8,128)(2,1)S(1)}, bf16[128,1024]{1,0:T(8,128)(2,1)}, u32[]{:S(2)}) %copy-start.1) | copy-done | bytes 262168
  3.5 0.8 shard_map.75
  4.3 0.0 collective-permute-done.recv_q
  4.3 0.0 collective-permute-done.1.recv_g
  4.3 8.0 %collective-permute-start.6 = (bf16[128,1024]{1,0:T(8,128)(2,1)S(1)}, bf16[128,1024]{1,0:T(8,128)(2,1)S(1)}, u32[]{:S(2)}, u32[]{:S(2)}) collective-permute-start(bf16[128,1024]{1,0:T(8,128)(2,1)S(1)} %get-tuple-element.60), channel_id=1, source_target_pairs={{1,0},{3,1},{0,2},{5,3},{2,4},{7,5},{4,6},{9,7},{6,8},{11,9},{8,10... | collective-permute-start | bytes 786440 | tf_op jit(solution)/shard_map/ppermute | solution.py:439
  12.3 0.8 collective-permute-start.2
  13.1 0.0 collective-permute-start.3
  13.1 4.4 %collective-permute-done.6.half_same = bf16[128,1024]{1,0:T(8,128)(2,1)S(1)} collective-permute-done((bf16[128,1024]{1,0:T(8,128)(2,1)S(1)}, bf16[128,1024]{1,0:T(8,128)(2,1)S(1)}, u32[]{:S(2)}, u32[]{:S(2)}) %collective-permute-start.6) | collective-permute-done | bytes 262176 | tf_op jit(solution)/shard_map/ppermute | solution.py:439
  17.5 1.3 %collective-permute-start.7 = (bf16[128,1024]{1,0:T(8,128)(2,1)S(1)}, bf16[128,1024]{1,0:T(8,128)(2,1)S(1)}, u32[]{:S(2)}, u32[]{:S(2)}) collective-permute-start(bf16[128,1024]{1,0:T(8,128)(2,1)S(1)} %collective-permute-done.6.half_same), channel_id=1, source_target_pairs={{0,1},{1,0},{2,3},{3,2},{4,5},{5,4},{6,7},{7,6},{8,9},{9,8},{10,11... | collective-permute-start | bytes 786440 | tf_op jit(solution)/shard_map/ppermute | solution.py:428
  18.8 3.0 %collective-permute-done.4 = bf16[128,1024]{1,0:T(8,128)(2,1)S(1)} collective-permute-done((bf16[128,1024]{1,0:T(8,128)(2,1)S(1)}, bf16[128,1024]{1,0:T(8,128)(2,1)S(1)}, u32[]{:S(2)}, u32[]{:S(2)}) %collective-permute-start.4) | collective-permute-done | bytes 262176 | tf_op jit(solution)/shard_map/ppermute | solution.py:439
  21.8 0.0 collective-permute-start.5
  21.8 0.0 collective-permute-done.2.recv_kv.recv
  21.8 2.8 %collective-permute-done.3.fine_same = bf16[128,1024]{1,0:T(8,128)(2,1)S(1)} collective-permute-done((bf16[128,1024]{1,0:T(8,128)(2,1)S(1)}, bf16[128,1024]{1,0:T(8,128)(2,1)S(1)}, u32[]{:S(2)}, u32[]{:S(2)}) %collective-permute-start.3) | collective-permute-done | bytes 262176 | tf_op jit(solution)/shard_map/ppermute | solution.py:439
  24.6 0.0 collective-permute-done.7.half_cross
  24.6 0.0 collective-permute-done.5.fine_cross
  24.6 0.9 %shard_map.77 = (bf16[64,1024]{1,0:T(8,128)(2,1)S(1)}, bf16[64,1024]{1,0:T(8,128)(2,1)S(1)}, bf16[64,1024]{1,0:T(8,128)(2,1)S(1)}) custom-call(s32[2]{0:T(128)S(1)} %pad_add_fusion.where, bf16[128,1024]{1,0:T(8,128)(2,1)S(1)} %get-tuple-element.58.own_kv.own, bf16[128,1024]{1,0:T(8,128)(2,1)S(1)} %collective-permute-done.2.recv_kv.recv, ...), custom_call_target="tpu_custom_call" | custom-call | tf_op jit(solution)/shard_map/pallas_call | solution.py:378
  25.5 0.1 collective-permute-start.11
  25.6 0.1 collective-permute-start.9
  25.7 3.0 %collective-permute-start.10 = (bf16[64,1024]{1,0:T(8,128)(2,1)S(1)}, bf16[64,1024]{1,0:T(8,128)(2,1)S(1)}, u32[]{:S(2)}, u32[]{:S(2)}) collective-permute-start(bf16[64,1024]{1,0:T(8,128)(2,1)S(1)} %get-tuple-element.68), channel_id=1, source_target_pairs={{4,0},{5,1},{0,2},{1,3},{8,4},{9,5},{2,6},{3,7},{12,8},{13,9},{6,1... | collective-permute-start | bytes 393224 | tf_op jit(solution)/shard_map/ppermute | solution.py:439
  28.7 3.8 %collective-permute-start.8 = (bf16[64,1024]{1,0:T(8,128)(2,1)S(1)}, bf16[64,1024]{1,0:T(8,128)(2,1)S(1)}, u32[]{:S(2)}, u32[]{:S(2)}) collective-permute-start(bf16[64,1024]{1,0:T(8,128)(2,1)S(1)} %get-tuple-element.68), channel_id=1, source_target_pairs={{1,0},{0,1},{4,2},{5,3},{2,4},{3,5},{8,6},{9,7},{6,8},{7,9},{12,10... | collective-permute-start | bytes 393224 | tf_op jit(solution)/shard_map/ppermute | solution.py:439
  32.5 0.0 collective-permute-start.13
  32.5 1.7 %collective-permute-done.11.z3 = bf16[64,1024]{1,0:T(8,128)(2,1)S(1)} collective-permute-done((bf16[64,1024]{1,0:T(8,128)(2,1)S(1)}, bf16[64,1024]{1,0:T(8,128)(2,1)S(1)}, u32[]{:S(2)}, u32[]{:S(2)}) %collective-permute-start.11) | collective-permute-done | bytes 131104 | tf_op jit(solution)/shard_map/ppermute | solution.py:439
  34.2 0.0 collective-permute-start.12
  34.2 0.9 %copy-done.2 = bf16[128,1024]{1,0:T(8,128)(2,1)S(1)} copy-done((bf16[128,1024]{1,0:T(8,128)(2,1)S(1)}, bf16[128,1024]{1,0:T(8,128)(2,1)}, u32[]{:S(2)}) %copy-start.2) | copy-done | bytes 262168
  35.1 0.9 %copy-done.3 = bf16[128,1024]{1,0:T(8,128)(2,1)S(1)} copy-done((bf16[128,1024]{1,0:T(8,128)(2,1)S(1)}, bf16[128,1024]{1,0:T(8,128)(2,1)}, u32[]{:S(2)}) %copy-start.3) | copy-done | bytes 262168
  36.1 2.8 %shard_map.76 = (bf16[256,512]{1,0:T(8,128)(2,1)S(1)}, bf16[256,512]{1,0:T(8,128)(2,1)S(1)}, bf16[768,1024]{1,0:T(8,128)(2,1)S(1)}, f32[2304,256]{1,0:T(8,128)S(...) custom-call(s32[2]{0:T(128)S(1)} %pad_add_fusion.where, ...), custom_call_target="tpu_custom_call" | custom-call | tf_op jit(solution)/shard_map/pallas_call | solution.py:378
  38.9 0.0 collective-permute-done.9.p2
  38.9 0.0 collective-permute-done.10.s2
  38.9 2.8 %collective-permute-done.8.m2 = bf16[64,1024]{1,0:T(8,128)(2,1)S(1)} collective-permute-done((bf16[64,1024]{1,0:T(8,128)(2,1)S(1)}, bf16[64,1024]{1,0:T(8,128)(2,1)S(1)}, u32[]{:S(2)}, u32[]{:S(2)}) %collective-permute-start.8) | collective-permute-done | bytes 131104 | tf_op jit(solution)/shard_map/ppermute | solution.py:439
  41.8 0.0 collective-permute-done.13.s3
  41.8 1.5 %collective-permute-done.12.x3 = bf16[64,1024]{1,0:T(8,128)(2,1)S(1)} collective-permute-done((bf16[64,1024]{1,0:T(8,128)(2,1)S(1)}, bf16[64,1024]{1,0:T(8,128)(2,1)S(1)}, u32[]{:S(2)}, u32[]{:S(2)}) %collective-permute-start.12) | collective-permute-done | bytes 131104 | tf_op jit(solution)/shard_map/ppermute | solution.py:439
  43.3 2.3 %shard_map.78 = (f32[256,512]{1,0:T(8,128)S(1)}, f32[8,256]{1,0:T(8,128)S(1)}, bf16[1536,256]{1,0:T(8,128)(2,1)S(1)}, bf16[64,1024]{1,0:T(8,128)(2,1)S(1)}, bf16...) custom-call(s32[2]{0:T(128)S(1)} %pad_add_fusion.where, ...), custom_call_target="tpu_custom_call" | custom-call | tf_op jit(solution)/shard_map/pallas_call | solution.py:378
  45.6 0.1 collective-permute-start.14
  45.7 2.7 %collective-permute-start.15 = (bf16[64,1024]{1,0:T(8,128)(2,1)S(1)}, bf16[64,1024]{1,0:T(8,128)(2,1)S(1)}, u32[]{:S(2)}, u32[]{:S(2)}) collective-permute-start(bf16[64,1024]{1,0:T(8,128)(2,1)S(1)} %get-tuple-element.73), channel_id=1, source_target_pairs={{2,0},{3,1},{0,2},{1,3},{6,4},{7,5},{4,6},{5,7},{10,8},{11,9},{8,1... | collective-permute-start | bytes 393224 | tf_op jit(solution)/shard_map/ppermute | solution.py:439
  48.5 1.3 %collective-permute-start.19 = (bf16[64,1024]{1,0:T(8,128)(2,1)S(1)}, bf16[64,1024]{1,0:T(8,128)(2,1)S(1)}, u32[]{:S(2)}, u32[]{:S(2)}) collective-permute-start(bf16[64,1024]{1,0:T(8,128)(2,1)S(1)} %get-tuple-element.86), channel_id=1, source_target_pairs={{0,2},{1,3},{2,0},{3,1},{4,6},{5,7},{6,4},{7,5},{8,10},{9,11},{10,... | collective-permute-start | bytes 393224 | tf_op jit(solution)/shard_map/ppermute | solution.py:442
  49.8 0.1 collective-permute-done.14
  49.9 1.2 %collective-permute-done.15 = bf16[64,1024]{1,0:T(8,128)(2,1)S(1)} collective-permute-done((bf16[64,1024]{1,0:T(8,128)(2,1)S(1)}, bf16[64,1024]{1,0:T(8,128)(2,1)S(1)}, u32[]{:S(2)}, u32[]{:S(2)}) %collective-permute-start.15) | collective-permute-done | bytes 131104 | tf_op jit(solution)/shard_map/ppermute | solution.py:439
  51.1 3.9 %collective-permute-start.17 = (bf16[64,1024]{1,0:T(8,128)(2,1)S(1)}, bf16[64,1024]{1,0:T(8,128)(2,1)S(1)}, u32[]{:S(2)}, u32[]{:S(2)}) collective-permute-start(bf16[64,1024]{1,0:T(8,128)(2,1)S(1)} %add.10), channel_id=1, source_target_pairs={{0,10},{1,11},{2,8},{3,9},{4,14},{5,15},{6,12},{7,13},{8,2},{9,3},... | collective-permute-start | bytes 393224 | tf_op jit(solution)/shard_map/ppermute | solution.py:442
  55.1 1.7 %collective-permute-start.18 = (bf16[64,1024]{1,0:T(8,128)(2,1)S(1)}, bf16[64,1024]{1,0:T(8,128)(2,1)S(1)}, u32[]{:S(2)}, u32[]{:S(2)}) collective-permute-start(bf16[64,1024]{1,0:T(8,128)(2,1)S(1)} %add.11), channel_id=1, source_target_pairs={{0,1},{1,0},{2,4},{3,5},{4,2},{5,3},{6,8},{7,9},{8,6},{9,7},{10,12... | collective-permute-start | bytes 393224 | tf_op jit(solution)/shard_map/ppermute | solution.py:442
  56.8 3.2 %shard_map.79 = (f32[128,2048]{1,0:T(8,128)S(1)}, f32[128,2048]{1,0:T(8,128)S(1)}, bf16[192,1024]{1,0:T(8,128)(2,1)S(1)}, bf16[192,1024]{1,0:T(8,128)(2,1)S(1)}) custom-call(s32[2]{0:T(128)S(1)} %pad_add_fusion.where, bf16[256,512]{1,0:T(8,128)(2,1)S(1)} %get-tuple-element.61.queries, bf16[256,512]{1,0:T(8,128)(2,1)S(1)} %get-tuple-element.62.grads, ...), custom_call_target="tpu_custom_call" | custom-call | tf_op jit(solution)/shard_map/pallas_call | solution.py:378
  60.0 0.0 collective-permute-done.19.pair2
  60.0 0.0 collective-permute-done.17.z3
  60.0 6.9 %collective-permute-done.18.cross2 = bf16[64,1024]{1,0:T(8,128)(2,1)S(1)} collective-permute-done((bf16[64,1024]{1,0:T(8,128)(2,1)S(1)}, bf16[64,1024]{1,0:T(8,128)(2,1)S(1)}, u32[]{:S(2)}, u32[]{:S(2)}) %collective-permute-start.18) | collective-permute-done | bytes 131104 | tf_op jit(solution)/shard_map/ppermute | solution.py:442
  66.9 1.0 %shard_map.80 = (bf16[128,1024]{1,0:T(8,128)(2,1)S(1)}, bf16[128,1024]{1,0:T(8,128)(2,1)S(1)}, bf16[64,1024]{1,0:T(8,128)(2,1)S(1)}, bf16[64,1024]{1,0:T(8,128)(...) custom-call(s32[2]{0:T(128)S(1)} %pad_add_fusion.where, ...), custom_call_target="tpu_custom_call" | custom-call | tf_op jit(solution)/shard_map/pallas_call | solution.py:378
  67.9 1.1 %collective-permute-start.20 = (f32[128,2048]{1,0:T(8,128)S(1)}, f32[128,2048]{1,0:T(8,128)S(1)}, u32[]{:S(2)}, u32[]{:S(2)}) collective-permute-start(f32[128,2048]{1,0:T(8,128)S(1)} %get-tuple-element.88), channel_id=1, source_target_pairs={{0,1},{1,0},{2,3},{3,2},{4,5},{5,4},{6,7},{7,6},{8,9},{9,8},{10,11... | collective-permute-start | bytes 3145736 | tf_op jit(solution)/shard_map/ppermute | solution.py:428
  69.0 0.1 collective-permute-start.23
  69.1 0.4 collective-permute-start.26
  69.5 2.8 %collective-permute-start.22 = (bf16[128,1024]{1,0:T(8,128)(2,1)S(1)}, bf16[128,1024]{1,0:T(8,128)(2,1)S(1)}, u32[]{:S(2)}, u32[]{:S(2)}) collective-permute-start(bf16[128,1024]{1,0:T(8,128)(2,1)S(1)} %get-tuple-element.96), channel_id=1, source_target_pairs={{0,2},{1,0},{2,4},{3,1},{4,6},{5,3},{6,8},{7,5},{8,10},{9,7},{10,1... | collective-permute-start | bytes 786440 | tf_op jit(solution)/shard_map/ppermute | solution.py:442
  72.3 0.0 collective-permute-done.23
  72.4 2.1 %collective-permute-start.24 = (bf16[128,1024]{1,0:T(8,128)(2,1)S(1)}, bf16[128,1024]{1,0:T(8,128)(2,1)S(1)}, u32[]{:S(2)}, u32[]{:S(2)}) collective-permute-start(bf16[128,1024]{1,0:T(8,128)(2,1)S(1)} %collective-permute-done.23), channel_id=1, source_target_pairs={{0,2},{1,0},{2,4},{3,1},{4,6},{5,3},{6,8},{7,5},{8,10},{9,7},{10,1... | collective-permute-start | bytes 786440 | tf_op jit(solution)/shard_map/ppermute | solution.py:442
  74.5 0.0 collective-permute-start.25
  74.5 0.0 collective-permute-done.26
  74.5 0.0 collective-permute-start.27
  74.5 3.9 %collective-permute-start.21 = (bf16[16,1024]{1,0:T(8,128)(2,1)S(1)}, bf16[16,1024]{1,0:T(8,128)(2,1)S(1)}, u32[]{:S(2)}, u32[]{:S(2)}) collective-permute-start(bf16[16,1024]{1,0:T(8,128)(2,1)S(1)} %get-tuple-element.95), channel_id=1, source_target_pairs={{0,1},{1,0},{2,3},{3,2},{4,5},{5,4},{6,7},{7,6},{8,9},{9,8},{10,11... | collective-permute-start | bytes 98312 | tf_op jit(solution)/shard_map/ppermute | solution.py:428
  78.4 1.5 %shard_map.81 = (bf16[128,1024]{1,0:T(8,128)(2,1)}, f32[128,1024]{1,0:T(8,128)}) custom-call(s32[2]{0:T(128)S(1)} %pad_add_fusion.where, f32[128,2048]{1,0:T(8,128)S(1)} %get-tuple-element.78.out_keep.keep, f32[128,2048]{1,0:T(8,128)S(1)} %collective-permute-done.20.out_recv.recv), custom_call_target="tpu_custom_call" | custom-call | tf_op jit(solution)/shard_map/pallas_call | solution.py:378
  79.9 0.0 collective-permute-done.21.recv3
  79.9 3.9 %collective-permute-done.25.half_same = bf16[64,1024]{1,0:T(8,128)(2,1)S(1)} collective-permute-done((bf16[64,1024]{1,0:T(8,128)(2,1)S(1)}, bf16[64,1024]{1,0:T(8,128)(2,1)S(1)}, u32[]{:S(2)}, u32[]{:S(2)}) %collective-permute-start.25) | collective-permute-done | bytes 131104 | tf_op jit(solution)/shard_map/ppermute | solution.py:442
  83.8 1.4 %collective-permute-done.27.half_cross = bf16[64,1024]{1,0:T(8,128)(2,1)S(1)} collective-permute-done((bf16[64,1024]{1,0:T(8,128)(2,1)S(1)}, bf16[64,1024]{1,0:T(8,128)(2,1)S(1)}, u32[]{:S(2)}, u32[]{:S(2)}) %collective-permute-start.27) | collective-permute-done | bytes 131104 | tf_op jit(solution)/shard_map/ppermute | solution.py:442
  85.1 0.0 collective-permute-done.22.fine_same
  85.2 1.8 %shard_map.82 = (f32[128,1024]{1,0:T(8,128)}, f32[128,1024]{1,0:T(8,128)}) custom-call(s32[2]{0:T(128)S(1)} %pad_add_fusion.where, f32[128,2048]{1,0:T(8,128)S(1)} %get-tuple-element.78.out_keep.keep, f32[128,2048]{1,0:T(8,128)S(1)} %collective-permute-done.20.out_recv.recv, bf16[16,1024]{1,0:T(8,128)(2,1)S(1)} %get-tuple-element.94.keep3, ...), custom_call_target="tpu_custom_call" | custom-call | tf_op jit(solution)/shard_map/pallas_call | solution.py:378
  (11 shorter events, 0.1 us)
Async XLA Ops:
  0.6 3.6 %collective-permute-start = (bf16[128,1024]{1,0:T(8,128)(2,1)}, bf16[128,1024]{1,0:T(8,128)(2,1)S(1)}, u32[]{:S(2)}, u32[]{:S(2)}) collective-permute-start(bf16[128,1024]{1,0:T(8,128)(2,1)} %q.1), channel_id=1, source_target_pairs={{0,1},{1,0},{2,3},{3,2},{4,5},{5,4},{6,7},{7,6},{8,9},{9,8},{10,11... | collective-permute-start | bytes 786440 | tf_op jit(solution)/shard_map/ppermute | solution.py:428
  1.4 2.9 %collective-permute-start.1 = (bf16[128,1024]{1,0:T(8,128)(2,1)}, bf16[128,1024]{1,0:T(8,128)(2,1)S(1)}, u32[]{:S(2)}, u32[]{:S(2)}) collective-permute-start(bf16[128,1024]{1,0:T(8,128)(2,1)} %g.1), channel_id=1, source_target_pairs={{0,1},{1,0},{2,3},{3,2},{4,5},{5,4},{6,7},{7,6},{8,9},{9,8},{10,11... | collective-permute-start | bytes 786440 | tf_op jit(solution)/shard_map/ppermute | solution.py:428
  1.6 0.9 %copy-start = (bf16[128,1024]{1,0:T(8,128)(2,1)S(1)}, bf16[128,1024]{1,0:T(8,128)(2,1)}, u32[]{:S(2)}) copy-start(bf16[128,1024]{1,0:T(8,128)(2,1)} %k.1) | copy-start | bytes 786436
  2.5 0.9 %copy-start.1 = (bf16[128,1024]{1,0:T(8,128)(2,1)S(1)}, bf16[128,1024]{1,0:T(8,128)(2,1)}, u32[]{:S(2)}) copy-start(bf16[128,1024]{1,0:T(8,128)(2,1)} %v.1) | copy-start | bytes 786436
  4.3 13.2 %collective-permute-start.6 = (bf16[128,1024]{1,0:T(8,128)(2,1)S(1)}, bf16[128,1024]{1,0:T(8,128)(2,1)S(1)}, u32[]{:S(2)}, u32[]{:S(2)}) collective-permute-start(bf16[128,1024]{1,0:T(8,128)(2,1)S(1)} %get-tuple-element.60), channel_id=1, source_target_pairs={{1,0},{3,1},{0,2},{5,3},{2,4},{7,5},{4,6},{9,7},{6,8},{11,9},{8,10... | collective-permute-start | bytes 786440 | tf_op jit(solution)/shard_map/ppermute | solution.py:439
  12.3 9.4 %collective-permute-start.4 = (bf16[128,1024]{1,0:T(8,128)(2,1)S(1)}, bf16[128,1024]{1,0:T(8,128)(2,1)S(1)}, u32[]{:S(2)}, u32[]{:S(2)}) collective-permute-start(bf16[128,1024]{1,0:T(8,128)(2,1)S(1)} %get-tuple-element.59), channel_id=1, source_target_pairs={{2,0},{0,1},{4,2},{1,3},{6,4},{3,5},{8,6},{5,7},{10,8},{7,9},{12,1... | collective-permute-start | bytes 786440 | tf_op jit(solution)/shard_map/ppermute | solution.py:439
  12.3 9.4 %collective-permute-start.2 = (bf16[128,1024]{1,0:T(8,128)(2,1)S(1)}, bf16[128,1024]{1,0:T(8,128)(2,1)S(1)}, u32[]{:S(2)}, u32[]{:S(2)}) collective-permute-start(bf16[128,1024]{1,0:T(8,128)(2,1)S(1)} %get-tuple-element.59), channel_id=1, source_target_pairs={{0,1},{1,0},{2,3},{3,2},{4,5},{5,4},{6,7},{7,6},{8,9},{9,8},{10,11... | collective-permute-start | bytes 786440 | tf_op jit(solution)/shard_map/ppermute | solution.py:428
  13.1 11.5 %collective-permute-start.3 = (bf16[128,1024]{1,0:T(8,128)(2,1)S(1)}, bf16[128,1024]{1,0:T(8,128)(2,1)S(1)}, u32[]{:S(2)}, u32[]{:S(2)}) collective-permute-start(bf16[128,1024]{1,0:T(8,128)(2,1)S(1)} %get-tuple-element.58.own_kv.own), channel_id=1, source_target_pairs={{2,0},{0,1},{4,2},{1,3},{6,4},{3,5},{8,6},{5,7},{10,8},{7,9},{12,1... | collective-permute-start | bytes 786440 | tf_op jit(solution)/shard_map/ppermute | solution.py:439
  17.5 7.1 %collective-permute-start.7 = (bf16[128,1024]{1,0:T(8,128)(2,1)S(1)}, bf16[128,1024]{1,0:T(8,128)(2,1)S(1)}, u32[]{:S(2)}, u32[]{:S(2)}) collective-permute-start(bf16[128,1024]{1,0:T(8,128)(2,1)S(1)} %collective-permute-done.6.half_same), channel_id=1, source_target_pairs={{0,1},{1,0},{2,3},{3,2},{4,5},{5,4},{6,7},{7,6},{8,9},{9,8},{10,11... | collective-permute-start | bytes 786440 | tf_op jit(solution)/shard_map/ppermute | solution.py:428
  21.8 2.8 %collective-permute-start.5 = (bf16[128,1024]{1,0:T(8,128)(2,1)S(1)}, bf16[128,1024]{1,0:T(8,128)(2,1)S(1)}, u32[]{:S(2)}, u32[]{:S(2)}) collective-permute-start(bf16[128,1024]{1,0:T(8,128)(2,1)S(1)} %collective-permute-done.4), channel_id=1, source_target_pairs={{0,1},{1,0},{2,3},{3,2},{4,5},{5,4},{6,7},{7,6},{8,9},{9,8},{10,11... | collective-permute-start | bytes 786440 | tf_op jit(solution)/shard_map/ppermute | solution.py:428
  25.5 8.7 %collective-permute-start.11 = (bf16[64,1024]{1,0:T(8,128)(2,1)S(1)}, bf16[64,1024]{1,0:T(8,128)(2,1)S(1)}, u32[]{:S(2)}, u32[]{:S(2)}) collective-permute-start(bf16[64,1024]{1,0:T(8,128)(2,1)S(1)} %get-tuple-element.70), channel_id=1, source_target_pairs={{10,0},{11,1},{8,2},{9,3},{14,4},{15,5},{12,6},{13,7},{2,8},{3,9},... | collective-permute-start | bytes 393224 | tf_op jit(solution)/shard_map/ppermute | solution.py:439
  25.6 13.4 %collective-permute-start.9 = (bf16[64,1024]{1,0:T(8,128)(2,1)S(1)}, bf16[64,1024]{1,0:T(8,128)(2,1)S(1)}, u32[]{:S(2)}, u32[]{:S(2)}) collective-permute-start(bf16[64,1024]{1,0:T(8,128)(2,1)S(1)} %get-tuple-element.69), channel_id=1, source_target_pairs={{2,0},{3,1},{0,2},{1,3},{6,4},{7,5},{4,6},{5,7},{10,8},{11,9},{8,1... | collective-permute-start | bytes 393224 | tf_op jit(solution)/shard_map/ppermute | solution.py:439
  25.7 13.3 %collective-permute-start.10 = (bf16[64,1024]{1,0:T(8,128)(2,1)S(1)}, bf16[64,1024]{1,0:T(8,128)(2,1)S(1)}, u32[]{:S(2)}, u32[]{:S(2)}) collective-permute-start(bf16[64,1024]{1,0:T(8,128)(2,1)S(1)} %get-tuple-element.68), channel_id=1, source_target_pairs={{4,0},{5,1},{0,2},{1,3},{8,4},{9,5},{2,6},{3,7},{12,8},{13,9},{6,1... | collective-permute-start | bytes 393224 | tf_op jit(solution)/shard_map/ppermute | solution.py:439
  28.7 13.1 %collective-permute-start.8 = (bf16[64,1024]{1,0:T(8,128)(2,1)S(1)}, bf16[64,1024]{1,0:T(8,128)(2,1)S(1)}, u32[]{:S(2)}, u32[]{:S(2)}) collective-permute-start(bf16[64,1024]{1,0:T(8,128)(2,1)S(1)} %get-tuple-element.68), channel_id=1, source_target_pairs={{1,0},{0,1},{4,2},{5,3},{2,4},{3,5},{8,6},{9,7},{6,8},{7,9},{12,10... | collective-permute-start | bytes 393224 | tf_op jit(solution)/shard_map/ppermute | solution.py:439
  32.5 9.3 %collective-permute-start.13 = (bf16[64,1024]{1,0:T(8,128)(2,1)S(1)}, bf16[64,1024]{1,0:T(8,128)(2,1)S(1)}, u32[]{:S(2)}, u32[]{:S(2)}) collective-permute-start(bf16[64,1024]{1,0:T(8,128)(2,1)S(1)} %get-tuple-element.70), channel_id=1, source_target_pairs={{12,0},{13,1},{14,2},{15,3},{6,4},{7,5},{4,6},{5,7},{20,8},{21,9},... | collective-permute-start | bytes 393224 | tf_op jit(solution)/shard_map/ppermute | solution.py:439
  34.2 9.1 %collective-permute-start.12 = (bf16[64,1024]{1,0:T(8,128)(2,1)S(1)}, bf16[64,1024]{1,0:T(8,128)(2,1)S(1)}, u32[]{:S(2)}, u32[]{:S(2)}) collective-permute-start(bf16[64,1024]{1,0:T(8,128)(2,1)S(1)} %collective-permute-done.11.z3), channel_id=1, source_target_pairs={{14,0},{15,1},{12,2},{13,3},{10,4},{11,5},{8,6},{9,7},{24,8},{25,9... | collective-permute-start | bytes 393224 | tf_op jit(solution)/shard_map/ppermute | solution.py:439
  34.2 1.0 %copy-start.2 = (bf16[128,1024]{1,0:T(8,128)(2,1)S(1)}, bf16[128,1024]{1,0:T(8,128)(2,1)}, u32[]{:S(2)}) copy-start(bf16[128,1024]{1,0:T(8,128)(2,1)} %q.1) | copy-start | bytes 786436
  35.1 0.9 %copy-start.3 = (bf16[128,1024]{1,0:T(8,128)(2,1)S(1)}, bf16[128,1024]{1,0:T(8,128)(2,1)}, u32[]{:S(2)}) copy-start(bf16[128,1024]{1,0:T(8,128)(2,1)} %g.1) | copy-start | bytes 786436
  45.6 4.2 %collective-permute-start.14 = (bf16[64,1024]{1,0:T(8,128)(2,1)S(1)}, bf16[64,1024]{1,0:T(8,128)(2,1)S(1)}, u32[]{:S(2)}, u32[]{:S(2)}) collective-permute-start(bf16[64,1024]{1,0:T(8,128)(2,1)S(1)} %get-tuple-element.72), channel_id=1, source_target_pairs={{0,14},{1,15},{2,12},{3,13},{4,10},{5,11},{6,8},{7,9},{8,24},{9,25... | collective-permute-start | bytes 393224 | tf_op jit(solution)/shard_map/ppermute | solution.py:442
  45.7 5.4 %collective-permute-start.15 = (bf16[64,1024]{1,0:T(8,128)(2,1)S(1)}, bf16[64,1024]{1,0:T(8,128)(2,1)S(1)}, u32[]{:S(2)}, u32[]{:S(2)}) collective-permute-start(bf16[64,1024]{1,0:T(8,128)(2,1)S(1)} %get-tuple-element.73), channel_id=1, source_target_pairs={{2,0},{3,1},{0,2},{1,3},{6,4},{7,5},{4,6},{5,7},{10,8},{11,9},{8,1... | collective-permute-start | bytes 393224 | tf_op jit(solution)/shard_map/ppermute | solution.py:439
  48.4 11.5 %collective-permute-start.16 = (bf16[64,1024]{1,0:T(8,128)(2,1)S(1)}, bf16[64,1024]{1,0:T(8,128)(2,1)S(1)}, u32[]{:S(2)}, u32[]{:S(2)}) collective-permute-start(bf16[64,1024]{1,0:T(8,128)(2,1)S(1)} %get-tuple-element.82), channel_id=1, source_target_pairs={{0,12},{1,13},{2,14},{3,15},{4,6},{5,7},{6,4},{7,5},{8,20},{9,21},... | collective-permute-start | bytes 393224 | tf_op jit(solution)/shard_map/ppermute | solution.py:442
  48.5 11.6 %collective-permute-start.19 = (bf16[64,1024]{1,0:T(8,128)(2,1)S(1)}, bf16[64,1024]{1,0:T(8,128)(2,1)S(1)}, u32[]{:S(2)}, u32[]{:S(2)}) collective-permute-start(bf16[64,1024]{1,0:T(8,128)(2,1)S(1)} %get-tuple-element.86), channel_id=1, source_target_pairs={{0,2},{1,3},{2,0},{3,1},{4,6},{5,7},{6,4},{7,5},{8,10},{9,11},{10,... | collective-permute-start | bytes 393224 | tf_op jit(solution)/shard_map/ppermute | solution.py:442
  51.1 8.9 %collective-permute-start.17 = (bf16[64,1024]{1,0:T(8,128)(2,1)S(1)}, bf16[64,1024]{1,0:T(8,128)(2,1)S(1)}, u32[]{:S(2)}, u32[]{:S(2)}) collective-permute-start(bf16[64,1024]{1,0:T(8,128)(2,1)S(1)} %add.10), channel_id=1, source_target_pairs={{0,10},{1,11},{2,8},{3,9},{4,14},{5,15},{6,12},{7,13},{8,2},{9,3},... | collective-permute-start | bytes 393224 | tf_op jit(solution)/shard_map/ppermute | solution.py:442
  55.1 11.8 %collective-permute-start.18 = (bf16[64,1024]{1,0:T(8,128)(2,1)S(1)}, bf16[64,1024]{1,0:T(8,128)(2,1)S(1)}, u32[]{:S(2)}, u32[]{:S(2)}) collective-permute-start(bf16[64,1024]{1,0:T(8,128)(2,1)S(1)} %add.11), channel_id=1, source_target_pairs={{0,1},{1,0},{2,4},{3,5},{4,2},{5,3},{6,8},{7,9},{8,6},{9,7},{10,12... | collective-permute-start | bytes 393224 | tf_op jit(solution)/shard_map/ppermute | solution.py:442
  67.9 6.6 %collective-permute-start.20 = (f32[128,2048]{1,0:T(8,128)S(1)}, f32[128,2048]{1,0:T(8,128)S(1)}, u32[]{:S(2)}, u32[]{:S(2)}) collective-permute-start(f32[128,2048]{1,0:T(8,128)S(1)} %get-tuple-element.88), channel_id=1, source_target_pairs={{0,1},{1,0},{2,3},{3,2},{4,5},{5,4},{6,7},{7,6},{8,9},{9,8},{10,11... | collective-permute-start | bytes 3145736 | tf_op jit(solution)/shard_map/ppermute | solution.py:428
  69.0 3.3 %collective-permute-start.23 = (bf16[128,1024]{1,0:T(8,128)(2,1)S(1)}, bf16[128,1024]{1,0:T(8,128)(2,1)S(1)}, u32[]{:S(2)}, u32[]{:S(2)}) collective-permute-start(bf16[128,1024]{1,0:T(8,128)(2,1)S(1)} %get-tuple-element.97), channel_id=1, source_target_pairs={{0,1},{1,0},{2,3},{3,2},{4,5},{5,4},{6,7},{7,6},{8,9},{9,8},{10,11... | collective-permute-start | bytes 786440 | tf_op jit(solution)/shard_map/ppermute | solution.py:428
  69.1 5.4 %collective-permute-start.26 = (bf16[64,1024]{1,0:T(8,128)(2,1)S(1)}, bf16[64,1024]{1,0:T(8,128)(2,1)S(1)}, u32[]{:S(2)}, u32[]{:S(2)}) collective-permute-start(bf16[64,1024]{1,0:T(8,128)(2,1)S(1)} %get-tuple-element.99), channel_id=1, source_target_pairs={{0,1},{1,0},{2,3},{3,2},{4,5},{5,4},{6,7},{7,6},{8,9},{9,8},{10,11... | collective-permute-start | bytes 393224 | tf_op jit(solution)/shard_map/ppermute | solution.py:428
  69.5 15.6 %collective-permute-start.22 = (bf16[128,1024]{1,0:T(8,128)(2,1)S(1)}, bf16[128,1024]{1,0:T(8,128)(2,1)S(1)}, u32[]{:S(2)}, u32[]{:S(2)}) collective-permute-start(bf16[128,1024]{1,0:T(8,128)(2,1)S(1)} %get-tuple-element.96), channel_id=1, source_target_pairs={{0,2},{1,0},{2,4},{3,1},{4,6},{5,3},{6,8},{7,5},{8,10},{9,7},{10,1... | collective-permute-start | bytes 786440 | tf_op jit(solution)/shard_map/ppermute | solution.py:442
  72.4 12.8 %collective-permute-start.24 = (bf16[128,1024]{1,0:T(8,128)(2,1)S(1)}, bf16[128,1024]{1,0:T(8,128)(2,1)S(1)}, u32[]{:S(2)}, u32[]{:S(2)}) collective-permute-start(bf16[128,1024]{1,0:T(8,128)(2,1)S(1)} %collective-permute-done.23), channel_id=1, source_target_pairs={{0,2},{1,0},{2,4},{3,1},{4,6},{5,3},{6,8},{7,5},{8,10},{9,7},{10,1... | collective-permute-start | bytes 786440 | tf_op jit(solution)/shard_map/ppermute | solution.py:442
  74.5 9.3 %collective-permute-start.25 = (bf16[64,1024]{1,0:T(8,128)(2,1)S(1)}, bf16[64,1024]{1,0:T(8,128)(2,1)S(1)}, u32[]{:S(2)}, u32[]{:S(2)}) collective-permute-start(bf16[64,1024]{1,0:T(8,128)(2,1)S(1)} %get-tuple-element.98), channel_id=1, source_target_pairs={{0,1},{1,3},{2,0},{3,5},{4,2},{5,7},{6,4},{7,9},{8,6},{9,11},{10,8... | collective-permute-start | bytes 393224 | tf_op jit(solution)/shard_map/ppermute | solution.py:442
  74.5 10.6 %collective-permute-start.27 = (bf16[64,1024]{1,0:T(8,128)(2,1)S(1)}, bf16[64,1024]{1,0:T(8,128)(2,1)S(1)}, u32[]{:S(2)}, u32[]{:S(2)}) collective-permute-start(bf16[64,1024]{1,0:T(8,128)(2,1)S(1)} %collective-permute-done.26), channel_id=1, source_target_pairs={{0,1},{1,3},{2,0},{3,5},{4,2},{5,7},{6,4},{7,9},{8,6},{9,11},{10,8... | collective-permute-start | bytes 393224 | tf_op jit(solution)/shard_map/ppermute | solution.py:442
  74.5 5.4 %collective-permute-start.21 = (bf16[16,1024]{1,0:T(8,128)(2,1)S(1)}, bf16[16,1024]{1,0:T(8,128)(2,1)S(1)}, u32[]{:S(2)}, u32[]{:S(2)}) collective-permute-start(bf16[16,1024]{1,0:T(8,128)(2,1)S(1)} %get-tuple-element.95), channel_id=1, source_target_pairs={{0,1},{1,0},{2,3},{3,2},{4,5},{5,4},{6,7},{7,6},{8,9},{9,8},{10,11... | collective-permute-start | bytes 98312 | tf_op jit(solution)/shard_map/ppermute | solution.py:428
